TPU v7x, 128 devices: a whole 4x4x4 slice. The times are simulated.
128 devices in a mesh: dp: 16 (over y, x_lo, core), sp: 8 (over x_hi, z).
Axes of the slice: x: 4 (x_hi: 2, x_lo: 2; x = x_hi * 2 + x_lo), y: 4, z: 4, core: 2. Of those that a mesh axis runs over, the one named last changes fastest.
Arguments:
- tokens: bfloat16 [16384, 2048], P(('dp', 'sp')), may hold values from -6 to 6
- cotangent: bfloat16 [16384, 2048], P(('dp', 'sp')), may hold values from -6 to 6
- chosen: int32 [16384, 2], P(('dp', 'sp')), may hold values from 0 to 3, all different within a row; in each aligned block of 128 rows (0 to 127, 128 to 255, ...) at most 80 rows name the same one
- attn_gain: bfloat16 [2048], P('dp'), may hold values from 0.099609375 to 1.8984375
- w_query: bfloat16 [2048, 3072], P('dp'), may hold values from -0.125 to 0.125
- w_kv_down: bfloat16 [2048, 576], P('dp'), may hold values from -0.125 to 0.125
- kv_gain: bfloat16 [512], P('dp'), may hold values from 0.099609375 to 1.8984375
- w_kv_up: bfloat16 [512, 4096], P('dp'), may hold values from -0.25 to 0.25
- w_out: bfloat16 [2048, 2048], P('dp'), may hold values from -2 to 2
- ffn_gain: bfloat16 [2048], P('dp'), may hold values from 0.099609375 to 1.8984375
- w_router: bfloat16 [2048, 4], P('dp'), may hold values from -0.09375 to 0.09375
- shared_gate: bfloat16 [2048, 2, 1408], P('dp'), may hold values from -0.125 to 0.125
- shared_up: bfloat16 [2048, 2, 1408], P('dp'), may hold values from -0.125 to 0.125
- shared_down: bfloat16 [1408, 2, 2048], P('dp'), may hold values from -0.109375 to 0.109375
- expert_gate: bfloat16 [2048, 4, 1408], P('dp'), may hold values from -0.125 to 0.125
- expert_up: bfloat16 [2048, 4, 1408], P('dp'), may hold values from -0.125 to 0.125
- expert_down: bfloat16 [1408, 4, 2048], P('dp'), may hold values from -0.15625 to 0.15625
Outputs:
- mixed: bfloat16 [16384, 2048], P(('dp', 'sp'))
- tokens_grad: bfloat16 [16384, 2048], P(('dp', 'sp'))
- attn_gain_grad: float32 [2048], P('dp')
- w_query_grad: float32 [2048, 3072], P('dp')
- w_kv_down_grad: float32 [2048, 576], P('dp')
- kv_gain_grad: float32 [512], P('dp')
- w_kv_up_grad: float32 [512, 4096], P('dp')
- w_out_grad: float32 [2048, 2048], P('dp')
- ffn_gain_grad: float32 [2048], P('dp')
- w_router_grad: float32 [2048, 4], P('dp')
- shared_gate_grad: float32 [2048, 2, 1408], P('dp')
- shared_up_grad: float32 [2048, 2, 1408], P('dp')
- shared_down_grad: float32 [1408, 2, 2048], P('dp')
- expert_gate_grad: float32 [2048, 4, 1408], P('dp')
- expert_up_grad: float32 [2048, 4, 1408], P('dp')
- expert_down_grad: float32 [1408, 4, 2048], P('dp')
Inputs may be any that keep to these rules, and one draw needn't show every extreme that they name: `chosen`: each row names 2 different experts. Among the rows of one device (aligned blocks of 128 rows) no expert is named by more than 80 rows, and in every draw some expert is named by exactly 80 rows of some device.
All inputs are finite; a program needn't handle non-finite values.
Results may differ from a plain program's by a relative error of at most 0.025.
Values may be sent and summed in bfloat16 or wider, within the bound.
A program may use at most 576 MiB of HBM per device.

v0:
```python
import jax
import jax.numpy as jnp
from jax import lax
from jax.sharding import PartitionSpec as P

D = 2048
HEADS = 16
NOPE = 128
ROPE = 64
VDIM = 128
RANK = 512
FE = 1408
NS = 2
EXPERTS = 4
TOP = 2


epsilon = 1e-06
highest = lax.Precision.HIGHEST


def rms_norm(values, gain_vec):
    return (
        values * lax.rsqrt(jnp.mean(values * values, axis=-1, keepdims=True) + epsilon) * gain_vec
    )


def rotate(values, cosine, sine):
    half_dim = values.shape[-1] // 2
    first_half = values[..., :half_dim]
    second_half = values[..., half_dim:]
    return jnp.concatenate(
        [first_half * cosine - second_half * sine, second_half * cosine + first_half * sine],
        axis=-1,
    )


def unrotate(values, cosine, sine):
    half_dim = values.shape[-1] // 2
    first_half = values[..., :half_dim]
    second_half = values[..., half_dim:]
    return jnp.concatenate(
        [first_half * cosine + second_half * sine, second_half * cosine - first_half * sine],
        axis=-1,
    )


def rope_tables(positions):
    half_dim = ROPE // 2
    inverse = 10000.0 ** (-jnp.arange(half_dim, dtype=jnp.float32) * 2.0 / ROPE)
    angles = positions[:, None] * inverse[None, :]
    return (jnp.cos(angles), jnp.sin(angles))


def swiglu(gate_in, up_in):
    return jax.nn.silu(gate_in) * up_in


def per_device(
    tokens,
    cotangent,
    chosen,
    attn_gain,
    w_query,
    w_kv_down,
    kv_gain,
    w_kv_up,
    w_out,
    ffn_gain,
    w_router,
    shared_gate,
    shared_up,
    shared_down,
    expert_gate,
    expert_up,
    expert_down,
):
    tok_rows = tokens.shape[0]
    seq_groups = lax.axis_size("sp")
    seq_len = tok_rows * seq_groups
    local_heads = HEADS // seq_groups
    qk_dim = NOPE + ROPE
    capacity = tok_rows * TOP * 5 // (4 * EXPERTS)
    slot_total = EXPERTS * capacity
    block_rows = min(512, seq_len)
    score_scale = qk_dim ** (-0.5)
    gain_one, query_w, down_w, latent_gain, up_w, out_w, gain_two = (
        lax.all_gather(attn_gain, "dp", axis=0, tiled=True),
        lax.all_gather(w_query, "dp", axis=0, tiled=True),
        lax.all_gather(w_kv_down, "dp", axis=0, tiled=True),
        lax.all_gather(kv_gain, "dp", axis=0, tiled=True),
        lax.all_gather(w_kv_up, "dp", axis=0, tiled=True),
        lax.all_gather(w_out, "dp", axis=0, tiled=True),
        lax.all_gather(ffn_gain, "dp", axis=0, tiled=True),
    )
    gain_one = gain_one.astype(jnp.float32)
    latent_gain = latent_gain.astype(jnp.float32)
    gain_two = gain_two.astype(jnp.float32)
    positions = (lax.axis_index("sp") * tok_rows + jnp.arange(tok_rows, dtype=jnp.int32)).astype(
        jnp.float32
    )
    cosine, sine = rope_tables(positions)
    resid_one = tokens.astype(jnp.float32)
    norm_one_out, norm_one_pull = jax.vjp(rms_norm, resid_one, gain_one)
    hidden_one = norm_one_out.astype(jnp.bfloat16)
    query_pre = jnp.dot(hidden_one, query_w, preferred_element_type=jnp.float32).reshape(
        tok_rows, HEADS, qk_dim
    )
    query_rot = jnp.concatenate(
        [
            query_pre[..., :NOPE],
            rotate(query_pre[..., NOPE:], cosine[:, None, :], sine[:, None, :]),
        ],
        axis=-1,
    )
    query_send = query_rot.reshape(tok_rows, HEADS * qk_dim).astype(jnp.bfloat16)
    compressed = jnp.dot(hidden_one, down_w, preferred_element_type=jnp.float32)
    latent_out, latent_pull = jax.vjp(rms_norm, compressed[:, :RANK], latent_gain)
    latent = latent_out.astype(jnp.bfloat16)
    key_rope = rotate(compressed[:, RANK:], cosine, sine)
    expanded = jnp.dot(latent, up_w, preferred_element_type=jnp.float32).reshape(
        tok_rows, HEADS, NOPE + VDIM
    )
    key_send = jnp.concatenate(
        [expanded[..., :NOPE], jnp.broadcast_to(key_rope[:, None, :], (tok_rows, HEADS, ROPE))],
        axis=-1,
    )
    key_send = key_send.reshape(tok_rows, HEADS * qk_dim).astype(jnp.bfloat16)
    value_send = expanded[..., NOPE:].reshape(tok_rows, HEADS * VDIM).astype(jnp.bfloat16)
    query_seq, key_seq, value_seq = (
        lax.all_to_all(query_send, "sp", split_axis=1, concat_axis=0, tiled=True),
        lax.all_to_all(key_send, "sp", split_axis=1, concat_axis=0, tiled=True),
        lax.all_to_all(value_send, "sp", split_axis=1, concat_axis=0, tiled=True),
    )
    query_seq = query_seq.reshape(seq_len, local_heads, qk_dim)
    key_seq = key_seq.reshape(seq_len, local_heads, qk_dim)
    value_seq = value_seq.reshape(seq_len, local_heads, VDIM)
    block_starts = jnp.arange(seq_len // block_rows, dtype=jnp.int32) * block_rows
    column_ids = jnp.arange(seq_len, dtype=jnp.int32)

    def masked_scores(query_block, begin_at):
        raw_scores = jnp.einsum(
            "qhc,khc->hqk", query_block, key_seq, preferred_element_type=jnp.float32
        )
        row_ids = begin_at + jnp.arange(block_rows, dtype=jnp.int32)
        allowed = column_ids[None, :] <= row_ids[:, None]
        return jnp.where(allowed[None], raw_scores * score_scale, -1000000000.0)

    def attend_block(begin_at):
        query_block = lax.dynamic_slice_in_dim(query_seq, begin_at, block_rows, 0)
        scores = masked_scores(query_block, begin_at)
        row_max = jnp.max(scores, axis=-1, keepdims=True)
        weights = jnp.exp(scores - row_max)
        row_total = jnp.sum(weights, axis=-1, keepdims=True)
        prob_rows = (weights / row_total).astype(jnp.bfloat16)
        mixed_block = jnp.einsum(
            "hqk,khc->qhc", prob_rows, value_seq, preferred_element_type=jnp.float32
        )
        return (mixed_block, row_max + jnp.log(row_total))

    head_out, log_totals = lax.map(attend_block, block_starts)
    head_out = head_out.reshape(seq_len, local_heads * VDIM).astype(jnp.bfloat16)
    attn_tok = lax.all_to_all(head_out, "sp", split_axis=0, concat_axis=1, tiled=True)
    attn_proj = jnp.dot(attn_tok, out_w, preferred_element_type=jnp.float32)
    resid_two = resid_one + attn_proj
    norm_two_out, norm_two_pull = jax.vjp(rms_norm, resid_two, gain_two)
    hidden_two = norm_two_out.astype(jnp.bfloat16)
    expert_ids = jnp.arange(EXPERTS, dtype=jnp.int32)
    picks = (chosen[:, :, None] == expert_ids[None, None, :]).astype(jnp.int32)
    flat_picks = picks.reshape(tok_rows * TOP, EXPERTS)
    earlier = jnp.cumsum(flat_picks, axis=0) - flat_picks
    slot_rank = jnp.sum(earlier * flat_picks, axis=1).reshape(tok_rows, TOP)
    slot_of = chosen * capacity + slot_rank
    slot_ids = jnp.arange(slot_total, dtype=jnp.int32)
    slot_match = slot_of[:, :, None] == slot_ids[None, None, :]
    dispatch = jnp.any(slot_match, axis=1).astype(jnp.bfloat16)
    routed_in = jnp.einsum("ts,td->sd", dispatch, hidden_two, preferred_element_type=jnp.float32)
    routed_in = routed_in.astype(jnp.bfloat16).reshape(EXPERTS, capacity, D)
    router_piece = lax.all_gather(w_router, "dp", axis=0, tiled=True)
    gate_s_piece = lax.all_gather(shared_gate, "dp", axis=0, tiled=True)
    up_s_piece = lax.all_gather(shared_up, "dp", axis=0, tiled=True)
    gate_r_piece = lax.all_gather(expert_gate, "dp", axis=0, tiled=True)
    up_r_piece = lax.all_gather(expert_up, "dp", axis=0, tiled=True)
    columns = hidden_two
    routed_cols = routed_in
    logits = jnp.dot(columns, router_piece, preferred_element_type=jnp.float32)
    gate_shared = jnp.einsum(
        "td,dsf->tsf", columns, gate_s_piece, preferred_element_type=jnp.float32
    )
    up_shared = jnp.einsum("td,dsf->tsf", columns, up_s_piece, preferred_element_type=jnp.float32)
    gate_routed = jnp.einsum(
        "ecd,def->ecf", routed_cols, gate_r_piece, preferred_element_type=jnp.float32
    )
    up_routed = jnp.einsum(
        "ecd,def->ecf", routed_cols, up_r_piece, preferred_element_type=jnp.float32
    )
    router = jax.nn.softmax(logits, axis=-1)
    gate_pick = jnp.take_along_axis(router, chosen, axis=1)
    combine = jnp.sum(gate_pick[:, :, None] * slot_match.astype(jnp.float32), axis=1)
    act_shared_f, shared_pull = jax.vjp(swiglu, gate_shared, up_shared)
    act_routed_f, routed_pull = jax.vjp(swiglu, gate_routed, up_routed)
    act_shared = act_shared_f.astype(jnp.bfloat16)
    act_routed = act_routed_f.astype(jnp.bfloat16)
    shared_piece = lax.all_gather(shared_down, "dp", axis=0, tiled=True)
    routed_piece = lax.all_gather(expert_down, "dp", axis=0, tiled=True)
    shared_cols = act_shared
    routed_cols = act_routed
    shared_out = jnp.einsum(
        "tsf,fsd->td", shared_cols, shared_piece, preferred_element_type=jnp.float32
    )
    routed_out = jnp.einsum(
        "ecf,fed->ecd", routed_cols, routed_piece, preferred_element_type=jnp.float32
    )
    routed_flat = routed_out.reshape(slot_total, D)
    mixed = resid_two + shared_out + jnp.dot(combine, routed_flat, precision=highest)
    upstream = cotangent.astype(jnp.float32)
    routed_grad = (
        jnp.einsum("ts,td->sd", combine, upstream, precision=highest)
        .astype(jnp.bfloat16)
        .reshape(EXPERTS, capacity, D)
    )
    routed_rows = jnp.take(routed_flat, slot_of.reshape(-1), axis=0).reshape(tok_rows, TOP, D)
    gate_grad = jnp.sum(routed_rows * upstream[:, None, :], axis=-1)
    prob_grad = jnp.sum(gate_grad[:, :, None] * picks.astype(jnp.float32), axis=1)
    logit_grad = (
        router * (prob_grad - jnp.sum(router * prob_grad, axis=-1, keepdims=True))
    ).astype(jnp.bfloat16)
    shared_piece = lax.all_gather(shared_down, "dp", axis=0, tiled=True)
    routed_piece = lax.all_gather(expert_down, "dp", axis=0, tiled=True)
    shared_part = jnp.einsum(
        "td,fsd->tsf", cotangent, shared_piece, preferred_element_type=jnp.float32
    )
    routed_part = jnp.einsum(
        "ecd,fed->ecf", routed_grad, routed_piece, preferred_element_type=jnp.float32
    )
    act_shared_grad = shared_part
    act_routed_grad = routed_part
    gate_shared_grad, up_shared_grad = shared_pull(act_shared_grad)
    gate_routed_grad, up_routed_grad = routed_pull(act_routed_grad)
    gate_shared_grad = gate_shared_grad.astype(jnp.bfloat16)
    up_shared_grad = up_shared_grad.astype(jnp.bfloat16)
    gate_routed_grad = gate_routed_grad.astype(jnp.bfloat16)
    up_routed_grad = up_routed_grad.astype(jnp.bfloat16)
    router_piece = lax.all_gather(w_router, "dp", axis=0, tiled=True)
    gate_s_piece = lax.all_gather(shared_gate, "dp", axis=0, tiled=True)
    up_s_piece = lax.all_gather(shared_up, "dp", axis=0, tiled=True)
    gate_r_piece = lax.all_gather(expert_gate, "dp", axis=0, tiled=True)
    up_r_piece = lax.all_gather(expert_up, "dp", axis=0, tiled=True)
    hidden_part = (
        jnp.einsum("te,de->td", logit_grad, router_piece, preferred_element_type=jnp.float32)
        + jnp.einsum(
            "tsf,dsf->td", gate_shared_grad, gate_s_piece, preferred_element_type=jnp.float32
        )
        + jnp.einsum("tsf,dsf->td", up_shared_grad, up_s_piece, preferred_element_type=jnp.float32)
    )
    routed_part = jnp.einsum(
        "ecf,def->ecd", gate_routed_grad, gate_r_piece, preferred_element_type=jnp.float32
    ) + jnp.einsum("ecf,def->ecd", up_routed_grad, up_r_piece, preferred_element_type=jnp.float32)
    routed_in_grad = routed_part
    hidden_two_grad = hidden_part + jnp.einsum(
        "ts,sd->td",
        dispatch.astype(jnp.float32),
        routed_in_grad.reshape(slot_total, D),
        precision=highest,
    )
    resid_two_norm_grad, gain_two_grad = norm_two_pull(hidden_two_grad)
    resid_two_grad = upstream + resid_two_norm_grad
    in_rows = w_router.shape[0]
    out_rows = shared_down.shape[0]
    router_grad = jnp.einsum(
        "td,te->de", hidden_two, logit_grad, preferred_element_type=jnp.float32
    )
    row_count = lax.axis_size("dp") * in_rows
    columns = hidden_two
    routed_cols = routed_in
    ffn_in_share = lax.psum_scatter(
        jnp.concatenate(
            [
                jnp.einsum(
                    "td,tsf->dsf", columns, gate_shared_grad, preferred_element_type=jnp.float32
                ).reshape(row_count, NS * FE),
                jnp.einsum(
                    "td,tsf->dsf", columns, up_shared_grad, preferred_element_type=jnp.float32
                ).reshape(row_count, NS * FE),
                jnp.einsum(
                    "ecd,ecf->def",
                    routed_cols,
                    gate_routed_grad,
                    preferred_element_type=jnp.float32,
                ).reshape(row_count, EXPERTS * FE),
                jnp.einsum(
                    "ecd,ecf->def", routed_cols, up_routed_grad, preferred_element_type=jnp.float32
                ).reshape(row_count, EXPERTS * FE),
            ],
            axis=1,
        ).astype(jnp.bfloat16),
        "dp",
        scatter_dimension=0,
        tiled=True,
    )
    shared_cols = act_shared
    routed_cols = act_routed
    shared_part = jnp.einsum(
        "tsf,td->fsd", shared_cols, cotangent, preferred_element_type=jnp.float32
    )
    routed_part = jnp.einsum(
        "ecf,ecd->fed", routed_cols, routed_grad, preferred_element_type=jnp.float32
    )
    ffn_out_share = lax.psum_scatter(
        jnp.concatenate([shared_part, routed_part], axis=1)
        .reshape(lax.axis_size("dp") * out_rows, (NS + EXPERTS) * D)
        .astype(jnp.bfloat16),
        "dp",
        scatter_dimension=0,
        tiled=True,
    )
    proj_grad = resid_two_grad.astype(jnp.bfloat16)
    out_w_grad = jnp.einsum("tc,td->cd", attn_tok, proj_grad, preferred_element_type=jnp.float32)
    attn_tok_grad = jnp.einsum(
        "td,cd->tc", proj_grad, out_w, preferred_element_type=jnp.float32
    ).astype(jnp.bfloat16)
    head_out_grad = lax.all_to_all(
        attn_tok_grad, "sp", split_axis=1, concat_axis=0, tiled=True
    ).reshape(seq_len, local_heads, VDIM)

    def back_block(carry, inputs):
        key_acc, value_acc = carry
        begin_at, log_total = inputs
        query_block = lax.dynamic_slice_in_dim(query_seq, begin_at, block_rows, 0)
        out_block_grad = lax.dynamic_slice_in_dim(head_out_grad, begin_at, block_rows, 0)
        scores = masked_scores(query_block, begin_at)
        prob_block = jnp.exp(scores - log_total)
        prob_block_grad = jnp.einsum(
            "qhc,khc->hqk", out_block_grad, value_seq, preferred_element_type=jnp.float32
        )
        row_delta = jnp.sum(prob_block * prob_block_grad, axis=-1, keepdims=True)
        score_grad = (prob_block * (prob_block_grad - row_delta) * score_scale).astype(jnp.bfloat16)
        query_block_grad = jnp.einsum(
            "hqk,khc->qhc", score_grad, key_seq, preferred_element_type=jnp.float32
        )
        key_acc = key_acc + jnp.einsum(
            "hqk,qhc->khc", score_grad, query_block, preferred_element_type=jnp.float32
        )
        value_acc = value_acc + jnp.einsum(
            "hqk,qhc->khc",
            prob_block.astype(jnp.bfloat16),
            out_block_grad,
            preferred_element_type=jnp.float32,
        )
        return ((key_acc, value_acc), query_block_grad)

    acc_init = (
        jnp.zeros((seq_len, local_heads, qk_dim), jnp.float32),
        jnp.zeros((seq_len, local_heads, VDIM), jnp.float32),
    )
    (key_grad, value_grad), query_grad = lax.scan(back_block, acc_init, (block_starts, log_totals))
    query_grad = query_grad.reshape(seq_len, local_heads * qk_dim).astype(jnp.bfloat16)
    key_grad = key_grad.reshape(seq_len, local_heads * qk_dim).astype(jnp.bfloat16)
    value_grad = value_grad.reshape(seq_len, local_heads * VDIM).astype(jnp.bfloat16)
    query_back, key_back, value_back = (
        lax.all_to_all(query_grad, "sp", split_axis=0, concat_axis=1, tiled=True),
        lax.all_to_all(key_grad, "sp", split_axis=0, concat_axis=1, tiled=True),
        lax.all_to_all(value_grad, "sp", split_axis=0, concat_axis=1, tiled=True),
    )
    query_back = query_back.astype(jnp.float32).reshape(tok_rows, HEADS, qk_dim)
    query_pre_grad = jnp.concatenate(
        [
            query_back[..., :NOPE],
            unrotate(query_back[..., NOPE:], cosine[:, None, :], sine[:, None, :]),
        ],
        axis=-1,
    )
    query_pre_grad = query_pre_grad.reshape(tok_rows, HEADS * qk_dim).astype(jnp.bfloat16)
    key_back = key_back.reshape(tok_rows, HEADS, qk_dim)
    key_rope_grad = unrotate(
        jnp.sum(key_back[..., NOPE:].astype(jnp.float32), axis=1), cosine, sine
    )
    expanded_grad = jnp.concatenate(
        [key_back[..., :NOPE], value_back.reshape(tok_rows, HEADS, VDIM)], axis=-1
    ).reshape(tok_rows, HEADS * (NOPE + VDIM))
    up_w_grad = jnp.einsum("tr,tc->rc", latent, expanded_grad, preferred_element_type=jnp.float32)
    latent_grad = jnp.einsum("tc,rc->tr", expanded_grad, up_w, preferred_element_type=jnp.float32)
    latent_in_grad, latent_gain_grad = latent_pull(latent_grad)
    compressed_grad = jnp.concatenate([latent_in_grad, key_rope_grad], axis=-1).astype(jnp.bfloat16)
    down_w_grad = jnp.einsum(
        "td,tc->dc", hidden_one, compressed_grad, preferred_element_type=jnp.float32
    )
    query_w_grad = jnp.einsum(
        "td,tc->dc", hidden_one, query_pre_grad, preferred_element_type=jnp.float32
    )
    hidden_one_grad = jnp.einsum(
        "tc,dc->td", query_pre_grad, query_w, preferred_element_type=jnp.float32
    ) + jnp.einsum("tc,dc->td", compressed_grad, down_w, preferred_element_type=jnp.float32)
    resid_one_grad, gain_one_grad = norm_one_pull(hidden_one_grad)
    tokens_grad = (resid_two_grad + resid_one_grad).astype(jnp.bfloat16)
    (
        gain_one_share,
        query_share,
        down_share,
        latent_gain_share,
        up_share,
        out_share,
        gain_two_share,
        router_share,
    ) = (
        lax.psum_scatter(
            gain_one_grad.astype(jnp.bfloat16), "dp", scatter_dimension=0, tiled=True
        ).astype(jnp.float32),
        lax.psum_scatter(
            query_w_grad.astype(jnp.bfloat16), "dp", scatter_dimension=0, tiled=True
        ).astype(jnp.float32),
        lax.psum_scatter(
            down_w_grad.astype(jnp.bfloat16), "dp", scatter_dimension=0, tiled=True
        ).astype(jnp.float32),
        lax.psum_scatter(
            latent_gain_grad.astype(jnp.bfloat16), "dp", scatter_dimension=0, tiled=True
        ).astype(jnp.float32),
        lax.psum_scatter(
            up_w_grad.astype(jnp.bfloat16), "dp", scatter_dimension=0, tiled=True
        ).astype(jnp.float32),
        lax.psum_scatter(
            out_w_grad.astype(jnp.bfloat16), "dp", scatter_dimension=0, tiled=True
        ).astype(jnp.float32),
        lax.psum_scatter(
            gain_two_grad.astype(jnp.bfloat16), "dp", scatter_dimension=0, tiled=True
        ).astype(jnp.float32),
        lax.psum_scatter(
            router_grad.astype(jnp.bfloat16), "dp", scatter_dimension=0, tiled=True
        ).astype(jnp.float32),
    )
    (
        gain_one_total,
        query_total,
        down_total,
        latent_gain_total,
        up_total,
        out_total,
        gain_two_total,
        router_total,
        ffn_in_total,
        ffn_out_total,
    ) = (
        lax.psum(gain_one_share.astype(jnp.bfloat16), "sp").astype(jnp.float32),
        lax.psum(query_share.astype(jnp.bfloat16), "sp").astype(jnp.float32),
        lax.psum(down_share.astype(jnp.bfloat16), "sp").astype(jnp.float32),
        lax.psum(latent_gain_share.astype(jnp.bfloat16), "sp").astype(jnp.float32),
        lax.psum(up_share.astype(jnp.bfloat16), "sp").astype(jnp.float32),
        lax.psum(out_share.astype(jnp.bfloat16), "sp").astype(jnp.float32),
        lax.psum(gain_two_share.astype(jnp.bfloat16), "sp").astype(jnp.float32),
        lax.psum(router_share.astype(jnp.bfloat16), "sp").astype(jnp.float32),
        lax.psum(ffn_in_share, "sp").astype(jnp.float32),
        lax.psum(ffn_out_share, "sp").astype(jnp.float32),
    )
    width_shared = NS * FE
    width_routed = EXPERTS * FE
    shared_gate_grad = ffn_in_total[:, :width_shared].reshape(in_rows, NS, FE)
    shared_up_grad = ffn_in_total[:, width_shared : 2 * width_shared].reshape(in_rows, NS, FE)
    expert_gate_grad = ffn_in_total[:, 2 * width_shared : 2 * width_shared + width_routed].reshape(
        in_rows, EXPERTS, FE
    )
    expert_up_grad = ffn_in_total[:, 2 * width_shared + width_routed :].reshape(
        in_rows, EXPERTS, FE
    )
    down_total_all = ffn_out_total.reshape(out_rows, NS + EXPERTS, D)
    shared_down_grad = down_total_all[:, :NS, :]
    expert_down_grad = down_total_all[:, NS:, :]
    return (
        mixed.astype(jnp.bfloat16),
        tokens_grad,
        gain_one_total,
        query_total,
        down_total,
        latent_gain_total,
        up_total,
        out_total,
        gain_two_total,
        router_total,
        shared_gate_grad,
        shared_up_grad,
        shared_down_grad,
        expert_gate_grad,
        expert_up_grad,
        expert_down_grad,
    )


def solution(mesh):
    placed = (
        P(("dp", "sp"), None),
        P(("dp", "sp"), None),
        P(("dp", "sp"), None),
        P("dp"),
        P("dp", None),
        P("dp", None),
        P("dp"),
        P("dp", None),
        P("dp", None),
        P("dp"),
        P("dp", None),
        P("dp", None, None),
        P("dp", None, None),
        P("dp", None, None),
        P("dp", None, None),
        P("dp", None, None),
        P("dp", None, None),
    )
    return jax.shard_map(
        per_device,
        mesh=mesh,
        in_specs=placed,
        out_specs=(
            P(("dp", "sp"), None),
            P(("dp", "sp"), None),
            P("dp"),
            P("dp", None),
            P("dp", None),
            P("dp"),
            P("dp", None),
            P("dp", None),
            P("dp"),
            P("dp", None),
            P("dp", None, None),
            P("dp", None, None),
            P("dp", None, None),
            P("dp", None, None),
            P("dp", None, None),
            P("dp", None, None),
        ),
        check_vma=False,
    )
```

profile of v0, /device:TPU:1, one launch (start us, length us, event | category | flops | bytes accessed | tf_op | source)
XLA Modules:
  0.0 2813.8 jit_solution(7378826893160408970)
XLA Ops:
  24.7 28.2 %all-reduce = bf16[512]{0:T(512)(128)(2,1)S(1)} all-reduce(bf16[512]{0:T(512)(128)(2,1)S(1)} %dynamic-update-slice), channel_id=1, replica_groups=mesh['dp'=16,'sp'=8] {'dp'}, use_global_device_ids=true, to_apply=%add | all-reduce | flops 512 | bytes 2048
  52.9 19.5 all-gather
  72.4 17.8 all-gather.1
  108.6 14.1 all-to-all-done.2
  126.7 51.7 %all-gather.13.cloned.1.call-done = bf16[2048,3072]{1,0:T(8,128)(2,1)} async-done(((bf16[128,3072]{1,0:T(8,128)(2,1)}), bf16[2048,3072]{1,0:T(8,128)(2,1)}) %all-gather.13.cloned.1.call-update) | async-done | bytes 12582928 | tf_op jit(solution)/shard_map/all_gather | solution.py:89
  199.2 27.6 all_gather.59
  233.6 19.5 while.28
  275.2 37.0 %all-gather.19.cloned.1.call-done = bf16[2048,2048]{1,0:T(8,128)(2,1)} async-done(((bf16[128,2048]{1,0:T(8,128)(2,1)}), bf16[2048,2048]{1,0:T(8,128)(2,1)}) %all-gather.19.cloned.1.call-update) | async-done | bytes 8388624 | tf_op jit(solution)/shard_map/all_gather | solution.py:93
  318.4 62.8 %all-gather.23.cloned.1.call-done = bf16[2048,2,1408]{2,0,1:T(8,128)(2,1)} async-done(((bf16[128,2,1408]{2,0,1:T(8,128)(2,1)}), bf16[2048,2,1408]{2,0,1:T(8,128)(2,1)}) %all-gather.23.cloned.1.call-update) | async-done | bytes 11534352 | tf_op jit(solution)/shard_map/all_gather | solution.py:181
  388.3 62.5 %all-gather.21.cloned.1.call-done = bf16[2048,2,1408]{2,0,1:T(8,128)(2,1)} async-done(((bf16[128,2,1408]{2,0,1:T(8,128)(2,1)}), bf16[2048,2,1408]{2,0,1:T(8,128)(2,1)}) %all-gather.21.cloned.1.call-update) | async-done | bytes 11534352 | tf_op jit(solution)/shard_map/all_gather | solution.py:180
  473.0 102.2 %all-gather.27.cloned.1.call-done = bf16[2048,4,1408]{2,0,1:T(8,128)(2,1)} async-done(((bf16[128,4,1408]{2,0,1:T(8,128)(2,1)}), bf16[2048,4,1408]{2,0,1:T(8,128)(2,1)}) %all-gather.27.cloned.1.call-update) | async-done | bytes 23068688 | tf_op jit(solution)/shard_map/all_gather | solution.py:182
  584.9 114.7 %all-gather.29.cloned.1.call-done = bf16[2048,4,1408]{2,0,1:T(8,128)(2,1)} async-done(((bf16[128,4,1408]{2,0,1:T(8,128)(2,1)}), bf16[2048,4,1408]{2,0,1:T(8,128)(2,1)}) %all-gather.29.cloned.1.call-update) | async-done | bytes 23068688 | tf_op jit(solution)/shard_map/all_gather | solution.py:183
  699.7 13.1 multiply_convert_fusion.2
  712.8 111.1 %all-gather.31.cloned.1.call-done = bf16[1408,4,2048]{2,0,1:T(8,128)(2,1)} async-done(((bf16[88,4,2048]{2,0,1:T(8,128)(2,1)}), bf16[1408,4,2048]{2,0,1:T(8,128)(2,1)}) %all-gather.31.cloned.1.call-update) | async-done | bytes 23068688 | tf_op jit(solution)/shard_map/all_gather | solution.py:205
  844.5 13.1 multiply_convert_fusion.1
  870.5 14.9 convolution_add_fusion
  917.6 57.7 %while.29 = (s32[]{:T(128)}, f32[1024,2,192]{0,2,1:T(8,128)}, f32[1024,2,128]{0,2,1:T(8,128)S(1)}, bf16[2,512,2,192]{1,3,2,0:T(8,128)(2,1)}, s32[2]{0:T(128)S(1)...) while((s32[]{:T(128)}, f32[1024,2,192]{0,2,1:T(8,128)}, ...), condition=%wide.region_20.21_spmd.clone, body=%wide.region_18.20_spmd.clone.sunk | while | flops 1761350144 | bytes 73416944 | solution.py:356
  1027.2 15.8 copy.288
  1053.9 23.7 pad_maximum_fusion.1
  1077.6 44.7 %copy.289 = bf16[1408,12288]{1,0:T(8,128)(2,1)} copy(bf16[1408,12288]{0,1:T(8,128)(2,1)} %bitcast.238) | data formatting | bytes 69206016 | tf_op jit(solution)/shard_map/convert_element_type | solution.py:312
  1157.5 95.3 %pad_maximum_fusion = bf16[2048,16896]{0,1:T(8,128)(2,1)} fusion(bf16[2048,5632]{0,1:T(8,128)(2,1)} %bitcast.239, bf16[2048,5632]{0,1:T(8,128)(2,1)} %bitcast.240, bf16[2048,2816]{0,1:T(8,128)(2,1)} %bitcast.245, bf16[2048,2816]{0,1:T(8,128)(2,1)} %bitcast.246), kind=kLoop, calls=%fused_computation.52 | loop fusion | flops 276824064 | bytes 138412032 | tf_op jit(solution)/shard_map/concatenate | solution.py:277
  1252.9 85.9 %copy.306 = bf16[2048,16896]{1,0:T(8,128)(2,1)} copy(bf16[2048,16896]{0,1:T(8,128)(2,1)} %pad_maximum_fusion) | data formatting | bytes 138412032
  1354.7 24.6 all_to_all.107
  1390.2 100.3 %reduce-scatter.29.cloned.1.call-done = bf16[88,12288]{1,0:T(8,128)(2,1)} async-done(((bf16[1408,12288]{1,0:T(8,128)(2,1)}), bf16[88,12288]{1,0:T(8,128)(2,1)}) %reduce-scatter.29.cloned.1.call-update) | async-done | bytes 2162704
  1496.3 704.5 %reduce-scatter.27.cloned.1.call-done = bf16[128,16896]{1,0:T(8,128)(2,1)} async-done(((bf16[2048,16896]{1,0:T(8,128)(2,1)}), bf16[128,16896]{1,0:T(8,128)(2,1)}) %reduce-scatter.27.cloned.1.call-update) | async-done | bytes 4325392
  2207.3 63.5 %reduce-scatter.19.cloned.1.call-done = bf16[32,4096]{1,0:T(8,128)(2,1)} async-done(((bf16[512,4096]{1,0:T(8,128)(2,1)}), bf16[32,4096]{1,0:T(8,128)(2,1)}) %reduce-scatter.19.cloned.1.call-update) | async-done | bytes 262160 | tf_op jit(solution)/shard_map/reduce_scatter | solution.py:418
  2270.8 99.5 %reduce-scatter.21.cloned.1.call-done = bf16[128,2048]{1,0:T(8,128)(2,1)} async-done(((bf16[2048,2048]{1,0:T(8,128)(2,1)}), bf16[128,2048]{1,0:T(8,128)(2,1)}) %reduce-scatter.21.cloned.1.call-update) | async-done | bytes 524304 | tf_op jit(solution)/shard_map/reduce_scatter | solution.py:421
  2370.2 141.2 %reduce-scatter.17.cloned.1.call-done = bf16[128,3072]{1,0:T(8,128)(2,1)} async-done(((bf16[2048,3072]{1,0:T(8,128)(2,1)}), bf16[128,3072]{1,0:T(8,128)(2,1)}) %reduce-scatter.17.cloned.1.call-update) | async-done | bytes 786448 | tf_op jit(solution)/shard_map/reduce_scatter | solution.py:409
  2521.9 49.8 %reduce-scatter.25.cloned.1.call-done = bf16[128,4]{1,0:T(8,128)(2,1)} async-done(((bf16[2048,4]{1,0:T(8,128)(2,1)}), bf16[128,4]{1,0:T(8,128)(2,1)}) %reduce-scatter.25.cloned.1.call-update) | async-done | bytes 1040
  2583.4 35.3 %all-reduce.5 = (bf16[2048]{0:T(1024)(128)(2,1)S(1)}, bf16[512]{0:T(512)(128)(2,1)S(1)}, bf16[2048]{0:T(1024)(128)(2,1)S(1)}) all-reduce(bf16[2048]{0:T(1024)(128)(2,1)S(1)} %get-tuple-element.309, bf16[512]{0:T(512)(128)(2,1)S(1)} %copy-done.88, bf16[2048]{0:T(1024)(128)(2,1)S(1)} %copy-done.76), channel_id=2, replica_groups=mesh['dp'=16,'sp'=8] {'dp'}, use_global_device_ids=true, to_apply=%region_25.26.clone | all-reduce | flops 4608 | bytes 18432
  2618.9 23.2 all-reduce.6
  2646.6 131.5 %all-reduce.10.cloned.1.call-done = (bf16[128,16896]{0,1:T(8,128)(2,1)}, bf16[88,6,2048]{2,1,0:T(8,128)(2,1)}, bf16[128,3072]{1,0:T(8,128)(2,1)}, bf16[128,576]{...) async-done(((bf16[128,16896]{0,1:T(8,128)(2,1)}, bf16[88,6,2048]{2,1,0:T(8,128)(2,1)}, bf16[128,3072]{1,0:T(8,128)(2,1)}, ...) | async-done | bytes 8208400 | tf_op jit(solution)/shard_map/psum | solution.py:451
  (454 shorter events, 458.6 us)
Async XLA Ops:
  7.2 85.6 %all-gather.15.cloned.1.call-start = ((), (), s32[]{:S(2)}) async-start(), calls=%async_computation.16 | async-start | bytes 2506752 | tf_op jit(solution)/shard_map/all_gather | solution.py:90
  7.9 87.6 %all-gather.17.cloned.1.call-start = ((), (), s32[]{:S(2)}) async-start(), calls=%async_computation.17 | async-start | bytes 4456448 | tf_op jit(solution)/shard_map/all_gather | solution.py:92
  8.7 169.7 %all-gather.13.cloned.1.call-start = ((), (), s32[]{:S(2)}) async-start(), calls=%async_computation.15 | async-start | bytes 13369344 | tf_op jit(solution)/shard_map/all_gather | solution.py:89
  9.4 254.8 %all-gather.25.cloned.1.call-start = ((), (), s32[]{:S(2)}) async-start(), calls=%async_computation.21 | async-start | bytes 12255232 | tf_op jit(solution)/shard_map/all_gather | solution.py:204
  11.7 300.5 %all-gather.19.cloned.1.call-start = ((), (), s32[]{:S(2)}) async-start(), calls=%async_computation.18 | async-start | bytes 8912896 | tf_op jit(solution)/shard_map/all_gather | solution.py:93
  12.3 368.9 %all-gather.23.cloned.1.call-start = ((), (), s32[]{:S(2)}) async-start(), calls=%async_computation.20 | async-start | bytes 12255232 | tf_op jit(solution)/shard_map/all_gather | solution.py:181
  14.5 436.3 %all-gather.21.cloned.1.call-start = ((), (), s32[]{:S(2)}) async-start(), calls=%async_computation.19 | async-start | bytes 12255232 | tf_op jit(solution)/shard_map/all_gather | solution.py:180
  16.6 558.6 %all-gather.27.cloned.1.call-start = ((), (), s32[]{:S(2)}) async-start(), calls=%async_computation.22 | async-start | bytes 24510464 | tf_op jit(solution)/shard_map/all_gather | solution.py:182
  18.0 681.7 %all-gather.29.cloned.1.call-start = ((), (), s32[]{:S(2)}) async-start(), calls=%async_computation.23 | async-start | bytes 24510464 | tf_op jit(solution)/shard_map/all_gather | solution.py:183
  19.3 804.6 %all-gather.31.cloned.1.call-start = ((), (), s32[]{:S(2)}) async-start(), calls=%async_computation.24 | async-start | bytes 24510464 | tf_op jit(solution)/shard_map/all_gather | solution.py:205
  72.4 106.0 %copy-start.53 = (f32[16,1,128]{2,1,0:T(1,128)}, f32[16,1,128]{2,1,0:T(1,128)S(1)}, u32[]{:S(2)}) copy-start(f32[16,1,128]{2,1,0:T(1,128)S(1)} %convert_element_type.289) | copy-start | bytes 24580
  92.6 85.8 %copy-start.73 = (f32[128]{0:T(128)}, f32[128]{0:T(128)S(1)}, u32[]{:S(2)}) copy-start(f32[128]{0:T(128)S(1)} %fusion.108) | copy-start | bytes 1540
  92.8 93.8 %copy-start.61 = (f32[128,32]{0,1:T(8,128)}, f32[128,32]{0,1:T(8,128)S(1)}, u32[]{:S(2)}) copy-start(f32[128,32]{0,1:T(8,128)S(1)} %get-tuple-element.385) | copy-start | bytes 49156
  92.8 93.8 %copy-start.63 = (f32[128,32]{0,1:T(8,128)}, f32[128,32]{0,1:T(8,128)S(1)}, u32[]{:S(2)}) copy-start(f32[128,32]{0,1:T(8,128)S(1)} %get-tuple-element.386) | copy-start | bytes 49156
  100.1 22.6 all-to-all-start.2
  122.7 65.0 %all-to-all-start.1 = ((bf16[128,8,384]{0,2,1:T(8,128)(2,1)}), bf16[128,8,384]{0,2,1:T(8,128)(2,1)S(1)}, u32[]{:S(2)}, u32[]{:S(2)}) async-start(bf16[128,8,384]{0,2,1:T(8,128)(2,1)} %bitcast.6), calls=%async_computation.1 | async-start | bytes 1572864 | tf_op jit(solution)/shard_map/all_to_all | solution.py:132
  187.7 43.1 %all-to-all-start = ((bf16[128,8,384]{0,2,1:T(8,128)(2,1)}), bf16[128,8,384]{0,2,1:T(8,128)(2,1)}, u32[]{:S(2)}, u32[]{:S(2)}) async-start(bf16[128,8,384]{0,2,1:T(8,128)(2,1)} %bitcast.3), calls=%async_computation | async-start | bytes 1572864 | tf_op jit(solution)/shard_map/all_to_all | solution.py:131
  256.9 18.0 all-to-all-start.3
  317.1 133.7 %copy-start.11 = (bf16[128,2048]{1,0:T(8,128)(2,1)}, bf16[128,2048]{1,0:T(8,128)(2,1)S(1)}, u32[]{:S(2)}) copy-start(bf16[128,2048]{1,0:T(8,128)(2,1)S(1)} %multiply_convert_fusion.5) | copy-start | bytes 1572868
  318.4 381.3 %copy-start.4 = (bf16[320,2048]{1,0:T(8,128)(2,1)}, bf16[320,2048]{1,0:T(8,128)(2,1)S(1)}, u32[]{:S(2)}) copy-start(bf16[320,2048]{1,0:T(8,128)(2,1)S(1)} %convolution_convert_fusion.11) | copy-start | bytes 3932164
  584.9 127.9 %copy-start.6 = (f32[4,80,1408]{2,1,0:T(8,128)}, f32[4,80,1408]{2,1,0:T(8,128)S(1)}, u32[]{:S(2)}) copy-start(f32[4,80,1408]{2,1,0:T(8,128)S(1)} %fusion.125) | copy-start | bytes 5406724
  898.4 16.8 all-to-all-start.4
  978.1 15.6 all-to-all-start.6
  993.6 15.9 all-to-all-start.7
  1000.4 388.1 %reduce-scatter.23.cloned.1.call-start = ((), (), s32[]{:S(2)}) async-start(), calls=%async_computation.28 | async-start | bytes 2785280
  1021.2 469.4 %reduce-scatter.29.cloned.1.call-start = ((), (), s32[]{:S(2)}) async-start(), calls=%async_computation.31 | async-start | bytes 36765696
  1122.3 1078.5 %reduce-scatter.27.cloned.1.call-start = ((), (), s32[]{:S(2)}) async-start(), calls=%async_computation.30 | async-start | bytes 73531392
  1338.8 932.0 %reduce-scatter.19.cloned.1.call-start = ((), (), s32[]{:S(2)}) async-start(), calls=%async_computation.26 | async-start | bytes 4456448 | tf_op jit(solution)/shard_map/reduce_scatter | solution.py:418
  1344.3 1025.9 %reduce-scatter.21.cloned.1.call-start = ((), (), s32[]{:S(2)}) async-start(), calls=%async_computation.27 | async-start | bytes 8912896 | tf_op jit(solution)/shard_map/reduce_scatter | solution.py:421
  1350.0 1161.4 %reduce-scatter.17.cloned.1.call-start = ((), (), s32[]{:S(2)}) async-start(), calls=%async_computation.25 | async-start | bytes 13369344 | tf_op jit(solution)/shard_map/reduce_scatter | solution.py:409
  1386.3 1185.4 %reduce-scatter.25.cloned.1.call-start = ((), (), s32[]{:S(2)}) async-start(), calls=%async_computation.29 | async-start | bytes 557056
  1388.2 1390.0 %all-reduce.10.cloned.1.call-start = ((), (), s32[]{:S(2)}) async-start(), calls=%async_computation.32 | async-start | bytes 17858560 | tf_op jit(solution)/shard_map/psum | solution.py:451
  (92 other events, 1099.4 us)
Sparse Core Ops, SparseCore 0:
  9.6 41.9 all-gather.14
  53.3 37.4 all-gather.16
  92.6 85.7 all-gather.12
  180.5 76.1 all-gather.24
  258.3 53.8 all-gather.18
  314.3 66.9 all-gather.22
  382.9 67.8 all-gather.20
  453.0 122.1 all-gather.26
  577.5 122.1 all-gather.28
  701.7 122.1 all-gather.30
  1021.3 62.2 reduce-scatter.22
  1122.4 368.0 reduce-scatter.28
  1493.0 707.7 reduce-scatter.26
  2203.1 67.6 reduce-scatter.18
  2273.0 97.1 reduce-scatter.20
  2372.5 138.8 reduce-scatter.16
  2514.1 57.5 reduce-scatter.24
  2576.0 202.1 all-reduce.9
where the time goes:
time: 2830 us; the launch traced here: 2810 us
  waiting for transfers between devices  1880 us (66%)
  matrix products  294 us (10%)
  local copies, waits for them, and re-layouts  252 us (9%)
  blocking collectives  176 us (6%)
  other arithmetic  144 us (5%)
  starting transfers between devices  44.7 us (2%)
    unnamed x22, waiting for transfers between devices  857 us
    reduce_scatter x1, waiting for transfers between devices, per_device(): lax.psum_scatter(query_w_grad.astype(jnp.bfloat16), 'dp', scatter_dimensi...  141 us
    unnamed x212, local copies, waits for them, and re-layouts  134 us
    psum x1, waiting for transfers between devices, per_device(): lax.psum(ffn_in_share, 'sp').astype(jnp.float32)  132 us
    all_gather x1, waiting for transfers between devices, per_device(): up_r_piece = lax.all_gather(expert_up, 'dp', axis=0, tiled=True)  115 us
    all_gather x1, waiting for transfers between devices, per_device(): routed_piece = lax.all_gather(expert_down, 'dp', axis=0, tiled=True)  111 us
    all_gather x1, waiting for transfers between devices, per_device(): gate_r_piece = lax.all_gather(expert_gate, 'dp', axis=0, tiled=True)  102 us
    reduce_scatter x1, waiting for transfers between devices, per_device(): lax.psum_scatter(out_w_grad.astype(jnp.bfloat16), 'dp', scatter_dimension...  99.5 us
  transfers between devices with their start and end apart: 25, of which 19 were waited for; matrix products, arithmetic and copies ran while one was open for 18% of the time, Pallas kernels for 0%

commit v1 on v0

v1 whole, which is shorter than its diff:
```python
import functools

import jax
import jax.numpy as jnp
from jax import lax
from jax.experimental import pallas as pl
from jax.experimental.pallas import tpu as pltpu
from jax.sharding import PartitionSpec as P

D = 2048
HEADS = 16
NOPE = 128
ROPE = 64
QK = NOPE + ROPE
VDIM = 128
RANK = 512
FE = 1408
NS = 2
EXPERTS = 4
TOP = 2
SETS = NS + EXPERTS
DP = 16
SP = 8
ROWS = 128
SEQ = SP * ROWS
GROUP = DP * ROWS
HEADS_HERE = HEADS // SP
QW = HEADS_HERE * QK
KVW = HEADS_HERE * (NOPE + VDIM)
OW = HEADS_HERE * VDIM
SLICE = FE // DP
WIDE = SETS * SLICE
SCALE = QK ** (-0.5)
PACK = QW + RANK + ROPE + ROPE + OW + ROWS
GU_PART = 144
DN_PART = 80

epsilon = 1e-06
bf16 = jnp.bfloat16
f32 = jnp.float32


def mm(left, right, dims):
    return lax.dot_general(left, right, ((dims[0], dims[1]), ((), ())), preferred_element_type=f32)


def nn(left, right):
    return mm(left, right, ((1,), (0,)))


def nt(left, right):
    return mm(left, right, ((1,), (1,)))


def tn(left, right):
    return mm(left, right, ((0,), (0,)))


def rope_tables(positions):
    half_dim = ROPE // 2
    inverse = 10000.0 ** (-jnp.arange(half_dim, dtype=f32) * 2.0 / ROPE)
    angles = positions[:, None] * inverse[None, :]
    return (jnp.cos(angles), jnp.sin(angles))


def rotate(values, cosine, sine):
    first, second = values[..., : ROPE // 2], values[..., ROPE // 2 :]
    return jnp.concatenate([first * cosine - second * sine, second * cosine + first * sine], axis=-1)


def norm_back(values, scale, gain, grad):
    scaled = gain * grad
    total = jnp.sum(scaled * values, axis=-1, keepdims=True) / values.shape[-1]
    return scale * scaled - values * (scale * scale * scale) * total


def inverse_rms(values):
    return lax.rsqrt(jnp.mean(values * values, axis=-1, keepdims=True) + epsilon)


class Seat:
    def __init__(self, axis):
        own_dp, own_sp = lax.axis_index("dp"), lax.axis_index("sp")
        self.axis = axis
        if axis == "sp":
            self.pair, self.ring, self.core, self.cores = own_sp // 4, own_sp % 4, 0, 1
            self.own, self.size = own_sp, SP
            self.device = lambda index: (own_dp, index)
        else:
            self.ring, self.pair, self.core, self.cores = own_dp // 4, (own_dp // 2) % 2, own_dp % 2, 2
            self.own, self.size = own_dp, DP
            self.device = lambda index: (index, own_sp)

    def index(self, pair, ring, core=0):
        pair, ring = (self.pair + pair) % 2, (self.ring + ring) % 4
        if self.axis == "sp":
            return pair * 4 + ring
        return (ring * 2 + pair) * 2 + (self.core + core) % 2


def send(src, dst, send_sem, recv_sem, device):
    copy = pltpu.make_async_remote_copy(
        src_ref=src,
        dst_ref=dst,
        send_sem=send_sem,
        recv_sem=recv_sem,
        device_id=device,
        device_id_type=pl.DeviceIdType.MESH,
    )
    copy.start()
    return copy


def block_of(ref, start, size):
    return ref.at[pl.ds(pl.multiple_of(start, 16), size)]


def middle(rows):
    return (rows // 2 + 15) // 16 * 16


NEAR = ((0, 1), (0, -1), (1, 0))
ORDER = ((1, 2), (1, 1), (1, -1), (0, 2), (1, 0), (0, 1), (0, -1), (0, 0))


class Gather:
    def __init__(self, axis, rows, width):
        self.axis, self.rows, self.width = axis, rows, width
        self.count = SP if axis == "sp" else DP

    def in_spec(self):
        return pl.BlockSpec(memory_space=pl.ANY)

    def out(self):
        return (
            jax.ShapeDtypeStruct((self.count * self.rows, self.width), bf16),
            pl.BlockSpec(memory_space=pl.ANY),
        )

    def scratch(self):
        return [pltpu.SemaphoreType.DMA((16,)), pltpu.SemaphoreType.DMA((16,)), pltpu.SemaphoreType.DMA]

    def partners(self, seat):
        near = [seat.index(*n) for n in NEAR]
        return near + ([seat.index(0, 0, 1)] if seat.cores == 2 else [])

    def bind(self, src, out, scratch):
        self.src, self.dst = src, out
        self.send_sem, self.recv_sem, self.local_sem = scratch
        self.seat = Seat(self.axis)
        self.copies = {}

    def view(self, place, half=None):
        start = self.seat.index(*place) * self.rows
        if half is None:
            return block_of(self.dst, start, self.rows)
        cut = middle(self.rows)
        return block_of(self.dst, start + half * cut, (cut, self.rows - cut)[half])

    def go(self, number, src, dst, to):
        self.copies[number] = send(
            src,
            dst,
            self.send_sem.at[number],
            self.recv_sem.at[number],
            self.seat.device(self.seat.index(*to)),
        )

    def share(self, number, place, src=None):
        if self.seat.cores == 2:
            self.go(8 + number, self.view(place) if src is None else src, self.view(place), (0, 0, 1))

    def arrived(self, *numbers):
        for number in numbers:
            self.copies[number].wait_recv()

    def step(self, number):
        if number == 0:
            here = self.view((0, 0))
            self.local = pltpu.make_async_copy(self.src, here, self.local_sem)
            self.local.start()
            for k, to in enumerate(NEAR):
                self.go(k, self.src, here, to)
            self.share(0, (0, 0), self.src)
        elif number == 1:
            self.arrived(0, 1)
            self.go(3, self.view((0, -1), 0), self.view((0, -1), 0), (0, 1))
            self.go(4, self.view((0, 1), 1), self.view((0, 1), 1), (0, -1))
            self.share(1, (0, -1))
            self.share(2, (0, 1))
        elif number == 2:
            self.arrived(2)
            self.go(5, self.view((1, 0)), self.view((1, 0)), (0, 1))
            self.go(6, self.view((1, 0)), self.view((1, 0)), (0, -1))
            self.share(3, (1, 0))
        elif number == 3:
            self.arrived(3, 4)
            self.go(7, self.view((0, 2)), self.view((0, 2)), (1, 0))
            self.share(4, (0, 2))
        elif number == 4:
            self.arrived(5, 6, 7)
            self.share(5, (1, -1))
            self.share(6, (1, 1))
            self.share(7, (1, 2))
        else:
            if self.seat.cores == 2:
                self.arrived(*range(8, 16))
            for copy in self.copies.values():
                copy.wait_send()
            self.local.wait()


class Scatter:
    def __init__(self, axis, rows, width, kind=f32):
        self.axis, self.rows, self.width, self.kind = axis, rows, width, kind
        self.count = SP if axis == "sp" else DP

    def in_spec(self):
        return pl.BlockSpec(memory_space=pltpu.VMEM)

    def out(self):
        return (
            jax.ShapeDtypeStruct((self.rows, self.width), self.kind),
            pl.BlockSpec(memory_space=pltpu.VMEM),
        )

    def scratch(self):
        block, cut = (self.rows, self.width), middle(self.rows)
        first, second = (cut, self.width), (self.rows - cut, self.width)
        shapes = [block, block, block, first, second, block, block, block]
        shapes = shapes + [block] * 4
        if self.axis == "dp":
            shapes = shapes + [(8,) + block]
        return [pltpu.SemaphoreType.DMA((16,)), pltpu.SemaphoreType.DMA((16,))] + [
            pltpu.VMEM(shape, bf16) for shape in shapes
        ]

    partners = Gather.partners
    go = Gather.go
    arrived = Gather.arrived

    def bind(self, src, out, scratch):
        self.src, self.dst = src, out
        self.send_sem, self.recv_sem = scratch[:2]
        self.got, self.made = scratch[2:10], scratch[10:14]
        self.shared = scratch[14] if self.axis == "dp" else None
        self.seat = Seat(self.axis)
        self.copies = {}

    def part(self, place):
        if self.shared is None:
            return block_of(self.src, self.seat.index(*place) * self.rows, self.rows)
        return self.shared.at[ORDER.index(place)]

    def ready(self, place):
        if self.shared is not None:
            k = ORDER.index(place)
            self.arrived(8 + k)
            self.add(
                self.shared.at[k],
                [self.shared.at[k], block_of(self.src, self.seat.index(*place) * self.rows, self.rows)],
            )

    def add(self, dst, terms):
        rows = dst.shape[0]
        step = 16

        @pl.loop(0, rows // step)
        def _(i):
            at = pl.ds(pl.multiple_of(i * step, step), step)
            total = terms[0][at, :].astype(f32)
            for term in terms[1:]:
                total = total + term[at, :].astype(f32)
            dst[at, :] = total.astype(dst.dtype)

    def halves(self, ref):
        cut = middle(self.rows)
        return ref.at[pl.ds(0, cut)], ref.at[pl.ds(cut, self.rows - cut)]

    def step(self, number):
        if number == 0:
            if self.shared is not None:
                for k, place in enumerate(ORDER):
                    src = block_of(self.src, self.seat.index(*place, 1) * self.rows, self.rows)
                    self.go(8 + k, src, self.shared.at[k], (0, 0, 1))
            self.ready((1, 2))
            self.go(0, self.part((1, 2)), self.got[0], (1, 0))
            self.ready((1, 1))
            self.go(1, self.part((1, 1)), self.got[1], (0, 1))
            self.ready((1, -1))
            self.go(2, self.part((1, -1)), self.got[2], (0, -1))
            for place in ORDER[3:]:
                self.ready(place)
        elif number == 1:
            self.arrived(0)
            self.add(self.made[0], [self.part((0, 2)), self.got[0]])
            first, second = self.halves(self.made[0])
            self.go(3, first, self.got[3], (0, 1))
            self.go(4, second, self.got[4], (0, -1))
        elif number == 2:
            self.arrived(1, 2)
            self.add(self.made[1], [self.part((1, 0)), self.got[1], self.got[2]])
            self.go(5, self.made[1], self.got[5], (1, 0))
        elif number == 3:
            self.arrived(3, 4)
            for k, place, half in ((2, (0, 1), 0), (3, (0, -1), 1)):
                made, part = self.halves(self.made[k]), self.halves(self.part(place))
                self.add(made[half], [part[half], self.got[3 + half]])
                self.add(made[1 - half], [part[1 - half]])
                self.go(6 + half, self.made[k], self.got[6 + half], (0, 1 - 2 * half))
        elif number == 4:
            self.arrived(5, 6, 7)
            self.add(self.dst, [self.part((0, 0)), self.got[5], self.got[6], self.got[7]])
        else:
            for copy in self.copies.values():
                copy.wait_send()


class Swap:
    def __init__(self, axis, shape, take, put, kind="any"):
        self.axis, self.shape, self.take, self.put = axis, shape, take, put
        self.count = SP if axis == "sp" else DP

    def in_spec(self):
        return pl.BlockSpec(memory_space=pl.ANY)

    def out(self):
        return jax.ShapeDtypeStruct(self.shape, bf16), pl.BlockSpec(memory_space=pl.ANY)

    def scratch(self):
        sems = pltpu.SemaphoreType.DMA((self.count,))
        return [sems, sems, pltpu.SemaphoreType.DMA]

    def partners(self, seat):
        return [(seat.own + k) % seat.size for k in range(1, seat.size)]

    def bind(self, src, out, scratch):
        self.src, self.dst = src, out
        self.send_sem, self.recv_sem, self.local_sem = scratch
        self.seat = Seat(self.axis)

    def step(self, number):
        seat = self.seat
        if number == 0:
            here = self.put(self.dst, seat.own)
            self.local = pltpu.make_async_copy(self.take(self.src, seat.own), here, self.local_sem)
            self.local.start()
            self.copies = []
            for k in range(1, seat.size):
                to = (seat.own + k) % seat.size
                self.copies.append(
                    send(
                        self.take(self.src, to),
                        here,
                        self.send_sem.at[k],
                        self.recv_sem.at[k],
                        seat.device(to),
                    )
                )
        elif number == 5:
            for copy in self.copies:
                copy.wait_recv()
            for copy in self.copies:
                copy.wait_send()
            self.local.wait()


def exchange(name, number, ops, arrays, plan=None, chained=()):
    chained = dict(chained)
    plan = plan or [(op, step) for step in range(6) for op in range(len(ops))]
    counts = [len(op.scratch()) for op in ops]
    inputs = [k for k in range(len(ops)) if k not in chained]

    def body(*refs):
        given = dict(zip(inputs, refs[: len(inputs)]))
        outs = refs[len(inputs) : len(inputs) + len(ops)]
        rest = refs[len(inputs) + len(ops) :]
        for k, op in enumerate(ops):
            op.bind(given[k] if k in given else outs[chained[k]], outs[k], rest[: counts[k]])
            rest = rest[counts[k] :]
        barrier = pltpu.get_barrier_semaphore()
        total = 0
        for axis in ("sp", "dp"):
            mine = [op for op in ops if op.axis == axis]
            if not mine:
                continue
            seat = Seat(axis)
            widest = max(mine, key=lambda op: len(op.partners(seat)))
            for partner in widest.partners(seat):
                pl.semaphore_signal(
                    barrier,
                    inc=1,
                    device_id=seat.device(partner),
                    device_id_type=pl.DeviceIdType.MESH,
                )
                total += 1
        pl.semaphore_wait(barrier, total)
        for op, step in plan:
            ops[op].step(step)

    outs = [op.out() for op in ops]
    return pl.pallas_call(
        body,
        name=name,
        out_shape=[shape for shape, _ in outs],
        in_specs=[ops[k].in_spec() for k in inputs],
        out_specs=[spec for _, spec in outs],
        scratch_shapes=[entry for op in ops for entry in op.scratch()],
        compiler_params=pltpu.CompilerParams(
            collective_id=number, has_side_effects=True, vmem_limit_bytes=56 * 2**20
        ),
    )(*arrays)


def per_device(
    tokens,
    cotangent,
    chosen,
    attn_gain,
    w_query,
    w_kv_down,
    kv_gain,
    w_kv_up,
    w_out,
    ffn_gain,
    w_router,
    shared_gate,
    shared_up,
    shared_down,
    expert_gate,
    expert_up,
    expert_down,
):
    own_sp = lax.axis_index("sp")
    picks = jnp.any(chosen[:, :, None] == jnp.arange(EXPERTS, dtype=jnp.int32), axis=1).astype(bf16)
    pack = jnp.concatenate(
        [
            lax.dynamic_slice_in_dim(w_query, own_sp * QW, QW, 1),
            w_kv_down,
            attn_gain[:, None],
            ffn_gain[:, None],
            jnp.pad(kv_gain, (0, ROWS - kv_gain.shape[0]))[:, None],
            w_router,
            picks,
            jnp.zeros((ROWS, ROPE - 11), bf16),
            lax.dynamic_slice_in_dim(w_out, own_sp * OW, OW, 1),
            lax.dynamic_slice_in_dim(w_kv_up, own_sp * KVW, KVW, 1).reshape(ROWS, ROWS),
        ],
        axis=1,
    )
    at = QW + RANK + ROPE
    out_at = at + ROPE
    tok_all, pack, cot_all, out_w = exchange(
        "gather_tokens_weights",
        0,
        [
            Gather("sp", ROWS, D),
            Gather("dp", ROWS, PACK),
            Gather("dp", ROWS, D),
            Swap(
                "sp",
                (OW, D),
                lambda ref, j: ref.at[pl.ds(pl.multiple_of(j * OW, OW), OW), pl.ds(out_at, OW)],
                lambda ref, j: ref.at[:, pl.ds(pl.multiple_of(j * OW, OW), OW)],
            ),
        ],
        [tokens, pack, cotangent],
        plan=[(0, 0), (1, 0), (0, 1), (1, 1), (0, 2), (1, 2), (0, 3), (1, 3), (1, 4), (1, 5)]
        + [(2, 0), (3, 0), (0, 4), (2, 1), (0, 5), (2, 2), (2, 3), (3, 5), (2, 4), (2, 5)],
        chained=[(3, 1)],
    )
    qc_w = pack[:, :at]
    up_w = pack[:, out_at + OW :].reshape(RANK, KVW)
    gain_one = pack[:, at].astype(f32)
    gain_two = pack[:, at + 1].astype(f32)
    latent_gain = pack[:, at + 2].reshape(DP, ROWS)[:, : RANK // DP].reshape(RANK).astype(f32)
    router_w = pack[:, at + 3 : at + 7]
    picks_all = pack[:, at + 7 : at + 11].astype(f32)
    gate_up = jnp.stack(
        [
            jnp.concatenate([shared_gate, expert_gate], axis=1),
            jnp.concatenate([shared_up, expert_up], axis=1),
        ]
    )
    gate_up = gate_up.reshape(2, ROWS, SETS, DP, SLICE).transpose(3, 0, 2, 4, 1)
    gate_up = gate_up.reshape(DP, 2 * WIDE, ROWS)
    down = jnp.concatenate([shared_down, expert_down], axis=1).transpose(1, 0, 2).reshape(WIDE, D)

    cosine, sine = rope_tables(jnp.arange(SEQ, dtype=f32))
    resid_all = tok_all.astype(f32)
    scale_one = inverse_rms(resid_all)
    hidden_one = (resid_all * scale_one * gain_one).astype(bf16)
    qc = nn(hidden_one, qc_w)
    compressed = qc[:, QW : QW + RANK]
    scale_latent = inverse_rms(compressed)
    latent = (compressed * scale_latent * latent_gain).astype(bf16)
    key_rope = rotate(qc[:, QW + RANK :], cosine, sine).astype(bf16)
    expanded = nn(latent, up_w).astype(bf16)
    rows = jnp.arange(SEQ, dtype=jnp.int32)
    allowed = rows[None, :] <= rows[:, None]
    queries, keys, values, probs, heads = [], [], [], [], []
    for h in range(HEADS_HERE):
        raw = qc[:, h * QK : (h + 1) * QK]
        query = jnp.concatenate([raw[:, :NOPE], rotate(raw[:, NOPE:], cosine, sine)], axis=1).astype(bf16)
        base = h * (NOPE + VDIM)
        key = jnp.concatenate([expanded[:, base : base + NOPE], key_rope], axis=1)
        value = expanded[:, base + NOPE : base + NOPE + VDIM]
        scores = jnp.where(allowed, nt(query, key) * SCALE, -1e9)
        weights = jnp.exp(scores - jnp.max(scores, axis=-1, keepdims=True))
        prob = weights / jnp.sum(weights, axis=-1, keepdims=True)
        queries.append(query)
        keys.append(key)
        values.append(value)
        probs.append(prob)
        heads.append(nn(prob.astype(bf16), value).astype(bf16))
    head_out = jnp.concatenate(heads, axis=1)
    attn_proj, gate_up = exchange(
        "sum_projection",
        1,
        [
            Scatter("sp", ROWS, D),
            Swap(
                "dp",
                (2 * WIDE, D),
                lambda ref, j: ref.at[j],
                lambda ref, j: ref.at[:, pl.ds(pl.multiple_of(j * ROWS, ROWS), ROWS)],
            ),
        ],
        [nn(head_out, out_w).astype(bf16), gate_up],
    )
    resid_two = tokens.astype(f32) + attn_proj
    scale_two = inverse_rms(resid_two)
    hidden_two = (resid_two * scale_two * gain_two).astype(bf16)

    (hidden_all,) = exchange("gather_hidden", 2, [Gather("dp", ROWS, D)], [hidden_two])
    router_all = jax.nn.softmax(nn(hidden_all, router_w), axis=-1)
    gate_dense = router_all * picks_all
    column_set = jnp.arange(WIDE, dtype=jnp.int32) // SLICE

    def spread(per_expert, shared):
        out = jnp.full((GROUP, WIDE), shared, f32)
        for e in range(EXPERTS):
            out = jnp.where(column_set[None, :] == NS + e, per_expert[:, e : e + 1], out)
        return out

    gates = spread(gate_dense, 1.0)
    gate = nt(hidden_all, gate_up[:WIDE])
    up = nt(hidden_all, gate_up[WIDE:])
    sig = jax.nn.sigmoid(gate)
    silu = gate * sig
    act = silu * up
    act_gated = (act.astype(bf16).astype(f32) * gates).astype(bf16)
    mixed_part = nn(act_gated, down).astype(bf16)
    act_grad_raw = nt(cot_all, down)
    reached = act * act_grad_raw
    prob_grad = jnp.stack(
        [
            jnp.sum(jnp.where(column_set[None, :] == NS + e, reached, 0.0), axis=1)
            for e in range(EXPERTS)
        ],
        axis=1,
    )
    act_grad = act_grad_raw * gates
    gate_grad = (act_grad * up * sig * (1.0 + gate * (1.0 - sig))).astype(bf16)
    up_grad = (act_grad * silu).astype(bf16)
    hidden_grad_part = (nn(gate_grad, gate_up[:WIDE]) + nn(up_grad, gate_up[WIDE:])).astype(bf16)
    hidden_grad_part = jnp.concatenate(
        [hidden_grad_part, prob_grad.astype(bf16), jnp.zeros((GROUP, ROWS - EXPERTS), bf16)], axis=1
    )
    (hidden_grad,) = exchange(
        "sum_hidden_grad", 3, [Scatter("dp", ROWS, D + ROWS)], [hidden_grad_part]
    )
    prob_grad = hidden_grad[:, D : D + EXPERTS]
    hidden_grad = hidden_grad[:, :D]

    def parts(grad, size):
        return jnp.pad(grad, ((0, SP * size - grad.shape[0]), (0, 0))).reshape(SP, size, D)

    gate_up_grad = jnp.concatenate([tn(gate_grad, hidden_all), tn(up_grad, hidden_all)]).astype(bf16)
    down_grad = tn(act_gated, cot_all).astype(bf16)
    ffn_grad = jnp.concatenate([parts(gate_up_grad, GU_PART), parts(down_grad, DN_PART)], axis=1)
    ffn_grad = ffn_grad.reshape(SP * (GU_PART + DN_PART), D)

    logits = nn(hidden_two, router_w)
    router = jax.nn.softmax(logits, axis=-1)
    prob_grad = prob_grad * picks.astype(f32)
    logit_grad = (
        router * (prob_grad - jnp.sum(router * prob_grad, axis=-1, keepdims=True))
    ).astype(bf16)
    hidden_grad = hidden_grad + nt(logit_grad, router_w)
    router_grad = tn(hidden_two, logit_grad)
    gain_two_grad = jnp.sum(hidden_grad * resid_two * scale_two, axis=0)
    upstream = cotangent.astype(f32)
    resid_two_grad = upstream + norm_back(resid_two, scale_two, gain_two, hidden_grad)
    proj_grad = resid_two_grad.astype(bf16)

    proj_grad_all, mixed = exchange(
        "gather_projection_grad",
        4,
        [Gather("sp", ROWS, D), Scatter("dp", ROWS, D)],
        [proj_grad, mixed_part],
    )
    mixed = (resid_two + mixed).astype(bf16)
    out_w_grad = tn(head_out, proj_grad_all)
    head_grad = nt(proj_grad_all, out_w).astype(bf16)
    query_grads, expanded_grads, rope_grad = [], [], 0.0
    for h in range(HEADS_HERE):
        piece = head_grad[:, h * VDIM : (h + 1) * VDIM]
        prob = probs[h]
        dprob = nt(piece, values[h])
        delta = jnp.sum(prob * dprob, axis=-1, keepdims=True)
        score_grad = (prob * (dprob - delta) * SCALE).astype(bf16)
        query_grad = nn(score_grad, keys[h]).astype(bf16).astype(f32)
        key_grad = tn(score_grad, queries[h]).astype(bf16)
        value_grad = tn(prob.astype(bf16), piece).astype(bf16)
        query_grads.append(query_grad[:, :NOPE].astype(bf16))
        query_grads.append(rotate(query_grad[:, NOPE:], cosine, -sine).astype(bf16))
        expanded_grads.append(key_grad[:, :NOPE])
        expanded_grads.append(value_grad)
        rope_grad = rope_grad + key_grad[:, NOPE:].astype(f32)
    query_pre_grad = jnp.concatenate(query_grads, axis=1)
    expanded_grad = jnp.concatenate(expanded_grads, axis=1)
    up_w_grad = tn(latent, expanded_grad)
    latent_grad = nt(expanded_grad, up_w)
    latent_in_grad = norm_back(compressed, scale_latent, latent_gain, latent_grad)
    latent_gain_grad = jnp.sum(latent_grad * compressed * scale_latent, axis=0)
    compressed_grad = jnp.concatenate(
        [latent_in_grad, rotate(rope_grad, cosine, -sine)], axis=1
    ).astype(bf16)
    qc_grad = jnp.concatenate([query_pre_grad, compressed_grad], axis=1)
    qc_w_grad = tn(hidden_one, qc_grad)
    hidden_one_grad = nt(qc_grad, qc_w)
    gain_one_grad = jnp.sum(hidden_one_grad * resid_all * scale_one, axis=0)
    (out_cols_grad,) = exchange(
        "swap_projection_weight_grad",
        5,
        [
            Swap(
                "sp",
                (D, OW),
                lambda ref, j: ref.at[:, pl.ds(pl.multiple_of(j * OW, OW), OW)],
                lambda ref, j: ref.at[pl.ds(pl.multiple_of(j * OW, OW), OW)],
            )
        ],
        [out_w_grad.astype(bf16)],
    )
    latent_gain_grad = jnp.pad(
        latent_gain_grad.reshape(DP, RANK // DP), ((0, 0), (0, ROWS - RANK // DP))
    ).reshape(D)
    grads = jnp.concatenate(
        [
            qc_w_grad.astype(bf16),
            gain_one_grad.astype(bf16)[:, None],
            gain_two_grad.astype(bf16)[:, None],
            latent_gain_grad.astype(bf16)[:, None],
            router_grad.astype(bf16),
            jnp.zeros((D, ROPE - 7), bf16),
            out_cols_grad,
            up_w_grad.astype(bf16).reshape(D, ROWS),
        ],
        axis=1,
    )
    grads, ffn_grad, hidden_one_grad = exchange(
        "sum_grads",
        6,
        [
            Scatter("dp", ROWS, PACK, bf16),
            Scatter("sp", GU_PART + DN_PART, D, bf16),
            Scatter("sp", ROWS, D),
        ],
        [grads, ffn_grad, hidden_one_grad.astype(bf16)],
    )
    grads, dn_total, gu_piece = exchange(
        "gather_grads",
        7,
        [
            Gather("sp", ROWS, PACK),
            Gather("sp", DN_PART, D),
            Swap(
                "dp",
                (DP, GU_PART, ROWS),
                lambda ref, j: ref.at[:, pl.ds(pl.multiple_of(j * ROWS, ROWS), ROWS)],
                lambda ref, j: ref.at[j],
            ),
        ],
        [grads, ffn_grad[GU_PART:], ffn_grad[:GU_PART]],
    )
    (gu_total,) = exchange(
        "gather_expert_grads",
        8,
        [Gather("sp", DP * GU_PART, ROWS)],
        [gu_piece.reshape(DP * GU_PART, ROWS)],
    )
    gu_total = gu_total.reshape(SP, DP, GU_PART, ROWS)
    grads = grads.reshape(SP, ROWS, PACK)
    resid_one = tokens.astype(f32)
    own_scale = inverse_rms(resid_one)
    tokens_grad = resid_two_grad + norm_back(resid_one, own_scale, gain_one, hidden_one_grad)
    tokens_grad = tokens_grad.astype(bf16)

    def side_by_side(block, width):
        return block.astype(f32).transpose(1, 0, 2).reshape(-1, SP * width)

    query_total = side_by_side(grads[:, :, :QW], QW)
    tail = jnp.sum(grads[:, :, QW:out_at].astype(f32), axis=0)
    down_total, tail = tail[:, : RANK + ROPE], tail[:, RANK + ROPE :]
    out_total = side_by_side(grads[:, :, out_at : out_at + OW], OW)
    up_total = side_by_side(grads[:, :, out_at + OW :].reshape(SP, RANK // DP, KVW), KVW)

    gu_total = gu_total.transpose(0, 2, 1, 3).reshape(SP * GU_PART, DP, ROWS)[: 2 * WIDE]
    gu_total = gu_total.reshape(2, SETS, SLICE, DP, ROWS).transpose(0, 4, 1, 3, 2)
    gu_total = gu_total.reshape(2, ROWS, SETS, FE).astype(f32)
    dn_total = dn_total[:WIDE].reshape(SETS, SLICE, D).transpose(1, 0, 2).astype(f32)
    return (
        mixed,
        tokens_grad,
        tail[:, 0],
        query_total,
        down_total,
        tail[: RANK // DP, 2],
        up_total,
        out_total,
        tail[:, 1],
        tail[:, 3:7],
        gu_total[0, :, :NS],
        gu_total[1, :, :NS],
        dn_total[:, :NS],
        gu_total[0, :, NS:],
        gu_total[1, :, NS:],
        dn_total[:, NS:],
    )


def solution(mesh):
    rows = P(("dp", "sp"), None)
    vec, mat, cube = P("dp"), P("dp", None), P("dp", None, None)
    return jax.shard_map(
        per_device,
        mesh=mesh,
        in_specs=(rows, rows, rows, vec, mat, mat, vec, mat, mat, vec, mat) + (cube,) * 6,
        out_specs=(rows, rows, vec, mat, mat, vec, mat, mat, vec, mat) + (cube,) * 6,
        check_vma=False,
    )
```

time: 2830 us -> 839 us (0.30)
  waiting for transfers between devices: 1880 us -> 0 us
  Pallas kernels: 0 us -> 501 us
  blocking collectives: 176 us -> 0 us
  matrix products: 294 us -> 142 us
  local copies, waits for them, and re-layouts: 252 us -> 129 us
  other arithmetic: 144 us -> 51.9 us
  starting transfers between devices: 44.7 us -> 0 us
    unnamed x22 -> x0, waiting for transfers between devices: 857 us -> none
    all_gather x10 -> x0, waiting for transfers between devices: 542 us -> none  [the longest x1 115 us: per_device(): up_r_piece = lax.all_gather(expert_up, 'dp', axis=0, tiled=True)]
    pallas_call x0 -> x9, Pallas kernels: none -> 501 us  [exchange(): pl.pallas_call(body, name=name, out_shape=[shape for shape, _ in outs], i...]
    reduce_scatter x3 -> x0, waiting for transfers between devices: 304 us -> none  [the longest x1 141 us: per_device(): lax.psum_scatter(query_w_grad.astype(jnp.bfloat16), 'dp', scatter_dimensi...]
    dot_general x51 -> x34, matrix products: 294 us -> 142 us  [mm(): lax.dot_general(left, right, ((dims[0], dims[1]), ((), ())), preferred_el...]
    psum x1 -> x0, waiting for transfers between devices: 132 us -> none  [per_device(): lax.psum(ffn_in_share, 'sp').astype(jnp.float32)]
    concatenate x6, other arithmetic: 121 us -> 13.9 us  [the longest x1 7.56 us: per_device(): jnp.concatenate([parts(gate_up_grad, GU_PART), parts(down_grad, DN_PART)]...]
    unnamed x212 -> x210, local copies, waits for them, and re-layouts: 134 us -> 43.2 us
  transfers between devices with their start and end apart: 25 -> 0, of which waited for: 19 -> 0; matrix products, arithmetic and copies ran while one was open for 18% -> 0% of each run, Pallas kernels for 0% -> 0%
where the time goes in v1:
time: 839 us; the launch traced here: 826 us
  Pallas kernels  501 us (60%)
  matrix products  142 us (17%)
  local copies, waits for them, and re-layouts  129 us (15%)
  other arithmetic  51.9 us (6%)
    pallas_call x9, Pallas kernels, exchange(): pl.pallas_call(body, name=name, out_shape=[shape for shape, _ in outs], i...  501 us
    dot_general x34, matrix products, mm(): lax.dot_general(left, right, ((dims[0], dims[1]), ((), ())), preferred_el...  142 us
    unnamed x210, local copies, waits for them, and re-layouts  43.2 us

profile of v1, /device:TPU:1, one launch (start us, length us, event | category | flops | bytes accessed | tf_op | source)
XLA Modules:
  0.0 826.2 jit_solution(18044907285316169660)
XLA Ops:
  10.0 91.8 %gather_tokens_weights.1 = (bf16[1024,2048]{1,0:T(8,128)(2,1)}, bf16[2048,1408]{1,0:T(8,128)(2,1)}, bf16[2048,2048]{1,0:T(8,128)(2,1)}, bf16[256,2048]{1,0:T(8,128)(2,1)}) custom-call(bf16[128,2048]{1,0:T(8,128)(2,1)} %refs_0_.1, bf16[128,1408]{1,0:T(8,128)(2,1)} %concatenate.61.refs_1_, bf16[128,2048]{1,0:T(8,128)(2,1)} %refs_2_.1), custom_call_target="tpu_custom_call" | custom-call | tf_op jit(solution)/shard_map/gather_tokens_weights/pallas_call | solution.py:402
  107.0 6.6 fusion.92
  139.3 3.8 copy.211
  150.2 79.9 %sum_projection.1 = (f32[128,2048]{1,0:T(8,128)}, bf16[1056,2048]{1,0:T(8,128)(2,1)}) custom-call(bf16[1024,2048]{1,0:T(8,128)(2,1)} %convolution_convert_fusion.1.refs_0_, bf16[16,1056,128]{2,1,0:T(8,128)(2,1)} %bitcast.102), custom_call_target="tpu_custom_call" | custom-call | tf_op jit(solution)/shard_map/sum_projection/pallas_call | solution.py:402
  232.6 37.8 %gather_hidden.1 = bf16[2048,2048]{1,0:T(8,128)(2,1)} custom-call(bf16[128,2048]{1,0:T(8,128)(2,1)} %multiply_convert_fusion.6.refs_0_), custom_call_target="tpu_custom_call" | custom-call | tf_op jit(solution)/shard_map/gather_hidden/pallas_call | solution.py:402
  270.3 5.8 fusion.93
  281.4 11.1 %fusion.22 = f32[2048,528]{0,1:T(8,128)} fusion(bf16[2048,2048]{1,0:T(8,128)(2,1)} %gather_hidden.1, bf16[1056,2048]{1,0:T(8,128)(2,1)} %get-tuple-element.35), kind=kOutput, calls=%fused_computation.70 | convolution fusion | flops 4429185024 | bytes 14876672 | tf_op jit(solution)/shard_map/dot_general | solution.py:44
  292.6 6.5 fusion.25
  300.3 14.7 %multiply_multiply_fusion = (f32[2048,528]{0,1:T(8,128)}, bf16[2048,528]{0,1:T(8,128)(2,1)S(1)}, bf16[2048,528]{0,1:T(8,128)(2,1)}, bf16[2048,528]{0,1:T(8,128)(2,1)S(1)}) fusion(f32[2048,528]{0,1:T(8,128)} %fusion.25, f32[2048,528]{0,1:T(8,128)} %fusion.22, f32[2048]{0:T(1024)S(1)} %get-tuple-element.135, pred[528]{0:T(1024)(128)(4,1)S(1)} %get-tuple-element.196, ...), kind=kOutput, calls=%fused_computation.67 | convolution fusion | flops 4455137280 | bytes 30050368 | tf_op jit(solution)/shard_map/dot_general | solution.py:44
  315.1 4.9 convolution_convert_fusion.4
  320.0 4.9 convolution_convert_fusion.5
  327.4 4.9 convolution_convert_fusion.3
  334.1 7.6 pad_maximum_fusion
  343.7 12.8 %fusion.20 = f32[2048,2048]{1,0:T(8,128)} fusion(bf16[2048,528]{0,1:T(8,128)(2,1)} %copy-done.82, bf16[1056,2048]{1,0:T(8,128)(2,1)} %get-tuple-element.35), kind=kOutput, calls=%fused_computation.68 | convolution fusion | flops 4429185024 | bytes 21102592 | tf_op jit(solution)/shard_map/dot_general | solution.py:44
  356.4 13.1 %add_convert_fusion = bf16[2048,2048]{1,0:T(8,128)(2,1)} fusion(f32[2048,2048]{1,0:T(8,128)} %fusion.20, bf16[2048,528]{0,1:T(8,128)(2,1)S(1)} %copy-done.84, bf16[1056,2048]{1,0:T(8,128)(2,1)} %get-tuple-element.35), kind=kOutput, calls=%fused_computation | convolution fusion | flops 4437573632 | bytes 29491200 | tf_op jit(solution)/shard_map/dot_general | solution.py:44
  374.7 14.5 %concatenate.70.refs_0_ = bf16[2048,2176]{1,0:T(8,128)(2,1)} concatenate(bf16[2048,2048]{1,0:T(8,128)(2,1)} %add_convert_fusion, bf16[2048,1]{1,0:T(8,128)(2,1)S(1)} %stack.34, bf16[2048,1]{1,0:T(8,128)(2,1)S(1)} %stack.35, bf16[2048,1]{1,0:T(8,128)(2,1)S(1)} %stack.36, bf16[2048,1]{1,0:T(8,128)(2,1)} %stack.37, bf16[2048,124]{1,0:T(8,128)(2,1)} %broadcast_in_dim.166), dimensions={1} | concatenate | bytes 17825792 | tf_op jit(solution)/shard_map/concatenate | solution.py:567
  389.2 43.1 %sum_hidden_grad.1 = f32[128,2176]{1,0:T(8,128)} custom-call(bf16[2048,2176]{1,0:T(8,128)(2,1)} %concatenate.70.refs_0_), custom_call_target="tpu_custom_call" | custom-call | tf_op jit(solution)/shard_map/sum_hidden_grad/pallas_call | solution.py:402
  438.4 9.1 %convolution_convert_fusion.refs_1_ = bf16[2048,2048]{1,0:T(8,128)(2,1)} fusion(bf16[2048,528]{0,1:T(8,128)(2,1)S(1)} %copy-done.86, bf16[528,2048]{1,0:T(8,128)(2,1)S(1)} %bitcast.115), kind=kOutput, calls=%fused_computation.13 | convolution fusion | flops 4433379328 | bytes 12713984 | tf_op jit(solution)/shard_map/dot_general | solution.py:44
  447.4 53.1 %gather_projection_grad.1 = (bf16[1024,2048]{1,0:T(8,128)(2,1)}, f32[128,2048]{1,0:T(8,128)}) custom-call(bf16[128,2048]{1,0:T(8,128)(2,1)} %get-tuple-element.142.refs_0_, bf16[2048,2048]{1,0:T(8,128)(2,1)} %convolution_convert_fusion.refs_1_), custom_call_target="tpu_custom_call" | custom-call | tf_op jit(solution)/shard_map/gather_projection_grad/pallas_call | solution.py:402
  500.6 3.6 convolution_convert_fusion.10
  517.1 4.6 convolution_convert_fusion.6.refs_0_
  521.7 18.0 %swap_projection_weight_grad.1 = bf16[2048,256]{1,0:T(8,128)(2,1)} custom-call(bf16[256,2048]{1,0:T(8,128)(2,1)} %convolution_convert_fusion.6.refs_0_), custom_call_target="tpu_custom_call" | custom-call | tf_op jit(solution)/shard_map/swap_projection_weight_grad/pallas_call | solution.py:402
  549.9 9.5 %fusion.89 = (bf16[1024,2048]{1,0:T(8,128)(2,1)}, bf16[2048]{0:T(1024)(128)(2,1)S(1)}) fusion(f32[1024]{0:T(1024)S(1)} %copy-done.79, bf16[1024,2048]{1,0:T(8,128)(2,1)S(1)} %copy-done.20, bf16[1024,960]{0,1:T(8,128)(2,1)S(1)} %fusion.67, bf16[2048,1408]{1,0:T(8,128)(2,1)} %get-tuple-element.31), kind=kOutput, calls=%fused_computation.225 | convolution fusion | flops 4037015552 | bytes 14557184 | tf_op jit(solution)/shard_map/dot_general | solution.py:44
  560.6 6.0 convolution_convert_fusion.2
  566.6 6.4 copy.225
  576.2 10.7 %concatenate.73.refs_0_ = bf16[2048,1408]{1,0:T(8,128)(2,1)} concatenate(bf16[2048,960]{1,0:T(8,128)(2,1)} %copy.225, bf16[2048,1]{1,0:T(8,128)(2,1)} %convert_element_type.326, bf16[2048,1]{1,0:T(8,128)(2,1)} %convert_element_type.327, bf16[2048,1]{1,0:T(8,128)(2,1)} %bitcast.116, bf16[2048,4]{1,0:T(8,128)(2,1)S(1)} %copy.229, bf16[2048,57]{1,0:T(8,128)(2,1)} %broadcast_in_dim.167, ...), dimensions={1} | concatenate | bytes 11534336 | tf_op jit(solution)/shard_map/concatenate | solution.py:650
  586.9 96.7 %sum_grads.1 = (bf16[128,1408]{1,0:T(8,128)(2,1)}, bf16[224,2048]{1,0:T(8,128)(2,1)}, f32[128,2048]{1,0:T(8,128)}) custom-call(bf16[2048,1408]{1,0:T(8,128)(2,1)} %concatenate.73.refs_0_, bf16[1792,2048]{1,0:T(8,128)(2,1)} %bitcast.95, bf16[1024,2048]{1,0:T(8,128)(2,1)} %get-tuple-element.154.refs_2_), custom_call_target="tpu_custom_call" | custom-call | tf_op jit(solution)/shard_map/sum_grads/pallas_call | solution.py:402
  687.2 44.3 %gather_grads.1 = (bf16[1024,1408]{1,0:T(8,128)(2,1)}, bf16[640,2048]{1,0:T(8,128)(2,1)}, bf16[16,144,128]{2,1,0:T(8,128)(2,1)}) custom-call(bf16[128,1408]{1,0:T(8,128)(2,1)} %get-tuple-element.39.refs_0_, bf16[80,2048]{1,0:T(8,128)(2,1)} %slice.261.refs_1_, bf16[144,2048]{1,0:T(8,128)(2,1)} %slice.262.refs_2_), custom_call_target="tpu_custom_call" | custom-call | tf_op jit(solution)/shard_map/gather_grads/pallas_call | solution.py:402
  731.6 36.5 %gather_expert_grads.1 = bf16[18432,128]{1,0:T(8,128)(2,1)} custom-call(bf16[2304,128]{1,0:T(8,128)(2,1)} %bitcast.120), custom_call_target="tpu_custom_call" | custom-call | tf_op jit(solution)/shard_map/gather_expert_grads/pallas_call | solution.py:402
  768.0 3.6 copy.233
  781.0 4.7 copy.240
  785.6 4.7 copy.241
  (332 shorter events, 148.3 us)
Async XLA Ops:
  103.9 9.8 %copy-start.52 = (f32[2048]{0:T(1024)}, f32[2048]{0:T(1024)S(1)}, u32[]{:S(2)}) copy-start(f32[2048]{0:T(1024)S(1)} %get-tuple-element.127) | copy-start | bytes 24580
  107.0 6.7 copy-start.78
  116.4 5.6 copy-start.73
  118.0 6.6 copy-start.75
  119.4 6.1 copy-start.40
  122.0 6.9 copy-start.46
  130.9 5.8 copy-start.34
  150.2 79.9 %copy-start.12 = (bf16[128,2048]{1,0:T(8,128)(2,1)S(1)}, bf16[128,2048]{1,0:T(8,128)(2,1)}, u32[]{:S(2)}) copy-start(bf16[128,2048]{1,0:T(8,128)(2,1)} %refs_0_.1) | copy-start | bytes 1572868
  279.4 13.1 %slice-start = ((s8[8388608]{0:T(1024)(128)(4,1)}), s8[4194304]{0:T(1024)(128)(4,1)S(1)}, s32[]{:S(2)}) async-start(s8[8388608]{0:T(1024)(128)(4,1)} %bitcast.91), calls=%async_computation | async-start | bytes 8388608
  279.4 13.1 %slice-start.6 = ((s8[4325376]{0:T(1024)(128)(4,1)}), s8[4194304]{0:T(1024)(128)(4,1)S(1)}, s32[]{:S(2)}) async-start(s8[4325376]{0:T(1024)(128)(4,1)} %bitcast.128), calls=%async_computation.6 | async-start | bytes 8388608
  281.4 11.1 %slice-start.1 = ((s8[8388608]{0:T(1024)(128)(4,1)}), s8[4194304]{0:T(1024)(128)(4,1)S(1)}, s32[]{:S(2)}) async-start(s8[8388608]{0:T(1024)(128)(4,1)} %bitcast.91), calls=%async_computation.1 | async-start | bytes 8388608
  281.4 11.1 %slice-start.7 = ((s8[4325376]{0:T(1024)(128)(4,1)}), s8[131072]{0:T(1024)(128)(4,1)S(1)}, s32[]{:S(2)}) async-start(s8[4325376]{0:T(1024)(128)(4,1)} %bitcast.128), calls=%async_computation.7 | async-start | bytes 262144
  292.6 6.5 copy-start.26
  292.6 7.3 copy-start.35
  300.3 14.7 %copy-start.22 = (bf16[88,6,2048]{2,0,1:T(8,128)(2,1)}, bf16[88,6,2048]{2,0,1:T(8,128)(2,1)S(1)}, u32[]{:S(2)}) copy-start(bf16[88,6,2048]{2,0,1:T(8,128)(2,1)S(1)} %pad_maximum_fusion.3) | copy-start | bytes 6488068
  315.1 12.3 %slice-start.4 = ((s8[8388608]{0:T(1024)(128)(4,1)}), s8[4194304]{0:T(1024)(128)(4,1)S(1)}, s32[]{:S(2)}) async-start(s8[8388608]{0:T(1024)(128)(4,1)} %bitcast.126), calls=%async_computation.4 | async-start | bytes 8388608
  320.0 7.4 slice-start.5
  334.1 7.6 copy-start.7
  343.6 12.8 %copy-start.84 = (bf16[2048,528]{0,1:T(8,128)(2,1)S(1)}, bf16[2048,528]{0,1:T(8,128)(2,1)}, u32[]{:S(2)}) copy-start(bf16[2048,528]{0,1:T(8,128)(2,1)} %copy-done.83) | copy-start | bytes 6488068
  343.6 25.9 %slice-start.2 = ((s8[4325376]{0:T(1024)(128)(4,1)}), s8[4194304]{0:T(1024)(128)(4,1)S(1)}, s32[]{:S(2)}) async-start(s8[4325376]{0:T(1024)(128)(4,1)} %bitcast.107), calls=%async_computation.2 | async-start | bytes 8388608
  356.4 13.1 %slice-start.3 = ((s8[4325376]{0:T(1024)(128)(4,1)}), s8[131072]{0:T(1024)(128)(4,1)S(1)}, s32[]{:S(2)}) async-start(s8[4325376]{0:T(1024)(128)(4,1)} %bitcast.107), calls=%async_computation.3 | async-start | bytes 262144
  389.2 43.2 %copy-start.77 = (f32[128,4]{0,1:T(4,128)S(1)}, f32[128,4]{0,1:T(4,128)}, u32[]{:S(2)}) copy-start(f32[128,4]{0,1:T(4,128)} %get-tuple-element.172) | copy-start | bytes 6148
  432.5 5.9 copy-start.23
  432.5 5.9 copy-start.86
  447.4 53.2 %copy-start.28 = (bf16[256,2048]{1,0:T(8,128)(2,1)S(1)}, bf16[256,2048]{1,0:T(8,128)(2,1)}, u32[]{:S(2)}) copy-start(bf16[256,2048]{1,0:T(8,128)(2,1)} %get-tuple-element.32) | copy-start | bytes 3145732
  507.7 6.9 copy-start.44
  549.9 10.7 %copy-start.53 = (f32[2048]{0:T(1024)S(1)}, f32[2048]{0:T(1024)}, u32[]{:S(2)}) copy-start(f32[2048]{0:T(1024)} %copy-done.52) | copy-start | bytes 24580
  566.6 9.6 %copy-start.18 = (bf16[2048,256]{1,0:T(8,128)(2,1)S(1)}, bf16[2048,256]{1,0:T(8,128)(2,1)}, u32[]{:S(2)}) copy-start(bf16[2048,256]{1,0:T(8,128)(2,1)} %swap_projection_weight_grad.1) | copy-start | bytes 3145732
  808.0 12.7 %copy-start.13 = (bf16[128,2048]{1,0:T(8,128)(2,1)S(1)}, bf16[128,2048]{1,0:T(8,128)(2,1)}, u32[]{:S(2)}) copy-start(bf16[128,2048]{1,0:T(8,128)(2,1)} %refs_0_.1) | copy-start | bytes 1572868
  808.0 14.2 %copy-start.17 = (f32[128,2048]{1,0:T(8,128)S(1)}, f32[128,2048]{1,0:T(8,128)}, u32[]{:S(2)}) copy-start(f32[128,2048]{1,0:T(8,128)} %get-tuple-element.143) | copy-start | bytes 3145732
  811.9 13.8 %copy-start.1 = (bf16[128,3072]{1,0:T(8,128)(2,1)S(1)}, bf16[128,3072]{1,0:T(8,128)(2,1)}, u32[]{:S(2)}) copy-start(bf16[128,3072]{1,0:T(8,128)(2,1)} %param.21) | copy-start | bytes 2359300
  817.6 7.1 copy-start.33
  (63 other events, 176.4 us)

commit v2 on v1

v2 whole, which is shorter than its diff:
```python
import functools

import jax
import jax.numpy as jnp
from jax import lax
from jax.experimental import pallas as pl
from jax.experimental.pallas import tpu as pltpu
from jax.sharding import PartitionSpec as P

D = 2048
HEADS = 16
NOPE = 128
ROPE = 64
QK = NOPE + ROPE
VDIM = 128
RANK = 512
FE = 1408
NS = 2
EXPERTS = 4
TOP = 2
SETS = NS + EXPERTS
DP = 16
SP = 8
ROWS = 128
SEQ = SP * ROWS
GROUP = DP * ROWS
HEADS_HERE = HEADS // SP
QW = HEADS_HERE * QK
KVW = HEADS_HERE * (NOPE + VDIM)
OW = HEADS_HERE * VDIM
SLICE = FE // DP
CORE_W = 1024
UP_AT = CORE_W + OW
MISC_AT = CORE_W - ROWS
PICK_LANE, GAIN_ONE, GAIN_TWO, GAIN_KV, ROUTER_LANE = 64, 68, 69, 70, 80
ROOM = 96
HALF = SETS * ROOM
FULL = 640
CHUNK = 2 * ROWS
TILE = 512
SCALE = QK ** (-0.5)
PACK = QW + RANK + ROPE + ROPE + OW + ROWS
GU_PART = 2 * HALF // SP
DN_PART = FULL // SP

epsilon = 1e-06
bf16 = jnp.bfloat16
f32 = jnp.float32


def mm(left, right, dims):
    return lax.dot_general(left, right, ((dims[0], dims[1]), ((), ())), preferred_element_type=f32)


def nn(left, right):
    return mm(left, right, ((1,), (0,)))


def nt(left, right):
    return mm(left, right, ((1,), (1,)))


def tn(left, right):
    return mm(left, right, ((0,), (0,)))


def rope_tables(positions):
    half_dim = ROPE // 2
    inverse = 10000.0 ** (-jnp.arange(half_dim, dtype=f32) * 2.0 / ROPE)
    angles = positions[:, None] * inverse[None, :]
    return (jnp.cos(angles), jnp.sin(angles))


def rotate(values, cosine, sine):
    first, second = values[..., : ROPE // 2], values[..., ROPE // 2 :]
    return jnp.concatenate([first * cosine - second * sine, second * cosine + first * sine], axis=-1)


def norm_back(values, scale, gain, grad):
    scaled = gain * grad
    total = jnp.sum(scaled * values, axis=-1, keepdims=True) / values.shape[-1]
    return scale * scaled - values * (scale * scale * scale) * total


def inverse_rms(values):
    return lax.rsqrt(jnp.mean(values * values, axis=-1, keepdims=True) + epsilon)


class Seat:
    def __init__(self, axis):
        own_dp, own_sp = lax.axis_index("dp"), lax.axis_index("sp")
        self.axis = axis
        if axis == "sp":
            self.pair, self.ring, self.core, self.cores = own_sp // 4, own_sp % 4, 0, 1
            self.own, self.size = own_sp, SP
            self.device = lambda index: (own_dp, index)
        else:
            self.ring, self.pair, self.core, self.cores = own_dp // 4, (own_dp // 2) % 2, own_dp % 2, 2
            self.own, self.size = own_dp, DP
            self.device = lambda index: (index, own_sp)

    def index(self, pair, ring, core=0):
        pair, ring = (self.pair + pair) % 2, (self.ring + ring) % 4
        if self.axis == "sp":
            return pair * 4 + ring
        return (ring * 2 + pair) * 2 + (self.core + core) % 2


def remote(src, dst, send_sem, recv_sem, device):
    return pltpu.make_async_remote_copy(
        src_ref=src,
        dst_ref=dst,
        send_sem=send_sem,
        recv_sem=recv_sem,
        device_id=device,
        device_id_type=pl.DeviceIdType.MESH,
    )


def block_of(ref, start, size):
    return ref.at[pl.ds(pl.multiple_of(start, 16), size)]


def middle(rows):
    return (rows // 2 + 15) // 16 * 16


NEAR = ((0, 1), (0, -1), (1, 0))
SHARE = ((0, 0), (0, -1), (0, 1), (1, 0), (0, 2), (1, -1), (1, 1), (1, 2))
ORDER = ((1, 2), (1, 1), (1, -1), (0, 2), (1, 0), (0, 1), (0, -1), (0, 0))


class Gather:
    def __init__(self, axis, rows, width, spare=False):
        self.axis, self.rows, self.width, self.spare = axis, rows, width, spare
        self.count = SP if axis == "sp" else DP

    def in_spec(self):
        return pl.BlockSpec(memory_space=pl.ANY)

    def out(self):
        return (
            jax.ShapeDtypeStruct((self.count * self.rows, self.width), bf16),
            pl.BlockSpec(memory_space=pl.ANY),
        )

    def scratch(self):
        return [pltpu.SemaphoreType.DMA((17,)), pltpu.SemaphoreType.DMA((17,)), pltpu.SemaphoreType.DMA]

    def partners(self, seat):
        near = [seat.index(*n) for n in NEAR]
        return near + ([seat.index(0, 0, 1)] if seat.cores == 2 else [])

    def bind(self, src, out, scratch):
        self.src, self.dst = src, out
        self.send_sem, self.recv_sem, self.local_sem = scratch
        self.seat = Seat(self.axis)

    def view(self, place, half=None):
        start = self.seat.index(*place) * self.rows
        if half is None:
            return block_of(self.dst, start, self.rows)
        cut = middle(self.rows)
        return block_of(self.dst, start + half * cut, (cut, self.rows - cut)[half])

    def table(self, number):
        if number in (0, 1, 2, 8):
            return self.src, self.view((0, 0)), {0: (0, 1), 1: (0, -1), 2: (1, 0), 8: (0, 0, 1)}[number]
        if 8 <= number < 16:
            here = self.view(SHARE[number - 8])
            return here, here, (0, 0, 1)
        place, half, to = {
            7: ((1, -1), 0, (0, 1)),
            16: ((1, 1), 1, (0, -1)),
        }[number] if self.spare and number in (7, 16) else {
            3: ((0, -1), 0, (0, 1)),
            4: ((0, 1), 1, (0, -1)),
            5: ((1, 0), None, (0, 1)),
            6: ((1, 0), None, (0, -1)),
            7: ((0, 2), None, (1, 0)),
        }[number]
        here = self.view(place, half)
        return here, here, to

    def copy(self, number):
        src, dst, to = self.table(number)
        return remote(
            src,
            dst,
            self.send_sem.at[number],
            self.recv_sem.at[number],
            self.seat.device(self.seat.index(*to)),
        )

    def go(self, *numbers):
        for number in numbers:
            self.copy(number).start()

    def share(self, *numbers):
        if self.seat.cores == 2:
            self.go(*[8 + number for number in numbers])

    def arrived(self, *numbers):
        for number in numbers:
            self.copy(number).wait_recv()

    def local(self):
        return pltpu.make_async_copy(self.src, self.view((0, 0)), self.local_sem)

    def step(self, number, shared=True):
        if number == 0:
            self.local().start()
            self.go(0, 1, 2)
            self.share(0)
        elif number == 1:
            self.arrived(0, 1)
            self.go(3, 4)
            self.share(1, 2)
        elif number == 2:
            self.arrived(2)
            self.go(5, 6)
            self.share(3)
        elif number == 3:
            self.arrived(3, 4)
            if not self.spare:
                self.go(7)
            self.share(4)
        elif number == 4:
            self.arrived(5, 6)
            if self.spare:
                self.go(7, 16)
                self.share(5, 6)
                self.arrived(7, 16)
                self.share(7)
            else:
                self.arrived(7)
                self.share(5, 6, 7)
        else:
            numbers = list(range(8)) + [16] * self.spare
            if self.seat.cores == 2:
                numbers = numbers + list(range(8, 16))
                if shared:
                    self.arrived(*range(8, 16))
            for number in numbers:
                self.copy(number).wait_send()
            if shared:
                self.local().wait()


class Scatter:
    def __init__(self, axis, rows, width, kind=f32):
        self.axis, self.rows, self.width, self.kind = axis, rows, width, kind
        self.count = SP if axis == "sp" else DP

    def in_spec(self):
        return pl.BlockSpec(memory_space=pltpu.VMEM)

    def out(self):
        return (
            jax.ShapeDtypeStruct((self.rows, self.width), self.kind),
            pl.BlockSpec(memory_space=pltpu.VMEM),
        )

    def scratch(self):
        block, cut = (self.rows, self.width), middle(self.rows)
        first, second = (cut, self.width), (self.rows - cut, self.width)
        shapes = [block, block, block, first, second, block, block, block]
        shapes = shapes + [(8 if self.axis == "dp" else 4,) + block]
        return [pltpu.SemaphoreType.DMA((16,)), pltpu.SemaphoreType.DMA((16,))] + [
            pltpu.VMEM(shape, bf16) for shape in shapes
        ]

    partners = Gather.partners
    copy = Gather.copy
    go = Gather.go
    arrived = Gather.arrived

    def bind(self, src, out, scratch):
        self.src, self.dst = src, out
        self.send_sem, self.recv_sem = scratch[:2]
        self.got, self.made = scratch[2:10], scratch[10]
        self.seat = Seat(self.axis)

    def given(self, *place):
        return block_of(self.src, self.seat.index(*place) * self.rows, self.rows)

    def slot(self, place):
        if self.axis == "dp":
            return self.made.at[ORDER.index(place)]
        return self.made.at[((0, 2), (1, 0), (0, 1), (0, -1)).index(place)]

    def part(self, place):
        return self.slot(place) if self.axis == "dp" else self.given(*place)

    def ready(self, *places):
        if self.axis == "dp":
            for place in places:
                self.arrived(8 + ORDER.index(place))
                self.add(self.slot(place), [self.slot(place), self.given(*place)])

    def add(self, dst, terms):
        rows = dst.shape[0]
        step = 16

        @pl.loop(0, rows // step)
        def _(i):
            at = pl.ds(pl.multiple_of(i * step, step), step)
            total = terms[0][at, :].astype(f32)
            for term in terms[1:]:
                total = total + term[at, :].astype(f32)
            dst[at, :] = total.astype(dst.dtype)

    def halves(self, ref):
        cut = middle(self.rows)
        return ref.at[pl.ds(0, cut)], ref.at[pl.ds(cut, self.rows - cut)]

    def table(self, number):
        if number >= 8:
            return self.given(*ORDER[number - 8], 1), self.made.at[number - 8], (0, 0, 1)
        src, to = {
            0: (lambda: self.part((1, 2)), (1, 0)),
            1: (lambda: self.part((1, 1)), (0, 1)),
            2: (lambda: self.part((1, -1)), (0, -1)),
            3: (lambda: self.halves(self.slot((0, 2)))[0], (0, 1)),
            4: (lambda: self.halves(self.slot((0, 2)))[1], (0, -1)),
            5: (lambda: self.slot((1, 0)), (1, 0)),
            6: (lambda: self.slot((0, 1)), (0, 1)),
            7: (lambda: self.slot((0, -1)), (0, -1)),
        }[number]
        return src(), self.got[number], to

    def step(self, number):
        if number == 0:
            if self.axis == "dp":
                self.go(*range(8, 16))
            self.ready((1, 2))
            self.go(0)
            self.ready((1, 1))
            self.go(1)
            self.ready((1, -1))
            self.go(2)
        elif number == 1:
            self.ready((0, 2))
            self.arrived(0)
            self.add(self.slot((0, 2)), [self.part((0, 2)), self.got[0]])
            self.go(3, 4)
        elif number == 2:
            self.ready((1, 0))
            self.arrived(1, 2)
            self.add(self.slot((1, 0)), [self.part((1, 0)), self.got[1], self.got[2]])
            self.go(5)
        elif number == 3:
            self.ready((0, 1), (0, -1))
            self.arrived(3, 4)
            for place, half in (((0, 1), 0), ((0, -1), 1)):
                made, part = self.halves(self.slot(place)), self.halves(self.part(place))
                self.add(made[half], [part[half], self.got[3 + half]])
                if self.axis == "sp":
                    self.add(made[1 - half], [part[1 - half]])
                self.go(6 + half)
        elif number == 4:
            self.ready((0, 0))
            self.arrived(5, 6, 7)
            self.add(self.dst, [self.part((0, 0)), self.got[5], self.got[6], self.got[7]])
        else:
            for number in range(16 if self.axis == "dp" else 8):
                self.copy(number).wait_send()


class Swap:
    def __init__(self, axis, shape, take, put, kind="any"):
        self.axis, self.shape, self.take, self.put = axis, shape, take, put
        self.count = SP if axis == "sp" else DP

    def in_spec(self):
        return pl.BlockSpec(memory_space=pl.ANY)

    def out(self):
        return jax.ShapeDtypeStruct(self.shape, bf16), pl.BlockSpec(memory_space=pl.ANY)

    def scratch(self):
        sems = pltpu.SemaphoreType.DMA((self.count,))
        return [sems, sems, pltpu.SemaphoreType.DMA]

    def partners(self, seat):
        return [(seat.own + k) % seat.size for k in range(1, seat.size)]

    def bind(self, src, out, scratch):
        self.src, self.dst = src, out
        self.send_sem, self.recv_sem, self.local_sem = scratch
        self.seat = Seat(self.axis)

    def copy(self, k):
        to = (self.seat.own + k) % self.seat.size
        return remote(
            self.take(self.src, to),
            self.put(self.dst, self.seat.own),
            self.send_sem.at[k],
            self.recv_sem.at[k],
            self.seat.device(to),
        )

    def local(self):
        own = self.seat.own
        return pltpu.make_async_copy(self.take(self.src, own), self.put(self.dst, own), self.local_sem)

    def step(self, number):
        if number == 0:
            self.local().start()

            @pl.loop(1, self.seat.size)
            def _(k):
                self.copy(k).start()

        elif number == 5:

            @pl.loop(1, self.seat.size)
            def _(k):
                self.copy(k).wait_recv()
                self.copy(k).wait_send()

            self.local().wait()


def meet(ops):
    barrier = pltpu.get_barrier_semaphore()
    total = 0
    for axis in ("sp", "dp"):
        mine = [op for op in ops if op.axis == axis]
        if not mine:
            continue
        seat = Seat(axis)
        widest = max(mine, key=lambda op: len(op.partners(seat)))
        for partner in widest.partners(seat):
            pl.semaphore_signal(
                barrier, inc=1, device_id=seat.device(partner), device_id_type=pl.DeviceIdType.MESH
            )
            total += 1
    pl.semaphore_wait(barrier, total)


def exchange(name, number, ops, arrays, plan=None, chained=()):
    chained = dict(chained)
    plan = plan or [(op, step) for step in range(6) for op in range(len(ops))]
    counts = [len(op.scratch()) for op in ops]
    inputs = [k for k in range(len(ops)) if k not in chained]

    def body(*refs):
        given = dict(zip(inputs, refs[: len(inputs)]))
        outs = refs[len(inputs) : len(inputs) + len(ops)]
        rest = refs[len(inputs) + len(ops) :]
        for k, op in enumerate(ops):
            op.bind(given[k] if k in given else outs[chained[k]], outs[k], rest[: counts[k]])
            rest = rest[counts[k] :]
        meet(ops)
        for op, step in plan:
            ops[op].step(step)

    outs = [op.out() for op in ops]
    return pl.pallas_call(
        body,
        name=name,
        out_shape=[shape for shape, _ in outs],
        in_specs=[ops[k].in_spec() for k in inputs],
        out_specs=[spec for _, spec in outs],
        scratch_shapes=[entry for op in ops for entry in op.scratch()],
        compiler_params=pltpu.CompilerParams(
            collective_id=number, has_side_effects=True, vmem_limit_bytes=56 * 2**20
        ),
    )(*arrays)


def expert_kernel(
    hidden_own,
    weights,
    router_t,
    down,
    cot_all,
    picks,
    sum_out,
    mixed_out,
    weights_grad,
    down_grad,
    hidden,
    gate_up,
    down_w,
    sums,
    cot,
    cot_column,
    act_t,
    grads_t,
    gates_up,
    raw,
    acts,
    wide,
    stage,
    made_wide,
    made_down,
    load_sem,
    cot_sem,
    out_sem,
    *rest,
):
    gather, scatter = Gather("dp", ROWS, D), Scatter("dp", ROWS, D + ROWS)
    gather.bind(hidden_own, hidden, rest[:3])
    scatter.bind(sums, sum_out, rest[3:])
    loads = [
        pltpu.make_async_copy(weights.at[pl.ds(0, HALF)], gate_up.at[pl.ds(0, HALF)], load_sem.at[0]),
        pltpu.make_async_copy(weights.at[pl.ds(HALF, HALF)], gate_up.at[pl.ds(FULL, HALF)], load_sem.at[1]),
        pltpu.make_async_copy(down, down_w, load_sem.at[2]),
    ]
    for load in loads:
        load.start()
    meet([gather])
    gather.step(0)
    gate_up[pl.ds(HALF, 16), :] = router_t[...]
    gate_up[pl.ds(HALF + 16, FULL - HALF - 16), :] = jnp.zeros((FULL - HALF - 16, D), bf16)
    gate_up[pl.ds(FULL + HALF, FULL - HALF), :] = jnp.zeros((FULL - HALF, D), bf16)

    def at_least(i, k):
        return (i + 8 - k) // 8

    def rows_of(i):
        pair = i // 3 - i // 4 + i // 5 - i // 6
        ring = 3 * at_least(i, 1) - 2 * at_least(i, 2) - at_least(i, 3) + 2 * at_least(i, 4)
        ring = ring + at_least(i, 5) - 2 * at_least(i, 6) + at_least(i, 7)
        seat = gather.seat
        chip = ((seat.ring + ring) % 4) * 2 + (seat.pair + pair) % 2
        return pl.ds(pl.multiple_of(chip * CHUNK, CHUNK), CHUNK)

    def fetch(i):
        return pltpu.make_async_copy(cot_all.at[rows_of(i)], cot.at[i % 2], cot_sem.at[i % 2])

    def put(i):
        return pltpu.make_async_copy(stage.at[i % 2], mixed_out.at[rows_of(i)], out_sem.at[i % 2])

    fetch(0).start()
    for load in loads:
        load.wait()
    gather.local().wait()

    @pl.loop(0, 8)
    def _(i):
        @pl.when(i < 7)
        def _():
            fetch(i + 1).start()

        for step, when in ((1, 1), (2, 1), (3, 3), (4, 5)):

            @pl.when(i == when)
            def _():
                gather.step(step)

        rows = rows_of(i)
        sibling = rows.start + (1 - gather.seat.core) * ROWS
        landed = block_of(hidden, sibling, ROWS)
        remote(
            landed,
            landed,
            gather.send_sem.at[8 + i],
            gather.recv_sem.at[8 + i],
            gather.seat.device(gather.seat.index(0, 0, 1)),
        ).wait_recv()
        block = hidden[rows, :]

        @pl.loop(0, 2 * FULL // 256)
        def _(n):
            at = pl.ds(pl.multiple_of(n * 256, 256), 256)
            gates_up[:, at] = nt(block, gate_up[at, :])

        fetch(i).wait()
        cot_block = cot[i % 2]
        raw[...] = nt(cot_block, down_w[...])

        @pl.loop(0, CHUNK // 16)
        def _(k):
            at = pl.ds(pl.multiple_of(k * 16, 16), 16)
            lane = lax.broadcasted_iota(jnp.int32, (16, ROWS), 1)
            valid = (lane >= PICK_LANE) & (lane < PICK_LANE + EXPERTS)
            logits = jnp.where(valid, gates_up[at, FULL - ROWS : FULL], -1e30)
            top = jnp.max(logits, axis=1, keepdims=True)
            router = jnp.where(valid, jnp.exp(logits - top), 0.0)
            router = router / jnp.sum(router, axis=1, keepdims=True)
            chosen_rows = pl.ds(pl.multiple_of(rows.start + k * 16, 16), 16)
            dense = router * picks[chosen_rows, :].astype(f32)
            column = lax.broadcasted_iota(jnp.int32, (16, FULL), 1)
            gates = jnp.ones((16, FULL), f32)
            inside = []
            for e in range(EXPERTS):
                low, high = (NS + e) * ROOM, (NS + e + 1) * ROOM
                inside.append((column >= low) & (column < high))
                one = jnp.sum(jnp.where(lane == PICK_LANE + e, dense, 0.0), axis=1, keepdims=True)
                gates = jnp.where(inside[e], one, gates)
            gate, up, raw_grad = gates_up[at, :FULL], gates_up[at, FULL:], raw[at, :]
            sig = 1.0 / (1.0 + jnp.exp(-gate))
            silu = gate * sig
            act = silu * up
            acts[at, :] = (act.astype(bf16).astype(f32) * gates).astype(bf16)
            reached = act * raw_grad
            prob_grad = jnp.zeros((16, ROWS), f32)
            for e in range(EXPERTS):
                one = jnp.sum(jnp.where(inside[e], reached, 0.0), axis=1, keepdims=True)
                prob_grad = jnp.where(lane == PICK_LANE + e, one, prob_grad)
            sums[chosen_rows, D:] = prob_grad.astype(bf16)
            act_grad = raw_grad * gates
            wide[at, :FULL] = (act_grad * up * sig * (1.0 + gate * (1.0 - sig))).astype(bf16)
            wide[at, FULL:] = (act_grad * silu).astype(bf16)

        @pl.when(i >= 2)
        def _():
            put(i - 2).wait()

        @pl.loop(0, D // TILE)
        def _(n):
            at = pl.ds(pl.multiple_of(n * TILE, TILE), TILE)
            stage[i % 2, :, at] = nn(acts[...], down_w[:, at]).astype(bf16)
            sums[rows, at] = nn(wide[...], gate_up[:, at]).astype(bf16)

        put(i).start()
        act_t[:, rows] = acts[...].T
        grads_t[:, rows] = wide[...].T

    put(6).wait()
    put(7).wait()

    def columns(n):
        return pl.ds(pl.multiple_of(n * 256, 256), 256)

    def fetch_column(n):
        return pltpu.make_async_copy(cot_all.at[:, columns(n)], cot_column.at[n % 2], cot_sem.at[n % 2])

    def stores(n):
        k = n % 2
        return (
            pltpu.make_async_copy(made_wide.at[k], weights_grad.at[:, columns(n)], out_sem.at[k]),
            pltpu.make_async_copy(made_down.at[k], down_grad.at[:, columns(n)], out_sem.at[2 + k]),
        )

    def weight_grads(first, last):
        @pl.loop(first, last)
        def _(n):
            @pl.when(n < D // 256 - 1)
            def _():
                fetch_column(n + 1).start()

            @pl.when(n >= 2)
            def _():
                for store in stores(n - 2):
                    store.wait()

            made = nn(grads_t[...], hidden[:, columns(n)]).astype(bf16)
            made_wide[n % 2, :HALF, :] = made[:HALF]
            made_wide[n % 2, HALF:, :] = made[FULL : FULL + HALF]
            fetch_column(n).wait()
            made_down[n % 2] = nn(act_t[...], cot_column[n % 2]).astype(bf16)
            for store in stores(n):
                store.start()

    fetch_column(0).start()
    scatter.step(0)
    weight_grads(0, 4)
    scatter.step(1)
    scatter.step(2)
    weight_grads(4, 6)
    scatter.step(3)
    weight_grads(6, 8)
    scatter.step(4)
    for n in (6, 7):
        for store in stores(n):
            store.wait()
    gather.step(5, shared=False)
    scatter.step(5)


def experts(hidden_own, weights, router_t, down, cot_all, picks):
    any_spec, vmem = pl.BlockSpec(memory_space=pl.ANY), pl.BlockSpec(memory_space=pltpu.VMEM)
    gather, scatter = Gather("dp", ROWS, D), Scatter("dp", ROWS, D + ROWS)
    flops = 2 * GROUP * D * FULL * 9
    return pl.pallas_call(
        expert_kernel,
        name="experts",
        out_shape=[
            jax.ShapeDtypeStruct((ROWS, D + ROWS), f32),
            jax.ShapeDtypeStruct((GROUP, D), bf16),
            jax.ShapeDtypeStruct((2 * HALF, D), bf16),
            jax.ShapeDtypeStruct((FULL, D), bf16),
        ],
        in_specs=[any_spec, any_spec, vmem, any_spec, any_spec, vmem],
        out_specs=[vmem, any_spec, any_spec, any_spec],
        scratch_shapes=[
            pltpu.VMEM((GROUP, D), bf16),
            pltpu.VMEM((2 * FULL, D), bf16),
            pltpu.VMEM((FULL, D), bf16),
            pltpu.VMEM((GROUP, D + ROWS), bf16),
            pltpu.VMEM((2, CHUNK, D), bf16),
            pltpu.VMEM((2, GROUP, 256), bf16),
            pltpu.VMEM((FULL, GROUP), bf16),
            pltpu.VMEM((2 * FULL, GROUP), bf16),
            pltpu.VMEM((CHUNK, 2 * FULL), f32),
            pltpu.VMEM((CHUNK, FULL), f32),
            pltpu.VMEM((CHUNK, FULL), bf16),
            pltpu.VMEM((CHUNK, 2 * FULL), bf16),
            pltpu.VMEM((2, CHUNK, D), bf16),
            pltpu.VMEM((2, 2 * HALF, 256), bf16),
            pltpu.VMEM((2, FULL, 256), bf16),
            pltpu.SemaphoreType.DMA((3,)),
            pltpu.SemaphoreType.DMA((2,)),
            pltpu.SemaphoreType.DMA((4,)),
        ]
        + gather.scratch()
        + scatter.scratch(),
        compiler_params=pltpu.CompilerParams(
            collective_id=2, has_side_effects=True, vmem_limit_bytes=61 * 2**20
        ),
        cost_estimate=pl.CostEstimate(flops=flops, bytes_accessed=40 * 2**20, transcendentals=GROUP * FULL),
    )(hidden_own, weights, router_t, down, cot_all, picks)


def wait_all(copies):
    for copy in copies:
        copy.wait()


def swap_halves(values):
    lane = lax.broadcasted_iota(jnp.int32, values.shape, 1) % ROPE
    return jnp.where(lane < ROPE // 2, pltpu.roll(values, 96, 1), pltpu.roll(values, 32, 1))


def attention_ops():
    return (
        Gather("sp", ROWS, D, spare=True),
        Gather("dp", ROWS, PACK),
        Swap(
            "sp",
            (OW, D),
            lambda ref, j: ref.at[pl.ds(pl.multiple_of(j * OW, OW), OW), pl.ds(CORE_W, OW)],
            lambda ref, j: ref.at[:, pl.ds(pl.multiple_of(j * OW, OW), OW)],
        ),
        Gather("dp", ROWS, D, spare=True),
        Swap(
            "dp",
            (2 * HALF, D),
            lambda ref, j: ref.at[j],
            lambda ref, j: ref.at[:, pl.ds(pl.multiple_of(j * ROWS, ROWS), ROWS)],
        ),
        Scatter("sp", ROWS, D),
    )


def attention_kernel(
    tokens,
    pack,
    cotangent,
    pieces,
    cosine,
    sine,
    attn_sum,
    cot_all,
    gate_up,
    tok_out,
    weights_out,
    hidden_out,
    compressed_out,
    latent_out,
    query_out,
    key_out,
    value_out,
    head_out,
    out_w_out,
    misc_out,
    total_out,
    tok,
    weights,
    hidden,
    qc,
    latent,
    up_w,
    query,
    key,
    value,
    heads,
    out_w,
    misc_t,
    totals,
    sums,
    save_sem,
    *rest,
):
    ops = attention_ops()
    tok_op, pack_op, out_op, cot_op, piece_op, sum_op = ops
    bound = ((tokens, tok), (pack, weights), (weights, out_w), (cotangent, cot_all), (pieces, gate_up), (sums, attn_sum))
    for op, (src, dst) in zip(ops, bound):
        count = len(op.scratch())
        op.bind(src, dst, rest[:count])
        rest = rest[count:]
    meet(ops)
    tok_op.step(0)
    pack_op.step(0)
    for step in (1, 2, 3):
        tok_op.step(step)
        pack_op.step(step)
    pack_op.step(4)
    tok_op.step(4)
    pack_op.step(5)
    out_op.step(0)
    cot_op.step(0)
    piece_op.step(0)
    tok_op.step(5)
    saves = [
        pltpu.make_async_copy(src, dst, save_sem.at[k])
        for k, (src, dst) in enumerate(
            (
                (tok, tok_out),
                (weights, weights_out),
                (hidden, hidden_out),
                (qc.at[:, pl.ds(QW, RANK)], compressed_out),
                (latent, latent_out),
                (query, query_out),
                (key, key_out),
                (value, value_out),
                (heads, head_out),
                (out_w, out_w_out),
                (misc_t, misc_out),
                (totals, total_out),
            )
        )
    ]
    saves[0].start()
    saves[1].start()
    misc_t[...] = weights[:, MISC_AT:CORE_W].astype(f32).T
    saves[10].start()
    up = weights[:, UP_AT:].reshape(DP, 4, RANK // DP, ROWS)
    for k in range(4):
        up_w[:, k * ROWS : (k + 1) * ROWS] = up[:, k].reshape(RANK, ROWS)
    row = lax.broadcasted_iota(jnp.int32, (D, RANK), 0)
    column = lax.broadcasted_iota(jnp.int32, (D, RANK), 1)
    each = RANK // DP
    compact = ((row % ROWS < each) & (row // ROWS * each + row % ROWS == column)).astype(bf16)
    kv_gain = nn(misc_t[GAIN_KV - 6 : GAIN_KV + 2, :].astype(bf16), compact)[6:7]
    gain = misc_t[GAIN_ONE : GAIN_ONE + 1, :]

    @pl.loop(0, SEQ // 16)
    def _(k):
        at = pl.ds(pl.multiple_of(k * 16, 16), 16)
        values = tok[at, :].astype(f32)
        hidden[at, :] = (values * inverse_rms(values) * gain).astype(bf16)

    saves[2].start()
    cot_op.step(1)

    @pl.loop(0, SEQ // 256)
    def _(k):
        at = pl.ds(pl.multiple_of(k * 256, 256), 256)
        qc[at, :] = nn(hidden[at, :], weights[:, :CORE_W])

    saves[3].start()
    cot_op.step(2)

    @pl.loop(0, SEQ // 128)
    def _(k):
        at = pl.ds(pl.multiple_of(k * 128, 128), 128)
        inner = qc[at, QW : QW + RANK]
        latent[at, :] = (inner * inverse_rms(inner) * kv_gain).astype(bf16)
        ropes, key_rope = qc[at, 2 * NOPE : QW], qc[at, MISC_AT:CORE_W]
        cos, sin = cosine[at, :], sine[at, :]
        ropes = (ropes * cos + swap_halves(ropes) * sin).astype(bf16)
        key_rope = key_rope * cos + swap_halves(key_rope) * sin
        lane = lax.broadcasted_iota(jnp.int32, key_rope.shape, 1)
        key_rope = jnp.where(lane < ROPE, key_rope, 0.0)
        expanded = nn(latent[at, :], up_w[...]).astype(bf16)
        for h in range(HEADS_HERE):
            query[h, at, :NOPE] = qc[at, h * NOPE : (h + 1) * NOPE].astype(bf16)
            query[h, at, NOPE:] = ropes
            turned = key_rope if h == 0 else pltpu.roll(key_rope, ROPE, 1)
            key[h, at, NOPE:] = turned.astype(bf16)
            base = h * (NOPE + VDIM)
            key[h, at, :NOPE] = expanded[:, base : base + NOPE]
            value[h, at, :] = expanded[:, base + NOPE : base + NOPE + VDIM]

    for k in (4, 5, 6, 7):
        saves[k].start()
    for h in range(HEADS_HERE):
        for i in range(SEQ // 256):
            at, seen = pl.ds(i * 256, 256), (i + 1) * 256
            scores = nt(query[h, at, :], key[h, :seen, :]) * SCALE
            row = lax.broadcasted_iota(jnp.int32, scores.shape, 0) + i * 256
            column = lax.broadcasted_iota(jnp.int32, scores.shape, 1)
            scores = jnp.where(column <= row, scores, -1e9)
            top = jnp.max(scores, axis=1, keepdims=True)
            parts = jnp.exp(scores - top)
            total = jnp.sum(parts, axis=1, keepdims=True)
            probs = (parts / total).astype(bf16)
            heads[at, h * VDIM : (h + 1) * VDIM] = nn(probs, value[h, :seen, :]).astype(bf16)
            totals[h, at, :] = jnp.broadcast_to(top + jnp.log(total), (256, ROWS))

    saves[8].start()
    saves[11].start()
    out_op.step(5)
    saves[9].start()

    @pl.loop(0, D // TILE)
    def _(n):
        at = pl.ds(pl.multiple_of(n * TILE, TILE), TILE)
        sums[:, at] = nn(heads[...], out_w[:, at]).astype(bf16)

    sum_op.step(0)
    cot_op.step(3)
    sum_op.step(1)
    sum_op.step(2)
    cot_op.step(4)
    sum_op.step(3)
    sum_op.step(4)
    wait_all(saves)
    sum_op.step(5)
    cot_op.step(5)
    piece_op.step(5)


def attention(tokens, pack, cotangent, pieces, cosine, sine):
    any_spec, vmem = pl.BlockSpec(memory_space=pl.ANY), pl.BlockSpec(memory_space=pltpu.VMEM)
    kept = [
        ((SEQ, D), bf16),
        ((D, PACK), bf16),
        ((SEQ, D), bf16),
        ((SEQ, RANK), f32),
        ((SEQ, RANK), bf16),
        ((HEADS_HERE, SEQ, 2 * NOPE), bf16),
        ((HEADS_HERE, SEQ, 2 * NOPE), bf16),
        ((HEADS_HERE, SEQ, VDIM), bf16),
        ((SEQ, OW), bf16),
        ((OW, D), bf16),
        ((ROWS, D), f32),
        ((HEADS_HERE, SEQ, ROWS), f32),
    ]
    made = [((ROWS, D), f32), ((GROUP, D), bf16), ((2 * HALF, D), bf16)]
    scratch = kept[:3] + [((SEQ, CORE_W), f32), kept[4], ((RANK, KVW), bf16)] + kept[5:] + [((SEQ, D), bf16)]
    return pl.pallas_call(
        attention_kernel,
        name="attention",
        out_shape=[jax.ShapeDtypeStruct(*shape) for shape in made + kept],
        in_specs=[any_spec] * 4 + [vmem] * 2,
        out_specs=[vmem] + [any_spec] * (len(made) + len(kept) - 1),
        scratch_shapes=[pltpu.VMEM(*shape) for shape in scratch]
        + [pltpu.SemaphoreType.DMA((len(kept),))]
        + [entry for op in attention_ops() for entry in op.scratch()],
        compiler_params=pltpu.CompilerParams(
            collective_id=0, has_side_effects=True, vmem_limit_bytes=60 * 2**20
        ),
        cost_estimate=pl.CostEstimate(
            flops=2 * SEQ * D * (CORE_W + OW), bytes_accessed=60 * 2**20, transcendentals=SEQ * SEQ
        ),
    )(tokens, pack, cotangent, pieces, cosine, sine)


def per_device(
    tokens,
    cotangent,
    chosen,
    attn_gain,
    w_query,
    w_kv_down,
    kv_gain,
    w_kv_up,
    w_out,
    ffn_gain,
    w_router,
    shared_gate,
    shared_up,
    shared_down,
    expert_gate,
    expert_up,
    expert_down,
):
    own_sp = lax.axis_index("sp")
    picks = jnp.any(chosen[:, :, None] == jnp.arange(EXPERTS, dtype=jnp.int32), axis=1).astype(bf16)
    own_query = lax.dynamic_slice_in_dim(w_query, own_sp * QW, QW, 1)
    own_up = lax.dynamic_slice_in_dim(w_kv_up, own_sp * KVW, KVW, 1)
    pack = jnp.concatenate(
        [
            own_query[:, :NOPE],
            own_query[:, QK : QK + NOPE],
            own_query[:, NOPE:QK],
            own_query[:, QK + NOPE :],
            w_kv_down,
            picks,
            attn_gain[:, None],
            ffn_gain[:, None],
            jnp.pad(kv_gain, (0, ROWS - kv_gain.shape[0]))[:, None],
            jnp.zeros((ROWS, 9), bf16),
            w_router,
            jnp.zeros((ROWS, 44), bf16),
            lax.dynamic_slice_in_dim(w_out, own_sp * OW, OW, 1),
            own_up.reshape(RANK // DP, 4, ROWS).transpose(1, 0, 2).reshape(ROWS, ROWS),
        ],
        axis=1,
    )
    gate_up = jnp.stack(
        [
            jnp.concatenate([shared_gate, expert_gate], axis=1),
            jnp.concatenate([shared_up, expert_up], axis=1),
        ]
    )
    gate_up = gate_up.reshape(2, ROWS, SETS, DP, SLICE).transpose(3, 0, 2, 4, 1)
    gate_up = jnp.pad(gate_up, ((0, 0),) * 3 + ((0, ROOM - SLICE), (0, 0)))
    gate_up = gate_up.reshape(DP, 2 * HALF, ROWS)
    down = jnp.concatenate([shared_down, expert_down], axis=1).transpose(1, 0, 2)
    down = jnp.pad(down, ((0, 0), (0, ROOM - SLICE), (0, 0))).reshape(HALF, D)
    down = jnp.pad(down, ((0, FULL - HALF), (0, 0)))

    cosine, sine = rope_tables(jnp.arange(SEQ, dtype=f32))
    cosine = jnp.concatenate([cosine] * 4, axis=1)
    sine = jnp.concatenate([-sine, sine] * 2, axis=1)
    (
        attn_proj,
        cot_all,
        gate_up,
        tok_all,
        weights,
        hidden_one,
        compressed,
        latent,
        queries,
        keys,
        values,
        head_out,
        out_w,
        misc,
        log_totals,
    ) = attention(tokens, pack, cotangent, gate_up, cosine, sine)
    gain_one, gain_two = misc[GAIN_ONE], misc[GAIN_TWO]
    latent_gain = misc[GAIN_KV].reshape(DP, ROWS)[:, : RANK // DP].reshape(RANK)
    router_t = misc[ROUTER_LANE : ROUTER_LANE + 16].astype(bf16)
    router_w = router_t[:EXPERTS]
    picks_all = weights[:, MISC_AT:CORE_W]
    resid_two = tokens.astype(f32) + attn_proj
    scale_two = inverse_rms(resid_two)
    hidden_two = (resid_two * scale_two * gain_two).astype(bf16)

    hidden_grad, mixed_part, gate_up_grad, down_grad = experts(
        hidden_two, gate_up, router_t, down, cot_all, picks_all
    )
    prob_grad = hidden_grad[:, D + PICK_LANE : D + PICK_LANE + EXPERTS]
    hidden_grad = hidden_grad[:, :D]

    logits = nt(hidden_two, router_w)
    router = jax.nn.softmax(logits, axis=-1)
    prob_grad = prob_grad * picks.astype(f32)
    logit_grad = (
        router * (prob_grad - jnp.sum(router * prob_grad, axis=-1, keepdims=True))
    ).astype(bf16)
    hidden_grad = hidden_grad + nn(logit_grad, router_w)
    router_grad = tn(hidden_two, logit_grad)
    gain_two_grad = jnp.sum(hidden_grad * resid_two * scale_two, axis=0)
    upstream = cotangent.astype(f32)
    resid_two_grad = upstream + norm_back(resid_two, scale_two, gain_two, hidden_grad)
    proj_grad = resid_two_grad.astype(bf16)

    proj_grad_all, mixed, gate_up_grad, down_grad = exchange(
        "gather_projection_grad",
        4,
        [
            Gather("sp", ROWS, D, spare=True),
            Scatter("dp", ROWS, D),
            Scatter("sp", GU_PART, D, bf16),
            Scatter("sp", DN_PART, D, bf16),
        ],
        [proj_grad, mixed_part, gate_up_grad, down_grad],
    )
    mixed = (resid_two + mixed).astype(bf16)
    out_w_grad = tn(head_out, proj_grad_all)
    head_grad = nt(proj_grad_all, out_w).astype(bf16)
    rows = jnp.arange(SEQ, dtype=jnp.int32)
    allowed = rows[None, :] <= rows[:, None]
    low = jnp.arange(ROWS) < ROPE
    rope_grad, nope_grads, expanded_grads, key_rope_grad = 0.0, [], [], 0.0
    for h in range(HEADS_HERE):
        piece = head_grad[:, h * VDIM : (h + 1) * VDIM]
        prob = jnp.exp(jnp.where(allowed, nt(queries[h], keys[h]) * SCALE, -1e9) - log_totals[h, :, :1])
        dprob = nt(piece, values[h])
        delta = jnp.sum(prob * dprob, axis=-1, keepdims=True)
        score_grad = (prob * (dprob - delta) * SCALE).astype(bf16)
        query_grad = nn(score_grad, keys[h]).astype(bf16)
        key_grad = tn(score_grad, queries[h]).astype(bf16)
        value_grad = tn(prob.astype(bf16), piece).astype(bf16)
        nope_grads.append(query_grad[:, :NOPE])
        rope_grad = rope_grad + query_grad[:, NOPE:].astype(f32)
        expanded_grads += [key_grad[:, :NOPE], value_grad]
        own = key_grad[:, NOPE + h * ROPE : NOPE + (h + 1) * ROPE].astype(f32)
        key_rope_grad = key_rope_grad + own

    def unrotate(values, cos, sin):
        flipped = values.reshape(SEQ, -1, 2, ROPE // 2)[:, :, ::-1].reshape(values.shape)
        return values * cos - flipped * sin

    rope_grad = unrotate(rope_grad, cosine, sine).astype(bf16)
    key_rope_grad = unrotate(key_rope_grad, cosine[:, :ROPE], sine[:, :ROPE]).astype(bf16)
    expanded_grad = jnp.concatenate(expanded_grads, axis=1)
    up_w = weights[:, UP_AT:].reshape(DP, 4, RANK // DP, ROWS).transpose(0, 2, 1, 3).reshape(RANK, KVW)
    up_w_grad = tn(latent, expanded_grad)
    latent_grad = nt(expanded_grad, up_w)
    scale_latent = inverse_rms(compressed)
    latent_in_grad = norm_back(compressed, scale_latent, latent_gain, latent_grad)
    latent_gain_grad = jnp.sum(latent_grad * compressed * scale_latent, axis=0)
    qc_grad = jnp.concatenate(
        nope_grads
        + [rope_grad, latent_in_grad.astype(bf16), key_rope_grad, jnp.zeros((SEQ, ROPE), bf16)],
        axis=1,
    )
    qc_w_grad = tn(hidden_one, qc_grad)
    hidden_one_grad = nt(qc_grad, weights[:, :CORE_W])
    resid_all = tok_all.astype(f32)
    gain_one_grad = jnp.sum(hidden_one_grad * resid_all * inverse_rms(resid_all), axis=0)

    (out_cols_grad,) = exchange(
        "swap_projection_weight_grad",
        5,
        [
            Swap(
                "sp",
                (D, OW),
                lambda ref, j: ref.at[:, pl.ds(pl.multiple_of(j * OW, OW), OW)],
                lambda ref, j: ref.at[pl.ds(pl.multiple_of(j * OW, OW), OW)],
            )
        ],
        [out_w_grad.astype(bf16)],
    )
    latent_gain_grad = jnp.pad(
        latent_gain_grad.reshape(DP, RANK // DP), ((0, 0), (0, ROWS - RANK // DP))
    ).reshape(D)
    grads = jnp.concatenate(
        [
            qc_w_grad[:, : QW + RANK + ROPE].astype(bf16),
            gain_one_grad.astype(bf16)[:, None],
            gain_two_grad.astype(bf16)[:, None],
            latent_gain_grad.astype(bf16)[:, None],
            router_grad.astype(bf16),
            jnp.zeros((D, ROPE - 7), bf16),
            out_cols_grad,
            up_w_grad.astype(bf16).reshape(D, ROWS),
        ],
        axis=1,
    )
    grads, hidden_one_grad, _, gu_total, dn_total = exchange(
        "sum_grads",
        6,
        [
            Scatter("dp", ROWS, PACK, bf16),
            Scatter("sp", ROWS, D),
            Swap(
                "dp",
                (DP * GU_PART, ROWS),
                lambda ref, j: ref.at[:, pl.ds(pl.multiple_of(j * ROWS, ROWS), ROWS)],
                lambda ref, j: ref.at[pl.ds(pl.multiple_of(j * GU_PART, GU_PART), GU_PART)],
            ),
            Gather("sp", DP * GU_PART, ROWS),
            Gather("sp", DN_PART, D),
        ],
        [grads, hidden_one_grad.astype(bf16), gate_up_grad, down_grad],
        plan=[(2, 0), (0, 0), (1, 0), (4, 0), (2, 5), (3, 0)]
        + [(op, step) for step in range(1, 6) for op in (1, 0, 4, 3)],
        chained=[(3, 2)],
    )
    (grads,) = exchange("gather_grads", 7, [Gather("sp", ROWS, PACK)], [grads])
    gu_total = gu_total.reshape(SP, DP, GU_PART, ROWS)
    grads = grads.reshape(SP, ROWS, PACK)
    resid_one = tokens.astype(f32)
    own_scale = inverse_rms(resid_one)
    tokens_grad = resid_two_grad + norm_back(resid_one, own_scale, gain_one, hidden_one_grad)
    tokens_grad = tokens_grad.astype(bf16)

    def side_by_side(block, width):
        return block.astype(f32).transpose(1, 0, 2).reshape(-1, SP * width)

    query_total = grads[:, :, :QW]
    query_total = jnp.concatenate(
        [
            query_total[:, :, :NOPE],
            query_total[:, :, 2 * NOPE : 2 * NOPE + ROPE],
            query_total[:, :, NOPE : 2 * NOPE],
            query_total[:, :, 2 * NOPE + ROPE :],
        ],
        axis=2,
    )
    query_total = side_by_side(query_total, QW)
    tail = jnp.sum(grads[:, :, QW:CORE_W].astype(f32), axis=0)
    down_total, tail = tail[:, : RANK + ROPE], tail[:, RANK + ROPE :]
    out_total = side_by_side(grads[:, :, CORE_W:UP_AT], OW)
    up_total = side_by_side(grads[:, :, UP_AT:].reshape(SP, RANK // DP, KVW), KVW)

    gu_total = gu_total.transpose(0, 2, 1, 3).reshape(2, SETS, ROOM, DP, ROWS)[:, :, :SLICE]
    gu_total = gu_total.transpose(0, 4, 1, 3, 2).reshape(2, ROWS, SETS, FE).astype(f32)
    dn_total = dn_total[:HALF].reshape(SETS, ROOM, D)[:, :SLICE].transpose(1, 0, 2).astype(f32)
    return (
        mixed,
        tokens_grad,
        tail[:, 0],
        query_total,
        down_total,
        tail[: RANK // DP, 2],
        up_total,
        out_total,
        tail[:, 1],
        tail[:, 3:7],
        gu_total[0, :, :NS],
        gu_total[1, :, :NS],
        dn_total[:, :NS],
        gu_total[0, :, NS:],
        gu_total[1, :, NS:],
        dn_total[:, NS:],
    )


def solution(mesh):
    rows = P(("dp", "sp"), None)
    vec, mat, cube = P("dp"), P("dp", None), P("dp", None, None)
    return jax.shard_map(
        per_device,
        mesh=mesh,
        in_specs=(rows, rows, rows, vec, mat, mat, vec, mat, mat, vec, mat) + (cube,) * 6,
        out_specs=(rows, rows, vec, mat, mat, vec, mat, mat, vec, mat) + (cube,) * 6,
        check_vma=False,
    )
```

time: 839 us -> 732 us (0.87)
  matrix products: 142 us -> 40.2 us
  Pallas kernels: 501 us -> 532 us
  local copies, waits for them, and re-layouts: 129 us -> 102 us
  other arithmetic: 51.9 us -> 42.1 us
    pallas_call x0 -> x2, Pallas kernels: none -> 297 us  [the longest x1 151 us: attention(): pl.pallas_call(attention_kernel, name='attention', out_shape=[jax.ShapeDt...]
    pallas_call x9 -> x4, Pallas kernels: 501 us -> 236 us  [exchange(): pl.pallas_call(body, name=name, out_shape=[shape for shape, _ in outs], i...]
    dot_general x34 -> x19, matrix products: 142 us -> 40.2 us  [mm(): lax.dot_general(left, right, ((dims[0], dims[1]), ((), ())), preferred_el...]
    concatenate x3, local copies, waits for them, and re-layouts: 26.1 us -> 15.5 us  [the longest x1 10.6 us: per_device(): jnp.concatenate([qc_w_grad[:, :QW + RANK + ROPE].astype(bf16), gain_one_g...]
    concatenate x4 -> x1, other arithmetic: 10.8 us -> 1.85 us  [per_device(): cosine = jnp.concatenate([cosine] * 4, axis=1)]
    unnamed x210 -> x116, local copies, waits for them, and re-layouts: 43.2 us -> 35.8 us
where the time goes in v2:
time: 732 us; the launch traced here: 718 us
  Pallas kernels  532 us (73%)
  local copies, waits for them, and re-layouts  102 us (14%)
  other arithmetic  42.1 us (6%)
  matrix products  40.2 us (5%)
    pallas_call x4, Pallas kernels, exchange(): pl.pallas_call(body, name=name, out_shape=[shape for shape, _ in outs], i...  236 us
    pallas_call x1, Pallas kernels, attention(): pl.pallas_call(attention_kernel, name='attention', out_shape=[jax.ShapeDt...  151 us
    pallas_call x1, Pallas kernels, experts(): pl.pallas_call(expert_kernel, name='experts', out_shape=[jax.ShapeDtypeSt...  146 us
    dot_general x19, matrix products, mm(): lax.dot_general(left, right, ((dims[0], dims[1]), ((), ())), preferred_el...  40.2 us
    unnamed x116, local copies, waits for them, and re-layouts  35.8 us

profile of v2, /device:TPU:1, one launch (start us, length us, event | category | flops | bytes accessed | tf_op | source)
XLA Modules:
  0.0 718.4 jit_solution(9812070490248893169)
XLA Ops:
  9.6 3.0 copy.239
  13.7 2.5 copy.240
  17.9 3.8 copy.242
  24.4 3.5 pad.22.clone
  36.5 150.7 %attention.1 = (f32[128,2048]{1,0:T(8,128)}, bf16[2048,2048]{1,0:T(8,128)(2,1)}, bf16[1152,2048]{1,0:T(8,128)(2,1)}, bf16[1024,2048]{1,0:T(8,128)(2,1)}, bf16[20...) custom-call(bf16[128,2048]{1,0:T(8,128)(2,1)} %tokens.1, ...), custom_call_target="tpu_custom_call" | custom-call | flops 5368709120 | bytes 62914560 | tf_op jit(solution)/shard_map/attention/pallas_call | solution.py:937
  188.8 3.2 fusion.2
  198.9 146.1 %experts.1 = (f32[128,2176]{1,0:T(8,128)}, bf16[2048,2048]{1,0:T(8,128)(2,1)}, bf16[1152,2048]{1,0:T(8,128)(2,1)}, bf16[640,2048]{1,0:T(8,128)(2,1)}) custom-call(bf16[128,2048]{1,0:T(8,128)(2,1)} %copy-done.4, bf16[1152,2048]{1,0:T(8,128)(2,1)} %get-tuple-element.45.weights, bf16[16,2048]{1,0:T(8,128)(2,1)} %slice.241.router_t, ...), custom_call_target="tpu_custom_call" | custom-call | flops 48318382080 | bytes 41943040 | tf_op jit(solution)/shard_map/experts/pallas_call | solution.py:679
  347.1 2.6 multiply_reduce_fusion.5
  351.0 2.8 fusion.63
  353.8 97.9 %gather_projection_grad.1 = (bf16[1024,2048]{1,0:T(8,128)(2,1)}, f32[128,2048]{1,0:T(8,128)}, bf16[144,2048]{1,0:T(8,128)(2,1)}, bf16[80,2048]{1,0:T(8,128)(2,1)}) custom-call(bf16[128,2048]{1,0:T(8,128)(2,1)} %get-tuple-element.160.refs_0_, bf16[2048,2048]{1,0:T(8,128)(2,1)} %get-tuple-element.49.refs_1_, bf16[1152,2048]{1,0:T(8,128)(2,1)} %get-tuple-element.50.refs_2_, ...), custom_call_target="tpu_custom_call" | custom-call | tf_op jit(solution)/shard_map/gather_projection_grad/pallas_call | solution.py:460
  451.7 3.9 convolution_convert_fusion.7
  457.8 2.2 convolution_convert_fusion.refs_0_
  460.0 16.8 %swap_projection_weight_grad.1 = bf16[2048,256]{1,0:T(8,128)(2,1)} custom-call(bf16[256,2048]{1,0:T(8,128)(2,1)} %convolution_convert_fusion.refs_0_), custom_call_target="tpu_custom_call" | custom-call | tf_op jit(solution)/shard_map/swap_projection_weight_grad/pallas_call | solution.py:460
  493.8 2.1 convert_add_fusion.1
  501.4 2.4 fusion.25
  503.9 3.8 multiply_reduce_fusion.2
  507.8 3.1 subtract_convert_fusion
  511.0 4.0 concatenate.46
  516.3 9.2 %fusion.64 = (bf16[1024,2048]{1,0:T(8,128)(2,1)}, bf16[2048]{0:T(1024)(128)(2,1)S(1)}) fusion(f32[1024]{0:T(1024)S(1)} %add_rsqrt_fusion, bf16[1024,2048]{1,0:T(8,128)(2,1)} %get-tuple-element.61, bf16[1024,1024]{1,0:T(8,128)(2,1)S(1)} %concatenate.46, bf16[2048,1408]{1,0:T(8,128)(2,1)} %get-tuple-element.47), kind=kOutput, calls=%fused_computation.147 | convolution fusion | flops 4305451008 | bytes 14688256 | tf_op jit(solution)/shard_map/dot_general | solution.py:52
  525.6 8.0 %fusion.69 = bf16[2048,1024]{1,0:T(8,128)(2,1)} fusion(bf16[1024,2048]{1,0:T(8,128)(2,1)S(1)} %copy-done.46, bf16[1024,1024]{1,0:T(8,128)(2,1)} %copy-done.16), kind=kOutput, calls=%fused_computation.152 | convolution fusion | flops 4294967296 | bytes 10485760 | tf_op jit(solution)/shard_map/dot_general | solution.py:52
  535.9 10.6 %concatenate.47.refs_0_ = bf16[2048,1408]{1,0:T(8,128)(2,1)} concatenate(bf16[2048,960]{1,0:T(8,128)(2,1)} %bitcast.136, bf16[2048,1]{1,0:T(8,128)(2,1)} %convert_element_type.217, bf16[2048,1]{1,0:T(8,128)(2,1)S(1)} %copy-done.14, bf16[2048,1]{1,0:T(8,128)(2,1)S(1)} %bitcast.138, bf16[2048,4]{1,0:T(8,128)(2,1)S(1)} %copy-done.13, bf16[2048,57]{1,0:T(8,128)(2,1)} %broadcast_in_dim.26, ...), dimensions={1} | concatenate | bytes 11534336 | tf_op jit(solution)/shard_map/concatenate | solution.py:1130
  546.5 97.1 %sum_grads.1 = (bf16[128,1408]{1,0:T(8,128)(2,1)}, f32[128,2048]{1,0:T(8,128)}, bf16[2304,128]{1,0:T(8,128)(2,1)}, bf16[18432,128]{1,0:T(8,128)(2,1)}, bf16[640,2048]{1,0:T(8,128)(2,1)}) custom-call(bf16[2048,1408]{1,0:T(8,128)(2,1)} %concatenate.47.refs_0_, bf16[1024,2048]{1,0:T(8,128)(2,1)} %get-tuple-element.168.refs_1_, ...), custom_call_target="tpu_custom_call" | custom-call | tf_op jit(solution)/shard_map/sum_grads/pallas_call | solution.py:460
  643.6 5.8 copy.269
  651.7 23.6 %gather_grads.1 = bf16[1024,1408]{1,0:T(8,128)(2,1)} custom-call(bf16[128,1408]{1,0:T(8,128)(2,1)} %get-tuple-element.67.refs_0_), custom_call_target="tpu_custom_call" | custom-call | tf_op jit(solution)/shard_map/gather_grads/pallas_call | solution.py:460
  681.8 2.1 convert_bitcast_fusion.3
  686.8 2.3 copy.290
  693.7 2.4 slice.274
  697.0 2.6 copy.270
  703.4 4.7 copy.277
  708.0 3.5 copy.275
  711.5 3.5 copy.274
  715.1 2.8 copy.276
  (212 shorter events, 83.5 us)
Async XLA Ops:
  0.6 6.9 copy-start
  0.7 13.0 %copy-start.18 = (bf16[128,4,1408]{2,1,0:T(4,128)(2,1)S(1)}, bf16[128,4,1408]{2,1,0:T(4,128)(2,1)}, u32[]{:S(2)}) copy-start(bf16[128,4,1408]{2,1,0:T(4,128)(2,1)} %param.31) | copy-start | bytes 4325380
  0.7 12.0 %copy-start.34 = (bf16[128,2,1408]{2,1,0:T(2,128)(2,1)S(1)}, bf16[128,2,1408]{2,1,0:T(2,128)(2,1)}, u32[]{:S(2)}) copy-start(bf16[128,2,1408]{2,1,0:T(2,128)(2,1)} %param.29) | copy-start | bytes 2162692
  27.9 3.8 copy-start.19
  27.9 3.8 copy-start.33
  36.5 150.7 %copy-start.7 = (bf16[128,2048]{1,0:T(8,128)(2,1)S(1)}, bf16[128,2048]{1,0:T(8,128)(2,1)}, u32[]{:S(2)}) copy-start(bf16[128,2048]{1,0:T(8,128)(2,1)} %tokens.1) | copy-start | bytes 1572868
  187.2 4.9 copy-start.2
  188.8 3.5 copy-start.27
  188.8 3.8 copy-start.25
  194.4 4.5 copy-start.4
  344.9 4.8 copy-start.5
  345.0 6.1 copy-start.35
  451.7 4.0 copy-start.28
  451.7 6.0 copy-start.41
  457.8 19.1 %copy-start.36 = (bf16[2,1024,128]{2,1,0:T(8,128)(2,1)S(1)}, bf16[2,1024,128]{2,1,0:T(8,128)(2,1)}, u32[]{:S(2)}) copy-start(bf16[2,1024,128]{2,1,0:T(8,128)(2,1)} %get-tuple-element.59) | copy-start | bytes 1572868
  482.2 6.3 copy-start.37
  483.8 7.4 %copy-start.20 = (bf16[1024,256]{1,0:T(8,128)(2,1)}, bf16[1024,256]{1,0:T(8,128)(2,1)S(1)}, u32[]{:S(2)}) copy-start(bf16[1024,256]{1,0:T(8,128)(2,1)S(1)} %convolution_convert_fusion.5) | copy-start | bytes 1572868
  483.8 4.7 copy-start.39
  493.8 10.1 %copy-start.3 = (f32[1024,512]{1,0:T(8,128)S(1)}, f32[1024,512]{1,0:T(8,128)}, u32[]{:S(2)}) copy-start(f32[1024,512]{1,0:T(8,128)} %get-tuple-element.60) | copy-start | bytes 6291460
  507.7 3.3 slice-start.3
  507.7 3.3 copy-start.31
  516.3 9.2 %copy-start.46 = (bf16[1024,2048]{1,0:T(8,128)(2,1)S(1)}, bf16[1024,2048]{1,0:T(8,128)(2,1)}, u32[]{:S(2)}) copy-start(bf16[1024,2048]{1,0:T(8,128)(2,1)} %get-tuple-element.53) | copy-start | bytes 12582916
  525.5 10.4 %copy-start.10 = (bf16[2048,256]{1,0:T(8,128)(2,1)S(1)}, bf16[2048,256]{1,0:T(8,128)(2,1)}, u32[]{:S(2)}) copy-start(bf16[2048,256]{1,0:T(8,128)(2,1)} %swap_projection_weight_grad.1) | copy-start | bytes 3145732
  525.5 10.4 %copy-start.13 = (bf16[2048,4]{1,0:T(8,128)(2,1)S(1)}, bf16[2048,4]{1,0:T(8,128)(2,1)}, u32[]{:S(2)}) copy-start(bf16[2048,4]{1,0:T(8,128)(2,1)} %copy.265) | copy-start | bytes 49156
  525.5 10.4 %copy-start.14 = (bf16[2048,1]{1,0:T(8,128)(2,1)S(1)}, bf16[2048,1]{1,0:T(8,128)(2,1)}, u32[]{:S(2)}) copy-start(bf16[2048,1]{1,0:T(8,128)(2,1)} %convert_element_type.218) | copy-start | bytes 12292
  525.5 10.3 %copy-start.15 = (bf16[2048,128]{1,0:T(8,128)(2,1)S(1)}, bf16[2048,128]{1,0:T(8,128)(2,1)}, u32[]{:S(2)}) copy-start(bf16[2048,128]{1,0:T(8,128)(2,1)} %reshape.226) | copy-start | bytes 1572868
  643.6 5.9 copy-start.8
  643.6 5.9 copy-start.11
  643.6 6.2 copy-start.9
  690.7 5.4 slice-start
  692.0 4.1 slice-start.1
  711.5 6.4 copy-start.1
  (19 other events, 35.6 us)

commit v3 on v2

--- a/solution.py
+++ b/solution.py
@@ -2,6 +2,7 @@
 
 import jax
 import jax.numpy as jnp
+import numpy as np
 from jax import lax
 from jax.experimental import pallas as pl
 from jax.experimental.pallas import tpu as pltpu
@@ -30,7 +31,8 @@
 OW = HEADS_HERE * VDIM
 SLICE = FE // DP
 CORE_W = 1024
-UP_AT = CORE_W + OW
+UP_AT = CORE_W
+GRAD_UP_AT = CORE_W + OW
 MISC_AT = CORE_W - ROWS
 PICK_LANE, GAIN_ONE, GAIN_TWO, GAIN_KV, ROUTER_LANE = 64, 68, 69, 70, 80
 ROOM = 96
@@ -39,8 +41,11 @@
 CHUNK = 2 * ROWS
 TILE = 512
 SCALE = QK ** (-0.5)
-PACK = QW + RANK + ROPE + ROPE + OW + ROWS
+PACK = QW + RANK + ROPE + ROPE + ROWS
+GRAD_PACK = PACK + OW
 GU_PART = 2 * HALF // SP
+RELAY = 2 * HALF // SP
+UNITS = ROOM // SP
 DN_PART = FULL // SP
 
 epsilon = 1e-06
@@ -64,16 +69,13 @@
     return mm(left, right, ((0,), (0,)))
 
 
-def rope_tables(positions):
-    half_dim = ROPE // 2
-    inverse = 10000.0 ** (-jnp.arange(half_dim, dtype=f32) * 2.0 / ROPE)
-    angles = positions[:, None] * inverse[None, :]
-    return (jnp.cos(angles), jnp.sin(angles))
-
-
-def rotate(values, cosine, sine):
-    first, second = values[..., : ROPE // 2], values[..., ROPE // 2 :]
-    return jnp.concatenate([first * cosine - second * sine, second * cosine + first * sine], axis=-1)
+def rope_tables():
+    inverse = 10000.0 ** (-np.arange(ROPE // 2, dtype=np.float64) * 2.0 / ROPE)
+    angles = np.arange(SEQ, dtype=np.float64)[:, None] * inverse[None, :]
+    cosine, sine = np.cos(angles), np.sin(angles)
+    cosine = np.concatenate([cosine] * 4, axis=1)
+    sine = np.concatenate([-sine, sine] * 2, axis=1)
+    return jnp.asarray(cosine, f32), jnp.asarray(sine, f32)
 
 
 def norm_back(values, scale, gain, grad):
@@ -248,8 +250,8 @@
 
 
 class Scatter:
-    def __init__(self, axis, rows, width, kind=f32):
-        self.axis, self.rows, self.width, self.kind = axis, rows, width, kind
+    def __init__(self, axis, rows, width, kind=f32, spare=False):
+        self.axis, self.rows, self.width, self.kind, self.spare = axis, rows, width, kind, spare
         self.count = SP if axis == "sp" else DP
 
     def in_spec(self):
@@ -265,8 +267,8 @@
         block, cut = (self.rows, self.width), middle(self.rows)
         first, second = (cut, self.width), (self.rows - cut, self.width)
         shapes = [block, block, block, first, second, block, block, block]
-        shapes = shapes + [(8 if self.axis == "dp" else 4,) + block]
-        return [pltpu.SemaphoreType.DMA((16,)), pltpu.SemaphoreType.DMA((16,))] + [
+        shapes = shapes + [(8 if self.axis == "dp" else 5,) + block]
+        return [pltpu.SemaphoreType.DMA((17,)), pltpu.SemaphoreType.DMA((17,))] + [
             pltpu.VMEM(shape, bf16) for shape in shapes
         ]
 
@@ -287,7 +289,8 @@
     def slot(self, place):
         if self.axis == "dp":
             return self.made.at[ORDER.index(place)]
-        return self.made.at[((0, 2), (1, 0), (0, 1), (0, -1)).index(place)]
+        kept = ((1, 0), (0, 1), (0, -1)) + (((1, 1), (1, -1)) if self.spare else ((0, 2),))
+        return self.made.at[kept.index(place)]
 
     def part(self, place):
         return self.slot(place) if self.axis == "dp" else self.given(*place)
@@ -310,13 +313,26 @@
                 total = total + term[at, :].astype(f32)
             dst[at, :] = total.astype(dst.dtype)
 
+    def add_half(self, place, half, term):
+        made, part = self.halves(self.slot(place)), self.halves(self.part(place))
+        self.add(made[half], [part[half], term])
+        if self.axis == "sp":
+            self.add(made[1 - half], [part[1 - half]])
+
     def halves(self, ref):
         cut = middle(self.rows)
         return ref.at[pl.ds(0, cut)], ref.at[pl.ds(cut, self.rows - cut)]
 
     def table(self, number):
-        if number >= 8:
+        if 8 <= number < 16:
             return self.given(*ORDER[number - 8], 1), self.made.at[number - 8], (0, 0, 1)
+        if self.spare and number in (0, 1, 2, 3, 4, 16):
+            if number in (1, 2):
+                return self.slot((1, 3 - 2 * number)), self.got[number], (0, 3 - 2 * number)
+            half = 0 if number in (0, 3) else 1
+            src = self.halves(self.part((1, 2) if number in (0, 16) else (0, 2)))[half]
+            dst = self.halves(self.got[0])[half] if number in (0, 16) else self.got[number]
+            return src, dst, (0, 1 - 2 * half)
         src, to = {
             0: (lambda: self.part((1, 2)), (1, 0)),
             1: (lambda: self.part((1, 1)), (0, 1)),
@@ -334,11 +350,22 @@
             if self.axis == "dp":
                 self.go(*range(8, 16))
             self.ready((1, 2))
+            if self.spare:
+                self.go(0, 16)
+                self.ready((0, 2))
+                self.go(3, 4)
+                self.ready((1, 1), (1, -1))
+                return
             self.go(0)
             self.ready((1, 1))
             self.go(1)
             self.ready((1, -1))
             self.go(2)
+        elif number == 1 and self.spare:
+            self.arrived(0, 16)
+            for place, half in (((1, 1), 0), ((1, -1), 1)):
+                self.add_half(place, half, self.halves(self.got[0])[half])
+                self.go(1 + half)
         elif number == 1:
             self.ready((0, 2))
             self.arrived(0)
@@ -353,17 +380,15 @@
             self.ready((0, 1), (0, -1))
             self.arrived(3, 4)
             for place, half in (((0, 1), 0), ((0, -1), 1)):
-                made, part = self.halves(self.slot(place)), self.halves(self.part(place))
-                self.add(made[half], [part[half], self.got[3 + half]])
-                if self.axis == "sp":
-                    self.add(made[1 - half], [part[1 - half]])
+                self.add_half(place, half, self.got[3 + half])
                 self.go(6 + half)
         elif number == 4:
             self.ready((0, 0))
             self.arrived(5, 6, 7)
             self.add(self.dst, [self.part((0, 0)), self.got[5], self.got[6], self.got[7]])
         else:
-            for number in range(16 if self.axis == "dp" else 8):
+            numbers = list(range(16 if self.axis == "dp" else 8)) + [16] * self.spare
+            for number in numbers:
                 self.copy(number).wait_send()
 
 
@@ -470,6 +495,19 @@
     )(*arrays)
 
 
+def expert_of(column):
+    lane = jnp.zeros(column.shape, jnp.int32)
+    for e in range(EXPERTS):
+        low = (NS + e) * ROOM
+        lane = jnp.where((column >= low) & (column < low + ROOM), PICK_LANE + e, lane)
+    return lane
+
+
+def two_terms(values):
+    high = values.astype(bf16)
+    return high, (values - high.astype(f32)).astype(bf16)
+
+
 def expert_kernel(
     hidden_own,
     weights,
@@ -485,19 +523,21 @@
     gate_up,
     down_w,
     sums,
-    cot,
+    stage,
     cot_column,
-    act_t,
-    grads_t,
+    acts,
+    wide,
     gates_up,
     raw,
-    acts,
-    wide,
-    stage,
+    gates,
+    dense_terms,
+    reached,
+    spread,
+    collect,
     made_wide,
     made_down,
     load_sem,
-    cot_sem,
+    in_sem,
     out_sem,
     *rest,
 ):
@@ -505,39 +545,51 @@
     gather.bind(hidden_own, hidden, rest[:3])
     scatter.bind(sums, sum_out, rest[3:])
     loads = [
-        pltpu.make_async_copy(weights.at[pl.ds(0, HALF)], gate_up.at[pl.ds(0, HALF)], load_sem.at[0]),
-        pltpu.make_async_copy(weights.at[pl.ds(HALF, HALF)], gate_up.at[pl.ds(FULL, HALF)], load_sem.at[1]),
         pltpu.make_async_copy(down, down_w, load_sem.at[2]),
+        pltpu.make_async_copy(weights, sums.at[pl.ds(0, 2 * HALF), pl.ds(0, D)], load_sem.at[0]),
     ]
     for load in loads:
         load.start()
+
+    def chunk(i):
+        return pl.ds(pl.multiple_of(i * CHUNK, CHUNK), CHUNK)
+
+    def columns(n):
+        return pl.ds(pl.multiple_of(n * 256, 256), 256)
+
+    def fetch(i):
+        return pltpu.make_async_copy(cot_all.at[chunk(i)], stage.at[i % 2], in_sem.at[i % 2])
+
+    def put(i):
+        return pltpu.make_async_copy(stage.at[i % 2], mixed_out.at[chunk(i)], in_sem.at[i % 2])
+
+    def fetch_column(n):
+        return pltpu.make_async_copy(cot_all.at[:, columns(n)], cot_column.at[n % 2], in_sem.at[2 + n % 2])
+
+    def stores(n):
+        k = n % 2
+        return (
+            pltpu.make_async_copy(made_wide.at[k], weights_grad.at[:, columns(n)], out_sem.at[k]),
+            pltpu.make_async_copy(made_down.at[k], down_grad.at[:, columns(n)], out_sem.at[2 + k]),
+        )
+
+    fetch(0).start()
+    fetch_column(0).start()
     meet([gather])
     gather.step(0)
     gate_up[pl.ds(HALF, 16), :] = router_t[...]
     gate_up[pl.ds(HALF + 16, FULL - HALF - 16), :] = jnp.zeros((FULL - HALF - 16, D), bf16)
     gate_up[pl.ds(FULL + HALF, FULL - HALF), :] = jnp.zeros((FULL - HALF, D), bf16)
-
-    def at_least(i, k):
-        return (i + 8 - k) // 8
-
-    def rows_of(i):
-        pair = i // 3 - i // 4 + i // 5 - i // 6
-        ring = 3 * at_least(i, 1) - 2 * at_least(i, 2) - at_least(i, 3) + 2 * at_least(i, 4)
-        ring = ring + at_least(i, 5) - 2 * at_least(i, 6) + at_least(i, 7)
-        seat = gather.seat
-        chip = ((seat.ring + ring) % 4) * 2 + (seat.pair + pair) % 2
-        return pl.ds(pl.multiple_of(chip * CHUNK, CHUNK), CHUNK)
-
-    def fetch(i):
-        return pltpu.make_async_copy(cot_all.at[rows_of(i)], cot.at[i % 2], cot_sem.at[i % 2])
-
-    def put(i):
-        return pltpu.make_async_copy(stage.at[i % 2], mixed_out.at[rows_of(i)], out_sem.at[i % 2])
-
-    fetch(0).start()
-    for load in loads:
-        load.wait()
-    gather.local().wait()
+    row = lax.broadcasted_iota(jnp.int32, (ROWS, FULL), 0)
+    lane_of = expert_of(lax.broadcasted_iota(jnp.int32, (ROWS, FULL), 1))
+    hot = (row == lane_of).astype(bf16)
+    spread[:ROWS, :] = hot
+    spread[ROWS:, :] = hot
+    lane = lax.broadcasted_iota(jnp.int32, (FULL, ROWS), 1)
+    hot = (lane == expert_of(lax.broadcasted_iota(jnp.int32, (FULL, ROWS), 0))).astype(bf16)
+    collect[:FULL, :] = hot
+    collect[FULL:, :] = hot
+    loads[0].wait()
 
     @pl.loop(0, 8)
     def _(i):
@@ -545,15 +597,38 @@
         def _():
             fetch(i + 1).start()
 
+        fetch(i).wait()
+        raw[chunk(i), :] = nt(stage[i % 2], down_w[...])
+
+    loads[1].wait()
+    for k in range(2 * SETS):
+        for part in range(SP):
+            units = sums[part * RELAY + k * UNITS : part * RELAY + (k + 1) * UNITS, :D]
+            at = k // SETS * FULL + k % SETS * ROOM + part * UNITS
+            gate_up[at : at + UNITS, :] = units
+    gather.local().wait()
+
+    def at_least(i, k):
+        return (i + 8 - k) // 8
+
+    def chip_of(i):
+        pair = i // 3 - i // 4 + i // 5 - i // 6
+        ring = 3 * at_least(i, 1) - 2 * at_least(i, 2) - at_least(i, 3) + 2 * at_least(i, 4)
+        ring = ring + at_least(i, 5) - 2 * at_least(i, 6) + at_least(i, 7)
+        seat = gather.seat
+        return ((seat.ring + ring) % 4) * 2 + (seat.pair + pair) % 2
+
+    @pl.loop(0, 8)
+    def _(i):
         for step, when in ((1, 1), (2, 1), (3, 3), (4, 5)):
 
             @pl.when(i == when)
             def _():
                 gather.step(step)
 
-        rows = rows_of(i)
-        sibling = rows.start + (1 - gather.seat.core) * ROWS
-        landed = block_of(hidden, sibling, ROWS)
+        chip = chip_of(i)
+        rows = chunk(chip)
+        landed = block_of(hidden, chip * CHUNK + (1 - gather.seat.core) * ROWS, ROWS)
         remote(
             landed,
             landed,
@@ -561,80 +636,34 @@
             gather.recv_sem.at[8 + i],
             gather.seat.device(gather.seat.index(0, 0, 1)),
         ).wait_recv()
-        block = hidden[rows, :]
-
-        @pl.loop(0, 2 * FULL // 256)
-        def _(n):
-            at = pl.ds(pl.multiple_of(n * 256, 256), 256)
-            gates_up[:, at] = nt(block, gate_up[at, :])
-
-        fetch(i).wait()
-        cot_block = cot[i % 2]
-        raw[...] = nt(cot_block, down_w[...])
-
-        @pl.loop(0, CHUNK // 16)
+        gates_up[...] = nt(hidden[rows, :], gate_up[...])
+        lane = lax.broadcasted_iota(jnp.int32, (CHUNK, ROWS), 1)
+        valid = (lane >= PICK_LANE) & (lane < PICK_LANE + EXPERTS)
+        logits = jnp.where(valid, gates_up[:, FULL - ROWS : FULL], -1e30)
+        top = jnp.max(logits, axis=1, keepdims=True)
+        router = jnp.where(valid, jnp.exp(logits - top), 0.0)
+        router = router / jnp.sum(router, axis=1, keepdims=True)
+        dense_terms[:, :ROWS], dense_terms[:, ROWS:] = two_terms(router * picks[rows, :].astype(f32))
+        gates[...] = nn(dense_terms[...], spread[...])
+
+        @pl.loop(0, CHUNK // 32)
         def _(k):
-            at = pl.ds(pl.multiple_of(k * 16, 16), 16)
-            lane = lax.broadcasted_iota(jnp.int32, (16, ROWS), 1)
-            valid = (lane >= PICK_LANE) & (lane < PICK_LANE + EXPERTS)
-            logits = jnp.where(valid, gates_up[at, FULL - ROWS : FULL], -1e30)
-            top = jnp.max(logits, axis=1, keepdims=True)
-            router = jnp.where(valid, jnp.exp(logits - top), 0.0)
-            router = router / jnp.sum(router, axis=1, keepdims=True)
-            chosen_rows = pl.ds(pl.multiple_of(rows.start + k * 16, 16), 16)
-            dense = router * picks[chosen_rows, :].astype(f32)
-            column = lax.broadcasted_iota(jnp.int32, (16, FULL), 1)
-            gates = jnp.ones((16, FULL), f32)
-            inside = []
-            for e in range(EXPERTS):
-                low, high = (NS + e) * ROOM, (NS + e + 1) * ROOM
-                inside.append((column >= low) & (column < high))
-                one = jnp.sum(jnp.where(lane == PICK_LANE + e, dense, 0.0), axis=1, keepdims=True)
-                gates = jnp.where(inside[e], one, gates)
-            gate, up, raw_grad = gates_up[at, :FULL], gates_up[at, FULL:], raw[at, :]
+            at = pl.ds(pl.multiple_of(k * 32, 32), 32)
+            there = pl.ds(pl.multiple_of(chip * CHUNK + k * 32, 32), 32)
+            column = lax.broadcasted_iota(jnp.int32, (32, FULL), 1)
+            factor = jnp.where(column < NS * ROOM, 1.0, gates[at, :])
+            gate, up, raw_grad = gates_up[at, :FULL], gates_up[at, FULL:], raw[there, :]
             sig = 1.0 / (1.0 + jnp.exp(-gate))
             silu = gate * sig
             act = silu * up
-            acts[at, :] = (act.astype(bf16).astype(f32) * gates).astype(bf16)
-            reached = act * raw_grad
-            prob_grad = jnp.zeros((16, ROWS), f32)
-            for e in range(EXPERTS):
-                one = jnp.sum(jnp.where(inside[e], reached, 0.0), axis=1, keepdims=True)
-                prob_grad = jnp.where(lane == PICK_LANE + e, one, prob_grad)
-            sums[chosen_rows, D:] = prob_grad.astype(bf16)
-            act_grad = raw_grad * gates
-            wide[at, :FULL] = (act_grad * up * sig * (1.0 + gate * (1.0 - sig))).astype(bf16)
-            wide[at, FULL:] = (act_grad * silu).astype(bf16)
-
-        @pl.when(i >= 2)
-        def _():
-            put(i - 2).wait()
-
-        @pl.loop(0, D // TILE)
-        def _(n):
-            at = pl.ds(pl.multiple_of(n * TILE, TILE), TILE)
-            stage[i % 2, :, at] = nn(acts[...], down_w[:, at]).astype(bf16)
-            sums[rows, at] = nn(wide[...], gate_up[:, at]).astype(bf16)
-
-        put(i).start()
-        act_t[:, rows] = acts[...].T
-        grads_t[:, rows] = wide[...].T
-
-    put(6).wait()
-    put(7).wait()
-
-    def columns(n):
-        return pl.ds(pl.multiple_of(n * 256, 256), 256)
-
-    def fetch_column(n):
-        return pltpu.make_async_copy(cot_all.at[:, columns(n)], cot_column.at[n % 2], cot_sem.at[n % 2])
-
-    def stores(n):
-        k = n % 2
-        return (
-            pltpu.make_async_copy(made_wide.at[k], weights_grad.at[:, columns(n)], out_sem.at[k]),
-            pltpu.make_async_copy(made_down.at[k], down_grad.at[:, columns(n)], out_sem.at[2 + k]),
-        )
+            acts[there, :] = (act.astype(bf16).astype(f32) * factor).astype(bf16)
+            reached[at, :FULL], reached[at, FULL:] = two_terms(act * raw_grad)
+            act_grad = raw_grad * factor
+            wide[there, :FULL] = (act_grad * up * sig * (1.0 + gate * (1.0 - sig))).astype(bf16)
+            wide[there, FULL:] = (act_grad * silu).astype(bf16)
+
+        sums[rows, D:] = nn(reached[...], collect[...]).astype(bf16)
+        sums[rows, :D] = nn(wide[rows, :], gate_up[...]).astype(bf16)
 
     def weight_grads(first, last):
         @pl.loop(first, last)
@@ -648,31 +677,40 @@
                 for store in stores(n - 2):
                     store.wait()
 
-            made = nn(grads_t[...], hidden[:, columns(n)]).astype(bf16)
+            made = tn(wide[...], hidden[:, columns(n)]).astype(bf16)
             made_wide[n % 2, :HALF, :] = made[:HALF]
             made_wide[n % 2, HALF:, :] = made[FULL : FULL + HALF]
             fetch_column(n).wait()
-            made_down[n % 2] = nn(act_t[...], cot_column[n % 2]).astype(bf16)
+            made_down[n % 2] = tn(acts[...], cot_column[n % 2]).astype(bf16)
             for store in stores(n):
                 store.start()
 
-    fetch_column(0).start()
+    def outputs(first, last):
+        @pl.loop(first, last)
+        def _(i):
+            @pl.when(i >= 2)
+            def _():
+                put(i - 2).wait()
+
+            stage[i % 2] = nn(acts[chunk(i), :], down_w[...]).astype(bf16)
+            put(i).start()
+
     scatter.step(0)
-    weight_grads(0, 4)
+    outputs(0, 8)
     scatter.step(1)
     scatter.step(2)
-    weight_grads(4, 6)
+    weight_grads(0, 3)
     scatter.step(3)
-    weight_grads(6, 8)
+    weight_grads(3, 8)
     scatter.step(4)
-    for n in (6, 7):
-        for store in stores(n):
-            store.wait()
+    for i in (6, 7):
+        put(i).wait()
+        wait_all(stores(i))
     gather.step(5, shared=False)
     scatter.step(5)
 
 
-def experts(hidden_own, weights, router_t, down, cot_all, picks):
+def experts(*arrays):
     any_spec, vmem = pl.BlockSpec(memory_space=pl.ANY), pl.BlockSpec(memory_space=pltpu.VMEM)
     gather, scatter = Gather("dp", ROWS, D), Scatter("dp", ROWS, D + ROWS)
     flops = 2 * GROUP * D * FULL * 9
@@ -694,17 +732,19 @@
             pltpu.VMEM((GROUP, D + ROWS), bf16),
             pltpu.VMEM((2, CHUNK, D), bf16),
             pltpu.VMEM((2, GROUP, 256), bf16),
-            pltpu.VMEM((FULL, GROUP), bf16),
-            pltpu.VMEM((2 * FULL, GROUP), bf16),
+            pltpu.VMEM((GROUP, FULL), bf16),
+            pltpu.VMEM((GROUP, 2 * FULL), bf16),
             pltpu.VMEM((CHUNK, 2 * FULL), f32),
+            pltpu.VMEM((GROUP, FULL), f32),
             pltpu.VMEM((CHUNK, FULL), f32),
-            pltpu.VMEM((CHUNK, FULL), bf16),
+            pltpu.VMEM((CHUNK, 2 * ROWS), bf16),
             pltpu.VMEM((CHUNK, 2 * FULL), bf16),
-            pltpu.VMEM((2, CHUNK, D), bf16),
+            pltpu.VMEM((2 * ROWS, FULL), bf16),
+            pltpu.VMEM((2 * FULL, ROWS), bf16),
             pltpu.VMEM((2, 2 * HALF, 256), bf16),
             pltpu.VMEM((2, FULL, 256), bf16),
-            pltpu.SemaphoreType.DMA((3,)),
-            pltpu.SemaphoreType.DMA((2,)),
+            pltpu.SemaphoreType.DMA((4,)),
+            pltpu.SemaphoreType.DMA((4,)),
             pltpu.SemaphoreType.DMA((4,)),
         ]
         + gather.scratch()
@@ -713,7 +753,7 @@
             collective_id=2, has_side_effects=True, vmem_limit_bytes=61 * 2**20
         ),
         cost_estimate=pl.CostEstimate(flops=flops, bytes_accessed=40 * 2**20, transcendentals=GROUP * FULL),
-    )(hidden_own, weights, router_t, down, cot_all, picks)
+    )(*arrays)
 
 
 def wait_all(copies):
@@ -724,26 +764,35 @@
 def swap_halves(values):
     lane = lax.broadcasted_iota(jnp.int32, values.shape, 1) % ROPE
     return jnp.where(lane < ROPE // 2, pltpu.roll(values, 96, 1), pltpu.roll(values, 32, 1))
+
+
+def causal(scores):
+    rows, seen = scores.shape
+    row = lax.broadcasted_iota(jnp.int32, (rows, rows), 0)
+    column = lax.broadcasted_iota(jnp.int32, (rows, rows), 1)
+    last = jnp.where(column <= row, scores[:, seen - rows :], -1e9)
+    return last if seen == rows else jnp.concatenate([scores[:, : seen - rows], last], axis=1)
 
 
 def attention_ops():
     return (
         Gather("sp", ROWS, D, spare=True),
         Gather("dp", ROWS, PACK),
-        Swap(
-            "sp",
-            (OW, D),
-            lambda ref, j: ref.at[pl.ds(pl.multiple_of(j * OW, OW), OW), pl.ds(CORE_W, OW)],
-            lambda ref, j: ref.at[:, pl.ds(pl.multiple_of(j * OW, OW), OW)],
-        ),
+        Gather("dp", ROWS, D, spare=True),
         Gather("dp", ROWS, D, spare=True),
         Swap(
             "dp",
-            (2 * HALF, D),
+            (RELAY, D),
             lambda ref, j: ref.at[j],
             lambda ref, j: ref.at[:, pl.ds(pl.multiple_of(j * ROWS, ROWS), ROWS)],
         ),
-        Scatter("sp", ROWS, D),
+        Gather("sp", RELAY, D),
+        Swap(
+            "sp",
+            (ROWS, D),
+            lambda ref, j: ref.at[pl.ds(pl.multiple_of(j * ROWS, ROWS), ROWS)],
+            lambda ref, j: ref.at[:, pl.ds(pl.multiple_of(j * OW, OW), OW)],
+        ),
     )
 
 
@@ -751,12 +800,21 @@
     tokens,
     pack,
     cotangent,
-    pieces,
+    shared_gate,
+    expert_gate,
+    shared_up,
+    expert_up,
+    shared_down,
+    expert_down,
+    out_own,
     cosine,
     sine,
-    attn_sum,
+    resid_two,
+    hidden_two,
     cot_all,
+    gate_up_part,
     gate_up,
+    down_out,
     tok_out,
     weights_out,
     hidden_out,
@@ -782,30 +840,82 @@
     out_w,
     misc_t,
     totals,
-    sums,
+    tok_heads,
+    pieces,
+    down,
+    gate_shared,
+    gate_routed,
+    up_shared,
+    up_routed,
+    down_shared,
+    down_routed,
     save_sem,
+    load_sem,
     *rest,
 ):
     ops = attention_ops()
-    tok_op, pack_op, out_op, cot_op, piece_op, sum_op = ops
-    bound = ((tokens, tok), (pack, weights), (weights, out_w), (cotangent, cot_all), (pieces, gate_up), (sums, attn_sum))
+    tok_op, pack_op, out_op, cot_op, piece_op, gate_up_op, head_op = ops
+    bound = (
+        (tokens, tok),
+        (pack, weights),
+        (out_own, out_w),
+        (cotangent, cot_all),
+        (pieces, gate_up_part),
+        (gate_up_part, gate_up),
+        (heads, tok_heads),
+    )
     for op, (src, dst) in zip(ops, bound):
         count = len(op.scratch())
         op.bind(src, dst, rest[:count])
         rest = rest[count:]
+    loads = [
+        pltpu.make_async_copy(src, dst, load_sem.at[k])
+        for k, (src, dst) in enumerate(
+            (
+                (shared_gate, gate_shared),
+                (expert_gate, gate_routed),
+                (shared_up, up_shared),
+                (expert_up, up_routed),
+                (shared_down, down_shared),
+                (expert_down, down_routed),
+            )
+        )
+    ]
+    for load in loads:
+        load.start()
     meet(ops)
     tok_op.step(0)
     pack_op.step(0)
-    for step in (1, 2, 3):
+    for step in (1, 2):
         tok_op.step(step)
         pack_op.step(step)
+
+    wait_all(loads)
+    row = lax.broadcasted_iota(jnp.int32, (DP * UNITS, FE), 0)
+    column = lax.broadcasted_iota(jnp.int32, (DP * UNITS, FE), 1)
+    group, unit = row // UNITS, row - row // UNITS * UNITS + tok_op.seat.own * UNITS
+    pick = ((group * SLICE + unit == column) & (unit < SLICE)).astype(bf16)
+    for k, (shared, routed) in enumerate(((gate_shared, gate_routed), (up_shared, up_routed))):
+        for e in range(SETS):
+            piece = shared[:, e, :] if e < NS else routed[:, e - NS, :]
+            piece = nt(pick, piece).astype(bf16)
+            at = (k * SETS + e) * UNITS
+            for d in range(DP):
+                pieces[d, at : at + UNITS, :] = piece[d * UNITS : (d + 1) * UNITS]
+    piece_op.step(0)
+    for e in range(SETS):
+        part = down_shared[:, e, :] if e < NS else down_routed[:, e - NS, :]
+        down[e * ROOM : e * ROOM + SLICE, :] = part
+        down[e * ROOM + SLICE : (e + 1) * ROOM, :] = jnp.zeros((ROOM - SLICE, D), bf16)
+    down[HALF:, :] = jnp.zeros((FULL - HALF, D), bf16)
+    down_save = pltpu.make_async_copy(down, down_out, load_sem.at[0])
+    down_save.start()
+    tok_op.step(3)
+    pack_op.step(3)
     pack_op.step(4)
-    tok_op.step(4)
     pack_op.step(5)
     out_op.step(0)
-    cot_op.step(0)
-    piece_op.step(0)
-    tok_op.step(5)
+    tok_op.local().wait()
     saves = [
         pltpu.make_async_copy(src, dst, save_sem.at[k])
         for k, (src, dst) in enumerate(
@@ -825,40 +935,46 @@
             )
         )
     ]
-    saves[0].start()
     saves[1].start()
     misc_t[...] = weights[:, MISC_AT:CORE_W].astype(f32).T
-    saves[10].start()
     up = weights[:, UP_AT:].reshape(DP, 4, RANK // DP, ROWS)
     for k in range(4):
         up_w[:, k * ROWS : (k + 1) * ROWS] = up[:, k].reshape(RANK, ROWS)
-    row = lax.broadcasted_iota(jnp.int32, (D, RANK), 0)
-    column = lax.broadcasted_iota(jnp.int32, (D, RANK), 1)
     each = RANK // DP
-    compact = ((row % ROWS < each) & (row // ROWS * each + row % ROWS == column)).astype(bf16)
-    kv_gain = nn(misc_t[GAIN_KV - 6 : GAIN_KV + 2, :].astype(bf16), compact)[6:7]
+    for d in range(DP):
+        misc_t[0:1, d * each : (d + 1) * each] = misc_t[GAIN_KV : GAIN_KV + 1, d * ROWS : d * ROWS + each]
+    kv_gain = misc_t[0:1, :RANK]
+    saves[10].start()
     gain = misc_t[GAIN_ONE : GAIN_ONE + 1, :]
 
-    @pl.loop(0, SEQ // 16)
-    def _(k):
-        at = pl.ds(pl.multiple_of(k * 16, 16), 16)
-        values = tok[at, :].astype(f32)
-        hidden[at, :] = (values * inverse_rms(values) * gain).astype(bf16)
-
-    saves[2].start()
-    cot_op.step(1)
+    def project(*places):
+        for place in places:
+            start = tok_op.seat.index(*place) * ROWS
+
+            @pl.loop(0, ROWS // 32)
+            def _(k):
+                at = pl.ds(pl.multiple_of(start + k * 32, 32), 32)
+                values = tok[at, :].astype(f32)
+                hidden[at, :] = (values * inverse_rms(values) * gain).astype(bf16)
+
+            at = pl.ds(pl.multiple_of(start, ROWS), ROWS)
+            qc[at, :] = nn(hidden[at, :], weights[:, :CORE_W])
+
+    project((0, 0), (0, -1), (0, 1), (1, 0), (0, 2))
+    tok_op.step(4)
+    piece_op.step(5)
+    gate_up_op.step(0)
+    out_op.step(1)
+    out_op.step(2)
+    cot_op.step(0)
+    project((1, -1), (1, 1), (1, 2))
+    tok_op.step(5, shared=False)
+    for k in (0, 2, 3):
+        saves[k].start()
 
     @pl.loop(0, SEQ // 256)
     def _(k):
         at = pl.ds(pl.multiple_of(k * 256, 256), 256)
-        qc[at, :] = nn(hidden[at, :], weights[:, :CORE_W])
-
-    saves[3].start()
-    cot_op.step(2)
-
-    @pl.loop(0, SEQ // 128)
-    def _(k):
-        at = pl.ds(pl.multiple_of(k * 128, 128), 128)
         inner = qc[at, QW : QW + RANK]
         latent[at, :] = (inner * inverse_rms(inner) * kv_gain).astype(bf16)
         ropes, key_rope = qc[at, 2 * NOPE : QW], qc[at, MISC_AT:CORE_W]
@@ -879,44 +995,43 @@
 
     for k in (4, 5, 6, 7):
         saves[k].start()
+    out_op.step(3)
+    gate_up_op.step(1)
+    gate_up_op.step(2)
     for h in range(HEADS_HERE):
         for i in range(SEQ // 256):
             at, seen = pl.ds(i * 256, 256), (i + 1) * 256
-            scores = nt(query[h, at, :], key[h, :seen, :]) * SCALE
-            row = lax.broadcasted_iota(jnp.int32, scores.shape, 0) + i * 256
-            column = lax.broadcasted_iota(jnp.int32, scores.shape, 1)
-            scores = jnp.where(column <= row, scores, -1e9)
+            scores = causal(nt(query[h, at, :], key[h, :seen, :]) * SCALE)
             top = jnp.max(scores, axis=1, keepdims=True)
             parts = jnp.exp(scores - top)
             total = jnp.sum(parts, axis=1, keepdims=True)
-            probs = (parts / total).astype(bf16)
+            probs = (parts * (1.0 / total)).astype(bf16)
             heads[at, h * VDIM : (h + 1) * VDIM] = nn(probs, value[h, :seen, :]).astype(bf16)
             totals[h, at, :] = jnp.broadcast_to(top + jnp.log(total), (256, ROWS))
-
+        if h == 0:
+            out_op.step(4)
+            cot_op.step(1)
+            cot_op.step(2)
+    head_op.step(0)
     saves[8].start()
     saves[11].start()
+    gate_up_op.step(3)
     out_op.step(5)
     saves[9].start()
-
-    @pl.loop(0, D // TILE)
-    def _(n):
-        at = pl.ds(pl.multiple_of(n * TILE, TILE), TILE)
-        sums[:, at] = nn(heads[...], out_w[:, at]).astype(bf16)
-
-    sum_op.step(0)
     cot_op.step(3)
-    sum_op.step(1)
-    sum_op.step(2)
+    gate_up_op.step(4)
+    head_op.step(5)
+    own = tok_op.view((0, 0))[...].astype(f32)
+    resid = own + nn(tok_heads[...], out_w[...])
+    resid_two[...] = resid
+    hidden_two[...] = (resid * inverse_rms(resid) * misc_t[GAIN_TWO : GAIN_TWO + 1, :]).astype(bf16)
     cot_op.step(4)
-    sum_op.step(3)
-    sum_op.step(4)
-    wait_all(saves)
-    sum_op.step(5)
+    wait_all(saves + [down_save])
     cot_op.step(5)
-    piece_op.step(5)
-
-
-def attention(tokens, pack, cotangent, pieces, cosine, sine):
+    gate_up_op.step(5)
+
+
+def attention(*arrays):
     any_spec, vmem = pl.BlockSpec(memory_space=pl.ANY), pl.BlockSpec(memory_space=pltpu.VMEM)
     kept = [
         ((SEQ, D), bf16),
@@ -928,20 +1043,22 @@
         ((HEADS_HERE, SEQ, 2 * NOPE), bf16),
         ((HEADS_HERE, SEQ, VDIM), bf16),
         ((SEQ, OW), bf16),
-        ((OW, D), bf16),
+        ((D, D), bf16),
         ((ROWS, D), f32),
         ((HEADS_HERE, SEQ, ROWS), f32),
     ]
-    made = [((ROWS, D), f32), ((GROUP, D), bf16), ((2 * HALF, D), bf16)]
-    scratch = kept[:3] + [((SEQ, CORE_W), f32), kept[4], ((RANK, KVW), bf16)] + kept[5:] + [((SEQ, D), bf16)]
+    made = [((ROWS, D), f32), ((ROWS, D), bf16), ((GROUP, D), bf16), ((RELAY, D), bf16), ((SP * RELAY, D), bf16), ((FULL, D), bf16)]
+    scratch = kept[:3] + [((SEQ, CORE_W), f32), kept[4], ((RANK, KVW), bf16)] + kept[5:]
+    scratch = scratch + [((ROWS, D), bf16), ((DP, RELAY, ROWS), bf16), ((FULL, D), bf16)]
+    scratch = scratch + [(array.shape, bf16) for array in arrays[3:9]]
     return pl.pallas_call(
         attention_kernel,
         name="attention",
         out_shape=[jax.ShapeDtypeStruct(*shape) for shape in made + kept],
-        in_specs=[any_spec] * 4 + [vmem] * 2,
-        out_specs=[vmem] + [any_spec] * (len(made) + len(kept) - 1),
+        in_specs=[any_spec] * 10 + [vmem] * 2,
+        out_specs=[vmem] * 2 + [any_spec] * (len(made) + len(kept) - 2),
         scratch_shapes=[pltpu.VMEM(*shape) for shape in scratch]
-        + [pltpu.SemaphoreType.DMA((len(kept),))]
+        + [pltpu.SemaphoreType.DMA((len(kept),)), pltpu.SemaphoreType.DMA((6,))]
         + [entry for op in attention_ops() for entry in op.scratch()],
         compiler_params=pltpu.CompilerParams(
             collective_id=0, has_side_effects=True, vmem_limit_bytes=60 * 2**20
@@ -949,7 +1066,312 @@
         cost_estimate=pl.CostEstimate(
             flops=2 * SEQ * D * (CORE_W + OW), bytes_accessed=60 * 2**20, transcendentals=SEQ * SEQ
         ),
-    )(tokens, pack, cotangent, pieces, cosine, sine)
+    )(*arrays)
+
+
+def attention_grad_ops():
+    return (
+        Gather("sp", ROWS, D, spare=True),
+        Scatter("sp", GU_PART, D, bf16),
+        Scatter("sp", DN_PART, D, bf16),
+        Swap(
+            "sp",
+            (D, GRAD_PACK),
+            lambda ref, j: ref.at[:, pl.ds(pl.multiple_of(j * OW, OW), OW)],
+            lambda ref, j: ref.at[pl.ds(pl.multiple_of(j * OW, OW), OW), pl.ds(CORE_W, OW)],
+        ),
+        Swap(
+            "sp",
+            (SEQ, OW),
+            lambda ref, j: ref.at[:, pl.ds(pl.multiple_of(j * OW, OW), OW)],
+            lambda ref, j: ref.at[pl.ds(pl.multiple_of(j * ROWS, ROWS), ROWS)],
+        ),
+    )
+
+
+def attention_grad_kernel(
+    proj_own,
+    tok_all,
+    weights_all,
+    hidden_all,
+    compressed_all,
+    latent_all,
+    query_all,
+    key_all,
+    value_all,
+    head_all,
+    head_tok,
+    misc_all,
+    total_all,
+    gate_up_all,
+    down_all,
+    cosine,
+    sine,
+    norm_rows,
+    hidden_part,
+    gate_up_sum,
+    down_sum,
+    grads,
+    proj,
+    weights,
+    hidden,
+    compressed,
+    latent,
+    query,
+    key,
+    value,
+    heads,
+    misc_t,
+    totals,
+    gate_up_grad,
+    down_grad,
+    up_w,
+    out_w_grad,
+    head_grad,
+    key_grad,
+    value_grad,
+    rope_grad,
+    expanded_grad,
+    qc_grad,
+    scale_one,
+    misc_grad,
+    up_grad,
+    made_w,
+    made_h,
+    load_sem,
+    out_sem,
+    *rest,
+):
+    ops = attention_grad_ops()
+    proj_op, gate_up_op, down_op, out_op, head_op = ops
+    bound = (
+        (proj_own, proj),
+        (gate_up_grad, gate_up_sum),
+        (down_grad, down_sum),
+        (out_w_grad, grads),
+        (head_tok, head_grad),
+    )
+    for op, (src, dst) in zip(ops, bound):
+        count = len(op.scratch())
+        op.bind(src, dst, rest[:count])
+        rest = rest[count:]
+    loads = [
+        pltpu.make_async_copy(src, dst, load_sem.at[k])
+        for k, (src, dst) in enumerate(
+            (
+                (head_all, heads),
+                (query_all, query),
+                (key_all, key),
+                (value_all, value),
+                (total_all, totals),
+                (gate_up_all, gate_up_grad),
+                (down_all, down_grad),
+                (weights_all, weights),
+                (compressed_all, compressed),
+                (latent_all, latent),
+                (misc_all, misc_t),
+                (hidden_all, hidden),
+            )
+        )
+    ]
+    tok_load = pltpu.make_async_copy(tok_all, proj, load_sem.at[12])
+    for load in loads:
+        load.start()
+    meet(ops)
+    head_op.step(0)
+    proj_op.step(0)
+    wait_all(loads)
+    up = weights[:, UP_AT:].reshape(DP, 4, RANK // DP, ROWS)
+    for k in range(4):
+        up_w[:, k * ROWS : (k + 1) * ROWS] = up[:, k].reshape(RANK, ROWS)
+    head_op.step(5)
+    for h in range(HEADS_HERE):
+        for i in reversed(range(SEQ // 256)):
+            at, seen = pl.ds(i * 256, 256), (i + 1) * 256
+            piece = head_grad[at, h * VDIM : (h + 1) * VDIM]
+            scores = causal(nt(query[h, at, :], key[h, :seen, :]) * SCALE)
+            probs = jnp.exp(scores - totals[h, at, 0:1])
+            dprob = nt(piece, value[h, :seen, :])
+            delta = jnp.sum(probs * dprob, axis=1, keepdims=True)
+            score_grad = (probs * (dprob - delta) * SCALE).astype(bf16)
+            query_grad = nn(score_grad, key[h, :seen, :]).astype(bf16)
+            qc_grad[at, h * NOPE : (h + 1) * NOPE] = query_grad[:, :NOPE]
+            turned = query_grad[:, NOPE:].astype(f32)
+            rope_grad[at, :] = turned if h == 0 else rope_grad[at, :] + turned
+            from_query = tn(score_grad, query[h, at, :])
+            from_out = tn(probs.astype(bf16), piece)
+            if i == SEQ // 256 - 1:
+                key_grad[h, :seen, :] = from_query
+                value_grad[h, :seen, :] = from_out
+            else:
+                key_grad[h, :seen, :] += from_query
+                value_grad[h, :seen, :] += from_out
+            if (h, i) == (0, 2):
+                proj_op.step(1)
+                proj_op.step(2)
+        if h == 0:
+            proj_op.step(3)
+            gate_up_op.step(0)
+            down_op.step(0)
+    proj_op.step(4)
+    proj_op.step(5)
+    out_w_grad[...] = tn(heads[...], proj[...]).astype(bf16)
+    out_op.step(0)
+    tok_load.start()
+    gate_up_op.step(1)
+    down_op.step(1)
+    kv_gain = misc_t[0:1, :RANK]
+    lane = lax.broadcasted_iota(jnp.int32, (128, ROWS), 1)
+
+    @pl.loop(0, SEQ // 128)
+    def _(k):
+        at = pl.ds(pl.multiple_of(k * 128, 128), 128)
+        cos, sin = cosine[at, :], sine[at, :]
+        ropes = rope_grad[at, :]
+        qc_grad[at, 2 * NOPE : QW] = (ropes * cos - swap_halves(ropes) * sin).astype(bf16)
+        key_rope = jnp.zeros((128, ROWS), f32)
+        for h in range(HEADS_HERE):
+            base = h * (NOPE + VDIM)
+            expanded_grad[at, base : base + NOPE] = key_grad[h, at, :NOPE].astype(bf16)
+            expanded_grad[at, base + NOPE : base + NOPE + VDIM] = value_grad[h, at, :].astype(bf16)
+            turned = key_grad[h, at, NOPE:].astype(bf16).astype(f32)
+            turned = turned if h == 0 else pltpu.roll(turned, ROPE, 1)
+            key_rope = key_rope + jnp.where(lane < ROPE, turned, 0.0)
+        key_rope = key_rope * cos - swap_halves(key_rope) * sin
+        qc_grad[at, MISC_AT:CORE_W] = jnp.where(lane < ROPE, key_rope, 0.0).astype(bf16)
+
+    gate_up_op.step(2)
+    down_op.step(2)
+    made = tn(latent[...], expanded_grad[...]).astype(bf16)
+    each = RANK // DP
+    for d in range(DP):
+        for k in range(4):
+            at = pl.ds(d * ROWS + k * each, each)
+            up_grad[at, :] = made[d * each : (d + 1) * each, k * ROWS : (k + 1) * ROWS]
+    up_store = pltpu.make_async_copy(up_grad, grads.at[:, pl.ds(GRAD_UP_AT, ROWS)], out_sem.at[2])
+    up_store.start()
+    misc_grad[...] = jnp.zeros_like(misc_grad)
+    misc_grad[64:72, :] = norm_rows[...]
+    kv_total = jnp.zeros((1, RANK), f32)
+    for k in range(SEQ // 256):
+        at = pl.ds(k * 256, 256)
+        inner = compressed[at, :]
+        scale = inverse_rms(inner)
+        latent_grad = nt(expanded_grad[at, :], up_w[...])
+        kv_total = kv_total + jnp.sum(latent_grad * inner * scale, axis=0, keepdims=True)
+        qc_grad[at, QW : QW + RANK] = norm_back(inner, scale, kv_gain, latent_grad).astype(bf16)
+    for d in range(DP):
+        misc_grad[66:67, d * ROWS : d * ROWS + each] = kv_total[:, d * each : (d + 1) * each]
+    tok_load.wait()
+
+    @pl.loop(0, SEQ // 32)
+    def _(k):
+        at = pl.ds(pl.multiple_of(k * 32, 32), 32)
+        scale_one[at, :] = inverse_rms(proj[at, :].astype(f32))
+
+    def put(n):
+        at = pl.ds(pl.multiple_of(n * TILE, TILE), TILE)
+        return pltpu.make_async_copy(made_h.at[n % 2], hidden_part.at[:, at], out_sem.at[n % 2])
+
+    @pl.loop(0, D // TILE)
+    def _(n):
+        at = pl.ds(pl.multiple_of(n * TILE, TILE), TILE)
+
+        @pl.when(n >= 2)
+        def _():
+            put(n - 2).wait()
+
+        grad = nt(qc_grad[...], weights[at, :CORE_W])
+        made_h[n % 2] = grad.astype(bf16)
+        put(n).start()
+        grad = grad * proj[:, at].astype(f32) * scale_one[...]
+        misc_grad[64:65, at] = jnp.sum(grad, axis=0, keepdims=True)
+
+    put(2).wait()
+    put(3).wait()
+    gate_up_op.step(3)
+    down_op.step(3)
+
+    def store(n):
+        at = pl.ds(pl.multiple_of(n * TILE, TILE), TILE)
+        return pltpu.make_async_copy(
+            made_w.at[n % 2], grads.at[at, pl.ds(0, CORE_W)], out_sem.at[n % 2]
+        )
+
+    @pl.loop(0, D // TILE)
+    def _(n):
+        at = pl.ds(pl.multiple_of(n * TILE, TILE), TILE)
+
+        @pl.when(n >= 2)
+        def _():
+            store(n - 2).wait()
+
+        made = tn(hidden[:, at], qc_grad[...])
+        made_w[n % 2, :, :MISC_AT] = made[:, :MISC_AT].astype(bf16)
+        made_w[n % 2, :, MISC_AT:] = (made[:, MISC_AT:] + misc_grad[:, at].T).astype(bf16)
+        store(n).start()
+
+    store(2).wait()
+    store(3).wait()
+    up_store.wait()
+    gate_up_op.step(4)
+    down_op.step(4)
+    out_op.step(5)
+    gate_up_op.step(5)
+    down_op.step(5)
+
+
+def attention_grad(*arrays):
+    any_spec, vmem = pl.BlockSpec(memory_space=pl.ANY), pl.BlockSpec(memory_space=pltpu.VMEM)
+    scratch = [
+        ((SEQ, D), bf16),
+        ((D, PACK), bf16),
+        ((SEQ, D), bf16),
+        ((SEQ, RANK), f32),
+        ((SEQ, RANK), bf16),
+        ((HEADS_HERE, SEQ, 2 * NOPE), bf16),
+        ((HEADS_HERE, SEQ, 2 * NOPE), bf16),
+        ((HEADS_HERE, SEQ, VDIM), bf16),
+        ((SEQ, OW), bf16),
+        ((ROWS, D), f32),
+        ((HEADS_HERE, SEQ, ROWS), f32),
+        ((2 * HALF, D), bf16),
+        ((FULL, D), bf16),
+        ((RANK, KVW), bf16),
+        ((OW, D), bf16),
+        ((SEQ, OW), bf16),
+        ((HEADS_HERE, SEQ, 2 * NOPE), f32),
+        ((HEADS_HERE, SEQ, VDIM), f32),
+        ((SEQ, ROWS), f32),
+        ((SEQ, KVW), bf16),
+        ((SEQ, CORE_W), bf16),
+        ((SEQ, 1), f32),
+        ((ROWS, D), f32),
+        ((D, ROWS), bf16),
+        ((2, TILE, CORE_W), bf16),
+        ((2, SEQ, TILE), bf16),
+    ]
+    return pl.pallas_call(
+        attention_grad_kernel,
+        name="attention_grad",
+        out_shape=[
+            jax.ShapeDtypeStruct((SEQ, D), bf16),
+            jax.ShapeDtypeStruct((GU_PART, D), bf16),
+            jax.ShapeDtypeStruct((DN_PART, D), bf16),
+            jax.ShapeDtypeStruct((D, GRAD_PACK), bf16),
+        ],
+        in_specs=[any_spec] * 15 + [vmem] * 3,
+        out_specs=[any_spec, vmem, vmem, any_spec],
+        scratch_shapes=[pltpu.VMEM(*shape) for shape in scratch]
+        + [pltpu.SemaphoreType.DMA((13,)), pltpu.SemaphoreType.DMA((3,))]
+        + [entry for op in attention_grad_ops() for entry in op.scratch()],
+        compiler_params=pltpu.CompilerParams(
+            collective_id=4, has_side_effects=True, vmem_limit_bytes=61 * 2**20
+        ),
+        cost_estimate=pl.CostEstimate(
+            flops=6 * SEQ * D * CORE_W, bytes_accessed=60 * 2**20, transcendentals=SEQ * SEQ
+        ),
+    )(*arrays)
 
 
 def per_device(
@@ -989,31 +1411,18 @@
             jnp.zeros((ROWS, 9), bf16),
             w_router,
             jnp.zeros((ROWS, 44), bf16),
-            lax.dynamic_slice_in_dim(w_out, own_sp * OW, OW, 1),
             own_up.reshape(RANK // DP, 4, ROWS).transpose(1, 0, 2).reshape(ROWS, ROWS),
         ],
         axis=1,
     )
-    gate_up = jnp.stack(
-        [
-            jnp.concatenate([shared_gate, expert_gate], axis=1),
-            jnp.concatenate([shared_up, expert_up], axis=1),
-        ]
-    )
-    gate_up = gate_up.reshape(2, ROWS, SETS, DP, SLICE).transpose(3, 0, 2, 4, 1)
-    gate_up = jnp.pad(gate_up, ((0, 0),) * 3 + ((0, ROOM - SLICE), (0, 0)))
-    gate_up = gate_up.reshape(DP, 2 * HALF, ROWS)
-    down = jnp.concatenate([shared_down, expert_down], axis=1).transpose(1, 0, 2)
-    down = jnp.pad(down, ((0, 0), (0, ROOM - SLICE), (0, 0))).reshape(HALF, D)
-    down = jnp.pad(down, ((0, FULL - HALF), (0, 0)))
-
-    cosine, sine = rope_tables(jnp.arange(SEQ, dtype=f32))
-    cosine = jnp.concatenate([cosine] * 4, axis=1)
-    sine = jnp.concatenate([-sine, sine] * 2, axis=1)
+    cosine, sine = rope_tables()
     (
-        attn_proj,
+        resid_two,
+        hidden_two,
         cot_all,
+        _,
         gate_up,
+        down,
         tok_all,
         weights,
         hidden_one,
@@ -1026,15 +1435,26 @@
         out_w,
         misc,
         log_totals,
-    ) = attention(tokens, pack, cotangent, gate_up, cosine, sine)
+    ) = attention(
+        tokens,
+        pack,
+        cotangent,
+        shared_gate,
+        expert_gate,
+        shared_up,
+        expert_up,
+        shared_down,
+        expert_down,
+        w_out,
+        cosine,
+        sine,
+    )
     gain_one, gain_two = misc[GAIN_ONE], misc[GAIN_TWO]
     latent_gain = misc[GAIN_KV].reshape(DP, ROWS)[:, : RANK // DP].reshape(RANK)
     router_t = misc[ROUTER_LANE : ROUTER_LANE + 16].astype(bf16)
     router_w = router_t[:EXPERTS]
     picks_all = weights[:, MISC_AT:CORE_W]
-    resid_two = tokens.astype(f32) + attn_proj
     scale_two = inverse_rms(resid_two)
-    hidden_two = (resid_two * scale_two * gain_two).astype(bf16)
 
     hidden_grad, mixed_part, gate_up_grad, down_grad = experts(
         hidden_two, gate_up, router_t, down, cot_all, picks_all
@@ -1049,102 +1469,48 @@
         router * (prob_grad - jnp.sum(router * prob_grad, axis=-1, keepdims=True))
     ).astype(bf16)
     hidden_grad = hidden_grad + nn(logit_grad, router_w)
-    router_grad = tn(hidden_two, logit_grad)
+    router_grad = tn(logit_grad, hidden_two)
     gain_two_grad = jnp.sum(hidden_grad * resid_two * scale_two, axis=0)
     upstream = cotangent.astype(f32)
     resid_two_grad = upstream + norm_back(resid_two, scale_two, gain_two, hidden_grad)
     proj_grad = resid_two_grad.astype(bf16)
 
-    proj_grad_all, mixed, gate_up_grad, down_grad = exchange(
-        "gather_projection_grad",
-        4,
+    head_tok_grad = nt(proj_grad, out_w).astype(bf16)
+    norm_rows = jnp.concatenate(
         [
-            Gather("sp", ROWS, D, spare=True),
-            Scatter("dp", ROWS, D),
-            Scatter("sp", GU_PART, D, bf16),
-            Scatter("sp", DN_PART, D, bf16),
-        ],
-        [proj_grad, mixed_part, gate_up_grad, down_grad],
+            jnp.zeros((1, D), f32),
+            gain_two_grad[None],
+            jnp.zeros((1, D), f32),
+            router_grad,
+            jnp.zeros((1, D), f32),
+        ]
     )
-    mixed = (resid_two + mixed).astype(bf16)
-    out_w_grad = tn(head_out, proj_grad_all)
-    head_grad = nt(proj_grad_all, out_w).astype(bf16)
-    rows = jnp.arange(SEQ, dtype=jnp.int32)
-    allowed = rows[None, :] <= rows[:, None]
-    low = jnp.arange(ROWS) < ROPE
-    rope_grad, nope_grads, expanded_grads, key_rope_grad = 0.0, [], [], 0.0
-    for h in range(HEADS_HERE):
-        piece = head_grad[:, h * VDIM : (h + 1) * VDIM]
-        prob = jnp.exp(jnp.where(allowed, nt(queries[h], keys[h]) * SCALE, -1e9) - log_totals[h, :, :1])
-        dprob = nt(piece, values[h])
-        delta = jnp.sum(prob * dprob, axis=-1, keepdims=True)
-        score_grad = (prob * (dprob - delta) * SCALE).astype(bf16)
-        query_grad = nn(score_grad, keys[h]).astype(bf16)
-        key_grad = tn(score_grad, queries[h]).astype(bf16)
-        value_grad = tn(prob.astype(bf16), piece).astype(bf16)
-        nope_grads.append(query_grad[:, :NOPE])
-        rope_grad = rope_grad + query_grad[:, NOPE:].astype(f32)
-        expanded_grads += [key_grad[:, :NOPE], value_grad]
-        own = key_grad[:, NOPE + h * ROPE : NOPE + (h + 1) * ROPE].astype(f32)
-        key_rope_grad = key_rope_grad + own
-
-    def unrotate(values, cos, sin):
-        flipped = values.reshape(SEQ, -1, 2, ROPE // 2)[:, :, ::-1].reshape(values.shape)
-        return values * cos - flipped * sin
-
-    rope_grad = unrotate(rope_grad, cosine, sine).astype(bf16)
-    key_rope_grad = unrotate(key_rope_grad, cosine[:, :ROPE], sine[:, :ROPE]).astype(bf16)
-    expanded_grad = jnp.concatenate(expanded_grads, axis=1)
-    up_w = weights[:, UP_AT:].reshape(DP, 4, RANK // DP, ROWS).transpose(0, 2, 1, 3).reshape(RANK, KVW)
-    up_w_grad = tn(latent, expanded_grad)
-    latent_grad = nt(expanded_grad, up_w)
-    scale_latent = inverse_rms(compressed)
-    latent_in_grad = norm_back(compressed, scale_latent, latent_gain, latent_grad)
-    latent_gain_grad = jnp.sum(latent_grad * compressed * scale_latent, axis=0)
-    qc_grad = jnp.concatenate(
-        nope_grads
-        + [rope_grad, latent_in_grad.astype(bf16), key_rope_grad, jnp.zeros((SEQ, ROPE), bf16)],
-        axis=1,
+    hidden_one_grad, gate_up_grad, down_grad, grads = attention_grad(
+        proj_grad,
+        tok_all,
+        weights,
+        hidden_one,
+        compressed,
+        latent,
+        queries,
+        keys,
+        values,
+        head_out,
+        head_tok_grad,
+        misc,
+        log_totals,
+        gate_up_grad,
+        down_grad,
+        cosine,
+        sine,
+        norm_rows,
     )
-    qc_w_grad = tn(hidden_one, qc_grad)
-    hidden_one_grad = nt(qc_grad, weights[:, :CORE_W])
-    resid_all = tok_all.astype(f32)
-    gain_one_grad = jnp.sum(hidden_one_grad * resid_all * inverse_rms(resid_all), axis=0)
-
-    (out_cols_grad,) = exchange(
-        "swap_projection_weight_grad",
-        5,
-        [
-            Swap(
-                "sp",
-                (D, OW),
-                lambda ref, j: ref.at[:, pl.ds(pl.multiple_of(j * OW, OW), OW)],
-                lambda ref, j: ref.at[pl.ds(pl.multiple_of(j * OW, OW), OW)],
-            )
-        ],
-        [out_w_grad.astype(bf16)],
-    )
-    latent_gain_grad = jnp.pad(
-        latent_gain_grad.reshape(DP, RANK // DP), ((0, 0), (0, ROWS - RANK // DP))
-    ).reshape(D)
-    grads = jnp.concatenate(
-        [
-            qc_w_grad[:, : QW + RANK + ROPE].astype(bf16),
-            gain_one_grad.astype(bf16)[:, None],
-            gain_two_grad.astype(bf16)[:, None],
-            latent_gain_grad.astype(bf16)[:, None],
-            router_grad.astype(bf16),
-            jnp.zeros((D, ROPE - 7), bf16),
-            out_cols_grad,
-            up_w_grad.astype(bf16).reshape(D, ROWS),
-        ],
-        axis=1,
-    )
-    grads, hidden_one_grad, _, gu_total, dn_total = exchange(
+
+    _, hidden_one_grad, _, gu_total, dn_total, mixed, grads = exchange(
         "sum_grads",
         6,
         [
-            Scatter("dp", ROWS, PACK, bf16),
+            Scatter("dp", ROWS, GRAD_PACK, bf16, spare=True),
             Scatter("sp", ROWS, D),
             Swap(
                 "dp",
@@ -1153,16 +1519,21 @@
                 lambda ref, j: ref.at[pl.ds(pl.multiple_of(j * GU_PART, GU_PART), GU_PART)],
             ),
             Gather("sp", DP * GU_PART, ROWS),
-            Gather("sp", DN_PART, D),
+            Gather("sp", DN_PART, D, spare=True),
+            Scatter("dp", ROWS, D, spare=True),
+            Gather("sp", ROWS, GRAD_PACK),
         ],
-        [grads, hidden_one_grad.astype(bf16), gate_up_grad, down_grad],
-        plan=[(2, 0), (0, 0), (1, 0), (4, 0), (2, 5), (3, 0)]
-        + [(op, step) for step in range(1, 6) for op in (1, 0, 4, 3)],
-        chained=[(3, 2)],
+        [grads, hidden_one_grad, gate_up_grad, down_grad, mixed_part],
+        plan=[(2, 0), (0, 0), (1, 0), (2, 5), (3, 0), (4, 0)]
+        + [(0, 1), (1, 1), (0, 2), (0, 3), (1, 2), (3, 1), (4, 1), (0, 4), (6, 0), (5, 0), (1, 3)]
+        + [(3, 2), (4, 2), (5, 1), (1, 4), (3, 3), (4, 3), (6, 1), (6, 2), (5, 2), (5, 3)]
+        + [(3, 4), (4, 4), (6, 3), (5, 4), (6, 4)]
+        + [(op, 5) for op in (0, 1, 3, 4, 5, 6)],
+        chained=[(3, 2), (6, 0)],
     )
-    (grads,) = exchange("gather_grads", 7, [Gather("sp", ROWS, PACK)], [grads])
     gu_total = gu_total.reshape(SP, DP, GU_PART, ROWS)
-    grads = grads.reshape(SP, ROWS, PACK)
+    grads = grads.reshape(SP, ROWS, GRAD_PACK)
+    mixed = (resid_two + mixed).astype(bf16)
     resid_one = tokens.astype(f32)
     own_scale = inverse_rms(resid_one)
     tokens_grad = resid_two_grad + norm_back(resid_one, own_scale, gain_one, hidden_one_grad)
@@ -1184,8 +1555,9 @@
     query_total = side_by_side(query_total, QW)
     tail = jnp.sum(grads[:, :, QW:CORE_W].astype(f32), axis=0)
     down_total, tail = tail[:, : RANK + ROPE], tail[:, RANK + ROPE :]
-    out_total = side_by_side(grads[:, :, CORE_W:UP_AT], OW)
-    up_total = side_by_side(grads[:, :, UP_AT:].reshape(SP, RANK // DP, KVW), KVW)
+    out_total = side_by_side(grads[:, :, CORE_W:GRAD_UP_AT], OW)
+    up_total = grads[:, :, GRAD_UP_AT:].reshape(SP, 4, RANK // DP, ROWS).transpose(0, 2, 1, 3)
+    up_total = side_by_side(up_total.reshape(SP, RANK // DP, KVW), KVW)
 
     gu_total = gu_total.transpose(0, 2, 1, 3).reshape(2, SETS, ROOM, DP, ROWS)[:, :, :SLICE]
     gu_total = gu_total.transpose(0, 4, 1, 3, 2).reshape(2, ROWS, SETS, FE).astype(f32)

time: 732 us -> 580 us (0.79)
  local copies, waits for them, and re-layouts: 102 us -> 55.1 us
  Pallas kernels: 532 us -> 492 us
  other arithmetic: 42.1 us -> 12 us
  matrix products: 40.2 us -> 10.5 us
    pallas_call x0 -> x1, Pallas kernels: none -> 114 us  [attention_grad(): pl.pallas_call(attention_grad_kernel, name='attention_grad', out_shape=[j...]
    pallas_call x4 -> x1, Pallas kernels: 236 us -> 130 us  [exchange(): pl.pallas_call(body, name=name, out_shape=[shape for shape, _ in outs], i...]
    pallas_call x1, Pallas kernels: 146 us -> 104 us  [experts(): pl.pallas_call(expert_kernel, name='experts', out_shape=[jax.ShapeDtypeSt...]
    dot_general x19 -> x4, matrix products: 40.2 us -> 10.5 us  [mm(): lax.dot_general(left, right, ((dims[0], dims[1]), ((), ())), preferred_el...]
    concatenate x2 -> x1, local copies, waits for them, and re-layouts: 14.6 us -> 0.69 us  [per_device(): jnp.concatenate([jnp.zeros((1, D), f32), gain_two_grad[None], jnp.zeros((...]
    unnamed x116 -> x31, local copies, waits for them, and re-layouts: 35.8 us -> 22.2 us
    convert_element_type x7 -> x0, other arithmetic: 10.4 us -> none  [the longest x1 3.11 us: per_device(): latent_in_grad.astype(bf16)]
where the time goes in v3:
time: 580 us; the launch traced here: 571 us
  Pallas kernels  492 us (85%)
  local copies, waits for them, and re-layouts  55.1 us (10%)
  other arithmetic  12 us (2%)
  matrix products  10.5 us (2%)
    pallas_call x1, Pallas kernels, attention(): pl.pallas_call(attention_kernel, name='attention', out_shape=[jax.ShapeDt...  144 us
    pallas_call x1, Pallas kernels, exchange(): pl.pallas_call(body, name=name, out_shape=[shape for shape, _ in outs], i...  130 us
    pallas_call x1, Pallas kernels, attention_grad(): pl.pallas_call(attention_grad_kernel, name='attention_grad', out_shape=[j...  114 us
    pallas_call x1, Pallas kernels, experts(): pl.pallas_call(expert_kernel, name='experts', out_shape=[jax.ShapeDtypeSt...  104 us
    unnamed x31, local copies, waits for them, and re-layouts  22.2 us

profile of v3, /device:TPU:1, one launch (start us, length us, event | category | flops | bytes accessed | tf_op | source)
XLA Modules:
  0.0 571.3 jit_solution(1089088380645771909)
XLA Ops:
  3.4 1.1 copy.126
  8.6 144.3 %attention.1 = (f32[128,2048]{1,0:T(8,128)}, bf16[128,2048]{1,0:T(8,128)(2,1)}, bf16[2048,2048]{1,0:T(8,128)(2,1)}, bf16[144,2048]{1,0:T(8,128)(2,1)}, bf16[1152...) custom-call(bf16[128,2048]{1,0:T(8,128)(2,1)} %tokens.1, ...), custom_call_target="tpu_custom_call" | custom-call | flops 5368709120 | bytes 62914560 | tf_op jit(solution)/shard_map/attention/pallas_call | solution.py:1054
  152.9 1.3 convert.15
  154.2 1.3 fusion.16
  156.5 1.9 slice.114.picks
  158.3 104.4 %experts.1 = (f32[128,2176]{1,0:T(8,128)}, bf16[2048,2048]{1,0:T(8,128)(2,1)}, bf16[1152,2048]{1,0:T(8,128)(2,1)}, bf16[640,2048]{1,0:T(8,128)(2,1)}) custom-call(bf16[128,2048]{1,0:T(8,128)(2,1)} %get-tuple-element.48.hidden_own, bf16[1152,2048]{1,0:T(8,128)(2,1)} %get-tuple-element.49.weights, bf16[16,2048]{1,0:T(8,128)(2,1)} %slice.140.router_t, ...), custom_call_target="tpu_custom_call" | custom-call | flops 48318382080 | bytes 41943040 | tf_op jit(solution)/shard_map/experts/pallas_call | solution.py:717
  262.9 1.0 multiply_reduce_fusion.3
  263.9 1.0 multiply_convert_fusion
  265.3 0.9 fusion.15
  266.3 1.7 multiply_reduce_fusion
  268.7 2.4 fusion.12
  271.1 7.2 %convolution_convert_fusion.head_tok = bf16[128,2048]{1,0:T(8,128)(2,1)} fusion(bf16[128,2048]{1,0:T(8,128)(2,1)S(1)} %get-tuple-element.162.proj_own, bf16[2048,2048]{1,0:T(8,128)(2,1)} %get-tuple-element.62), kind=kOutput, calls=%fused_computation.6 | convolution fusion | flops 1074003968 | bytes 9437184 | tf_op jit(solution)/shard_map/dot_general | solution.py:57
  278.4 113.7 %attention_grad.1 = (bf16[1024,2048]{1,0:T(8,128)(2,1)}, bf16[144,2048]{1,0:T(8,128)(2,1)}, bf16[80,2048]{1,0:T(8,128)(2,1)}, bf16[2048,1408]{1,0:T(8,128)(2,1)}) custom-call(bf16[128,2048]{1,0:T(8,128)(2,1)} %copy-done.8, bf16[1024,2048]{1,0:T(8,128)(2,1)} %get-tuple-element.54.tok_all, bf16[2048,1152]{1,0:T(8,128)(2,1)} %get-tuple-element.52.weights_all, ...), custom_call_target="tpu_custom_call" | custom-call | flops 12884901888 | bytes 62914560 | tf_op jit(solution)/shard_map/attention_grad/pallas_call | solution.py:1354
  392.1 129.8 %sum_grads.1 = (bf16[128,1408]{1,0:T(8,128)(2,1)}, f32[128,2048]{1,0:T(8,128)}, bf16[2304,128]{1,0:T(8,128)(2,1)}, bf16[18432,128]{1,0:T(8,128)(2,1)}, bf16[640,...) custom-call(bf16[2048,1408]{1,0:T(8,128)(2,1)} %get-tuple-element.66.refs_0_, ...), custom_call_target="tpu_custom_call" | custom-call | tf_op jit(solution)/shard_map/sum_grads/pallas_call | solution.py:485
  521.9 3.6 copy.138
  526.3 2.6 copy.139
  528.9 3.3 slice_bitcast_fusion
  532.2 1.9 copy-done.2
  534.1 4.7 copy.145
  538.8 4.7 copy.146
  543.4 3.1 slice_bitcast_fusion.2
  546.5 3.5 copy.143
  550.0 2.3 copy.144
  552.3 1.8 slice.134
  554.4 1.3 convert_bitcast_fusion.1
  555.7 2.4 slice.161
  558.1 1.7 slice.158
  561.2 1.3 copy.148
  562.9 1.1 copy.150
  564.1 1.1 copy.149
  565.2 1.1 fusion
  566.3 1.3 fusion.4
  (63 shorter events, 15.1 us)
Async XLA Ops:
  0.6 1.9 copy-start
  158.3 106.6 %copy-start.9 = (bf16[128,2048]{1,0:T(8,128)(2,1)S(1)}, bf16[128,2048]{1,0:T(8,128)(2,1)}, u32[]{:S(2)}) copy-start(bf16[128,2048]{1,0:T(8,128)(2,1)} %get-tuple-element.48.hidden_own) | copy-start | bytes 1572868
  158.3 106.8 %copy-start.3 = (f32[128,2048]{1,0:T(8,128)S(1)}, f32[128,2048]{1,0:T(8,128)}, u32[]{:S(2)}) copy-start(f32[128,2048]{1,0:T(8,128)} %get-tuple-element.46) | copy-start | bytes 3145732
  271.1 7.2 %copy-start.8 = (bf16[128,2048]{1,0:T(8,128)(2,1)}, bf16[128,2048]{1,0:T(8,128)(2,1)S(1)}, u32[]{:S(2)}) copy-start(bf16[128,2048]{1,0:T(8,128)(2,1)S(1)} %get-tuple-element.162.proj_own) | copy-start | bytes 1572868
  528.9 5.2 copy-start.2
  558.1 2.3 copy-start.6
  562.5 2.6 copy-start.5
  562.5 2.6 copy-start.7
  562.5 2.6 copy-start.10
  564.1 2.3 copy-start.4
  566.3 4.5 copy-start.1

commit v4 on v3

--- a/solution.py
+++ b/solution.py
@@ -32,7 +32,6 @@
 SLICE = FE // DP
 CORE_W = 1024
 UP_AT = CORE_W
-GRAD_UP_AT = CORE_W + OW
 MISC_AT = CORE_W - ROWS
 PICK_LANE, GAIN_ONE, GAIN_TWO, GAIN_KV, ROUTER_LANE = 64, 68, 69, 70, 80
 ROOM = 96
@@ -42,7 +41,6 @@
 TILE = 512
 SCALE = QK ** (-0.5)
 PACK = QW + RANK + ROPE + ROPE + ROWS
-GRAD_PACK = PACK + OW
 GU_PART = 2 * HALF // SP
 RELAY = 2 * HALF // SP
 UNITS = ROOM // SP
@@ -277,6 +275,10 @@
     go = Gather.go
     arrived = Gather.arrived
 
+    def sizes(self):
+        rows, cut = self.rows, middle(self.rows)
+        return [rows] * 3 + [cut, rows - cut] + [rows] * 3
+
     def bind(self, src, out, scratch):
         self.src, self.dst = src, out
         self.send_sem, self.recv_sem = scratch[:2]
@@ -290,7 +292,8 @@
         if self.axis == "dp":
             return self.made.at[ORDER.index(place)]
         kept = ((1, 0), (0, 1), (0, -1)) + (((1, 1), (1, -1)) if self.spare else ((0, 2),))
-        return self.made.at[kept.index(place)]
+        k = kept.index(place)
+        return self.made[k] if isinstance(self.made, list) else self.made.at[k]
 
     def part(self, place):
         return self.slot(place) if self.axis == "dp" else self.given(*place)
@@ -517,8 +520,8 @@
     picks,
     sum_out,
     mixed_out,
-    weights_grad,
-    down_grad,
+    gate_up_sum,
+    down_sum,
     hidden,
     gate_up,
     down_w,
@@ -534,16 +537,24 @@
     reached,
     spread,
     collect,
-    made_wide,
-    made_down,
+    running,
     load_sem,
     in_sem,
-    out_sem,
+    turn_sem,
+    gate_up_sems,
+    down_sems,
     *rest,
 ):
     gather, scatter = Gather("dp", ROWS, D), Scatter("dp", ROWS, D + ROWS)
     gather.bind(hidden_own, hidden, rest[:3])
     scatter.bind(sums, sum_out, rest[3:])
+    gate_up_op, down_op = Scatter("sp", GU_PART, D, bf16), Scatter("sp", DN_PART, D, bf16)
+    views, at = [], 0
+    for size in gate_up_op.sizes() + down_op.sizes() + [DN_PART] * 4:
+        views.append(hidden.at[pl.ds(at, size)])
+        at += size
+    gate_up_op.bind(gate_up, gate_up_sum, [gate_up_sems.at[0], gate_up_sems.at[1], *views[:8], running])
+    down_op.bind(down_w, down_sum, [down_sems.at[0], down_sems.at[1], *views[8:16], views[16:]])
     loads = [
         pltpu.make_async_copy(down, down_w, load_sem.at[2]),
         pltpu.make_async_copy(weights, sums.at[pl.ds(0, 2 * HALF), pl.ds(0, D)], load_sem.at[0]),
@@ -566,16 +577,9 @@
     def fetch_column(n):
         return pltpu.make_async_copy(cot_all.at[:, columns(n)], cot_column.at[n % 2], in_sem.at[2 + n % 2])
 
-    def stores(n):
-        k = n % 2
-        return (
-            pltpu.make_async_copy(made_wide.at[k], weights_grad.at[:, columns(n)], out_sem.at[k]),
-            pltpu.make_async_copy(made_down.at[k], down_grad.at[:, columns(n)], out_sem.at[2 + k]),
-        )
-
     fetch(0).start()
     fetch_column(0).start()
-    meet([gather])
+    meet([gather, gate_up_op])
     gather.step(0)
     gate_up[pl.ds(HALF, 16), :] = router_t[...]
     gate_up[pl.ds(HALF + 16, FULL - HALF - 16), :] = jnp.zeros((FULL - HALF - 16, D), bf16)
@@ -665,25 +669,22 @@
         sums[rows, D:] = nn(reached[...], collect[...]).astype(bf16)
         sums[rows, :D] = nn(wide[rows, :], gate_up[...]).astype(bf16)
 
-    def weight_grads(first, last):
+    def gate_up_grads(first, last):
+        @pl.loop(first, last)
+        def _(n):
+            made = tn(wide[...], hidden[:, columns(n)]).astype(bf16)
+            gate_up[:HALF, columns(n)] = made[:HALF]
+            gate_up[HALF : 2 * HALF, columns(n)] = made[FULL : FULL + HALF]
+
+    def down_grads(first, last):
         @pl.loop(first, last)
         def _(n):
             @pl.when(n < D // 256 - 1)
             def _():
                 fetch_column(n + 1).start()
 
-            @pl.when(n >= 2)
-            def _():
-                for store in stores(n - 2):
-                    store.wait()
-
-            made = tn(wide[...], hidden[:, columns(n)]).astype(bf16)
-            made_wide[n % 2, :HALF, :] = made[:HALF]
-            made_wide[n % 2, HALF:, :] = made[FULL : FULL + HALF]
             fetch_column(n).wait()
-            made_down[n % 2] = tn(acts[...], cot_column[n % 2]).astype(bf16)
-            for store in stores(n):
-                store.start()
+            down_w[:, columns(n)] = tn(acts[...], cot_column[n % 2]).astype(bf16)
 
     def outputs(first, last):
         @pl.loop(first, last)
@@ -696,17 +697,35 @@
             put(i).start()
 
     scatter.step(0)
-    outputs(0, 8)
+    gate_up_grads(0, 6)
     scatter.step(1)
+    gate_up_grads(6, 8)
+    gather.step(5, shared=False)
+    seat = gate_up_op.seat
+    for partner in gate_up_op.partners(seat):
+        pl.semaphore_signal(
+            turn_sem, inc=1, device_id=seat.device(partner), device_id_type=pl.DeviceIdType.MESH
+        )
     scatter.step(2)
-    weight_grads(0, 3)
+    outputs(0, 4)
     scatter.step(3)
-    weight_grads(3, 8)
+    pl.semaphore_wait(turn_sem, len(NEAR))
+    gate_up_op.step(0)
+    outputs(4, 8)
+    put(6).wait()
+    put(7).wait()
+    down_grads(0, 8)
+    down_op.step(0)
+    gate_up_op.step(1)
     scatter.step(4)
-    for i in (6, 7):
-        put(i).wait()
-        wait_all(stores(i))
-    gather.step(5, shared=False)
+    for step in (2, 3):
+        gate_up_op.step(step)
+        down_op.step(step - 1)
+    down_op.step(3)
+    gate_up_op.step(4)
+    down_op.step(4)
+    gate_up_op.step(5)
+    down_op.step(5)
     scatter.step(5)
 
 
@@ -720,11 +739,11 @@
         out_shape=[
             jax.ShapeDtypeStruct((ROWS, D + ROWS), f32),
             jax.ShapeDtypeStruct((GROUP, D), bf16),
-            jax.ShapeDtypeStruct((2 * HALF, D), bf16),
-            jax.ShapeDtypeStruct((FULL, D), bf16),
+            jax.ShapeDtypeStruct((GU_PART, D), bf16),
+            jax.ShapeDtypeStruct((DN_PART, D), bf16),
         ],
         in_specs=[any_spec, any_spec, vmem, any_spec, any_spec, vmem],
-        out_specs=[vmem, any_spec, any_spec, any_spec],
+        out_specs=[vmem, any_spec, vmem, vmem],
         scratch_shapes=[
             pltpu.VMEM((GROUP, D), bf16),
             pltpu.VMEM((2 * FULL, D), bf16),
@@ -741,11 +760,12 @@
             pltpu.VMEM((CHUNK, 2 * FULL), bf16),
             pltpu.VMEM((2 * ROWS, FULL), bf16),
             pltpu.VMEM((2 * FULL, ROWS), bf16),
-            pltpu.VMEM((2, 2 * HALF, 256), bf16),
-            pltpu.VMEM((2, FULL, 256), bf16),
+            pltpu.VMEM((4, GU_PART, D), bf16),
+            pltpu.SemaphoreType.DMA((3,)),
             pltpu.SemaphoreType.DMA((4,)),
-            pltpu.SemaphoreType.DMA((4,)),
-            pltpu.SemaphoreType.DMA((4,)),
+            pltpu.SemaphoreType.REGULAR,
+            pltpu.SemaphoreType.DMA((2, 17)),
+            pltpu.SemaphoreType.DMA((2, 17)),
         ]
         + gather.scratch()
         + scatter.scratch(),
@@ -836,11 +856,11 @@
     query,
     key,
     value,
-    heads,
+    tok_heads,
     out_w,
     misc_t,
     totals,
-    tok_heads,
+    heads,
     pieces,
     down,
     gate_shared,
@@ -886,6 +906,7 @@
     meet(ops)
     tok_op.step(0)
     pack_op.step(0)
+    out_op.step(0)
     for step in (1, 2):
         tok_op.step(step)
         pack_op.step(step)
@@ -902,19 +923,15 @@
             at = (k * SETS + e) * UNITS
             for d in range(DP):
                 pieces[d, at : at + UNITS, :] = piece[d * UNITS : (d + 1) * UNITS]
+        if k == 0:
+            tok_op.step(3)
+            pack_op.step(3)
+            out_op.step(1)
+            out_op.step(2)
     piece_op.step(0)
-    for e in range(SETS):
-        part = down_shared[:, e, :] if e < NS else down_routed[:, e - NS, :]
-        down[e * ROOM : e * ROOM + SLICE, :] = part
-        down[e * ROOM + SLICE : (e + 1) * ROOM, :] = jnp.zeros((ROOM - SLICE, D), bf16)
-    down[HALF:, :] = jnp.zeros((FULL - HALF, D), bf16)
-    down_save = pltpu.make_async_copy(down, down_out, load_sem.at[0])
-    down_save.start()
-    tok_op.step(3)
-    pack_op.step(3)
     pack_op.step(4)
     pack_op.step(5)
-    out_op.step(0)
+    cot_op.step(0)
     tok_op.local().wait()
     saves = [
         pltpu.make_async_copy(src, dst, save_sem.at[k])
@@ -928,7 +945,7 @@
                 (query, query_out),
                 (key, key_out),
                 (value, value_out),
-                (heads, head_out),
+                (tok_heads, head_out),
                 (out_w, out_w_out),
                 (misc_t, misc_out),
                 (totals, total_out),
@@ -964,9 +981,7 @@
     tok_op.step(4)
     piece_op.step(5)
     gate_up_op.step(0)
-    out_op.step(1)
-    out_op.step(2)
-    cot_op.step(0)
+    out_op.step(3)
     project((1, -1), (1, 1), (1, 2))
     tok_op.step(5, shared=False)
     for k in (0, 2, 3):
@@ -995,9 +1010,11 @@
 
     for k in (4, 5, 6, 7):
         saves[k].start()
-    out_op.step(3)
     gate_up_op.step(1)
     gate_up_op.step(2)
+    out_op.step(4)
+    cot_op.step(1)
+    cot_op.step(2)
     for h in range(HEADS_HERE):
         for i in range(SEQ // 256):
             at, seen = pl.ds(i * 256, 256), (i + 1) * 256
@@ -1009,18 +1026,22 @@
             heads[at, h * VDIM : (h + 1) * VDIM] = nn(probs, value[h, :seen, :]).astype(bf16)
             totals[h, at, :] = jnp.broadcast_to(top + jnp.log(total), (256, ROWS))
         if h == 0:
-            out_op.step(4)
-            cot_op.step(1)
-            cot_op.step(2)
+            gate_up_op.step(3)
     head_op.step(0)
-    saves[8].start()
     saves[11].start()
-    gate_up_op.step(3)
+    cot_op.step(3)
+    for e in range(SETS):
+        part = down_shared[:, e, :] if e < NS else down_routed[:, e - NS, :]
+        down[e * ROOM : e * ROOM + SLICE, :] = part
+        down[e * ROOM + SLICE : (e + 1) * ROOM, :] = jnp.zeros((ROOM - SLICE, D), bf16)
+    down[HALF:, :] = jnp.zeros((FULL - HALF, D), bf16)
+    down_save = pltpu.make_async_copy(down, down_out, load_sem.at[0])
+    down_save.start()
+    gate_up_op.step(4)
     out_op.step(5)
     saves[9].start()
-    cot_op.step(3)
-    gate_up_op.step(4)
     head_op.step(5)
+    saves[8].start()
     own = tok_op.view((0, 0))[...].astype(f32)
     resid = own + nn(tok_heads[...], out_w[...])
     resid_two[...] = resid
@@ -1042,14 +1063,14 @@
         ((HEADS_HERE, SEQ, 2 * NOPE), bf16),
         ((HEADS_HERE, SEQ, 2 * NOPE), bf16),
         ((HEADS_HERE, SEQ, VDIM), bf16),
-        ((SEQ, OW), bf16),
+        ((ROWS, D), bf16),
         ((D, D), bf16),
         ((ROWS, D), f32),
         ((HEADS_HERE, SEQ, ROWS), f32),
     ]
     made = [((ROWS, D), f32), ((ROWS, D), bf16), ((GROUP, D), bf16), ((RELAY, D), bf16), ((SP * RELAY, D), bf16), ((FULL, D), bf16)]
     scratch = kept[:3] + [((SEQ, CORE_W), f32), kept[4], ((RANK, KVW), bf16)] + kept[5:]
-    scratch = scratch + [((ROWS, D), bf16), ((DP, RELAY, ROWS), bf16), ((FULL, D), bf16)]
+    scratch = scratch + [((SEQ, OW), bf16), ((DP, RELAY, ROWS), bf16), ((FULL, D), bf16)]
     scratch = scratch + [(array.shape, bf16) for array in arrays[3:9]]
     return pl.pallas_call(
         attention_kernel,
@@ -1071,14 +1092,20 @@
 
 def attention_grad_ops():
     return (
-        Gather("sp", ROWS, D, spare=True),
-        Scatter("sp", GU_PART, D, bf16),
-        Scatter("sp", DN_PART, D, bf16),
+        Gather("dp", ROWS, D, spare=True),
         Swap(
-            "sp",
-            (D, GRAD_PACK),
-            lambda ref, j: ref.at[:, pl.ds(pl.multiple_of(j * OW, OW), OW)],
-            lambda ref, j: ref.at[pl.ds(pl.multiple_of(j * OW, OW), OW), pl.ds(CORE_W, OW)],
+            "dp",
+            (DP * GU_PART, ROWS),
+            lambda ref, j: ref.at[:, pl.ds(pl.multiple_of(j * ROWS, ROWS), ROWS)],
+            lambda ref, j: ref.at[pl.ds(pl.multiple_of(j * GU_PART, GU_PART), GU_PART)],
+        ),
+        Gather("sp", DP * GU_PART, ROWS),
+        Gather("sp", DN_PART, D),
+        Swap(
+            "dp",
+            (GROUP, ROWS),
+            lambda ref, j: ref.at[:, pl.ds(pl.multiple_of(j * ROWS, ROWS), ROWS)],
+            lambda ref, j: ref.at[pl.ds(pl.multiple_of(j * ROWS, ROWS), ROWS)],
         ),
         Swap(
             "sp",
@@ -1103,16 +1130,19 @@
     head_tok,
     misc_all,
     total_all,
-    gate_up_all,
-    down_all,
+    gate_up_sum,
+    down_sum,
     cosine,
     sine,
     norm_rows,
     hidden_part,
-    gate_up_sum,
-    down_sum,
+    gate_up_piece,
+    gate_up_total,
+    down_total,
     grads,
-    proj,
+    proj_all,
+    out_grad,
+    tok,
     weights,
     hidden,
     compressed,
@@ -1120,13 +1150,10 @@
     query,
     key,
     value,
-    heads,
+    head_cols,
     misc_t,
     totals,
-    gate_up_grad,
-    down_grad,
     up_w,
-    out_w_grad,
     head_grad,
     key_grad,
     value_grad,
@@ -1143,12 +1170,13 @@
     *rest,
 ):
     ops = attention_grad_ops()
-    proj_op, gate_up_op, down_op, out_op, head_op = ops
+    proj_op, piece_op, gate_up_op, down_op, out_op, head_op = ops
     bound = (
-        (proj_own, proj),
-        (gate_up_grad, gate_up_sum),
-        (down_grad, down_sum),
-        (out_w_grad, grads),
+        (proj_own, proj_all),
+        (gate_up_sum, gate_up_piece),
+        (gate_up_piece, gate_up_total),
+        (down_sum, down_total),
+        (head_all, head_cols),
         (head_tok, head_grad),
     )
     for op, (src, dst) in zip(ops, bound):
@@ -1159,13 +1187,11 @@
         pltpu.make_async_copy(src, dst, load_sem.at[k])
         for k, (src, dst) in enumerate(
             (
-                (head_all, heads),
+                (tok_all, tok),
                 (query_all, query),
                 (key_all, key),
                 (value_all, value),
                 (total_all, totals),
-                (gate_up_all, gate_up_grad),
-                (down_all, down_grad),
                 (weights_all, weights),
                 (compressed_all, compressed),
                 (latent_all, latent),
@@ -1174,17 +1200,27 @@
             )
         )
     ]
-    tok_load = pltpu.make_async_copy(tok_all, proj, load_sem.at[12])
     for load in loads:
         load.start()
     meet(ops)
     head_op.step(0)
+    piece_op.step(0)
+    down_op.step(0)
     proj_op.step(0)
+    out_op.step(0)
     wait_all(loads)
+
+    @pl.loop(0, SEQ // 32)
+    def _(k):
+        at = pl.ds(pl.multiple_of(k * 32, 32), 32)
+        scale_one[at, :] = inverse_rms(tok[at, :].astype(f32))
+
     up = weights[:, UP_AT:].reshape(DP, 4, RANK // DP, ROWS)
     for k in range(4):
         up_w[:, k * ROWS : (k + 1) * ROWS] = up[:, k].reshape(RANK, ROWS)
     head_op.step(5)
+    piece_op.step(5)
+    gate_up_op.step(0)
     for h in range(HEADS_HERE):
         for i in reversed(range(SEQ // 256)):
             at, seen = pl.ds(i * 256, 256), (i + 1) * 256
@@ -1206,20 +1242,15 @@
             else:
                 key_grad[h, :seen, :] += from_query
                 value_grad[h, :seen, :] += from_out
-            if (h, i) == (0, 2):
-                proj_op.step(1)
-                proj_op.step(2)
         if h == 0:
-            proj_op.step(3)
-            gate_up_op.step(0)
-            down_op.step(0)
-    proj_op.step(4)
-    proj_op.step(5)
-    out_w_grad[...] = tn(heads[...], proj[...]).astype(bf16)
-    out_op.step(0)
-    tok_load.start()
+            down_op.step(1)
+            down_op.step(2)
+            proj_op.step(1)
+            proj_op.step(2)
     gate_up_op.step(1)
-    down_op.step(1)
+    gate_up_op.step(2)
+    down_op.step(3)
+    proj_op.step(3)
     kv_gain = misc_t[0:1, :RANK]
     lane = lax.broadcasted_iota(jnp.int32, (128, ROWS), 1)
 
@@ -1240,15 +1271,13 @@
         key_rope = key_rope * cos - swap_halves(key_rope) * sin
         qc_grad[at, MISC_AT:CORE_W] = jnp.where(lane < ROPE, key_rope, 0.0).astype(bf16)
 
-    gate_up_op.step(2)
-    down_op.step(2)
     made = tn(latent[...], expanded_grad[...]).astype(bf16)
     each = RANK // DP
     for d in range(DP):
         for k in range(4):
             at = pl.ds(d * ROWS + k * each, each)
             up_grad[at, :] = made[d * each : (d + 1) * each, k * ROWS : (k + 1) * ROWS]
-    up_store = pltpu.make_async_copy(up_grad, grads.at[:, pl.ds(GRAD_UP_AT, ROWS)], out_sem.at[2])
+    up_store = pltpu.make_async_copy(up_grad, grads.at[:, pl.ds(UP_AT, ROWS)], out_sem.at[2])
     up_store.start()
     misc_grad[...] = jnp.zeros_like(misc_grad)
     misc_grad[64:72, :] = norm_rows[...]
@@ -1262,12 +1291,8 @@
         qc_grad[at, QW : QW + RANK] = norm_back(inner, scale, kv_gain, latent_grad).astype(bf16)
     for d in range(DP):
         misc_grad[66:67, d * ROWS : d * ROWS + each] = kv_total[:, d * each : (d + 1) * each]
-    tok_load.wait()
-
-    @pl.loop(0, SEQ // 32)
-    def _(k):
-        at = pl.ds(pl.multiple_of(k * 32, 32), 32)
-        scale_one[at, :] = inverse_rms(proj[at, :].astype(f32))
+    gate_up_op.step(3)
+    proj_op.step(4)
 
     def put(n):
         at = pl.ds(pl.multiple_of(n * TILE, TILE), TILE)
@@ -1284,13 +1309,29 @@
         grad = nt(qc_grad[...], weights[at, :CORE_W])
         made_h[n % 2] = grad.astype(bf16)
         put(n).start()
-        grad = grad * proj[:, at].astype(f32) * scale_one[...]
+        grad = grad * tok[:, at].astype(f32) * scale_one[...]
         misc_grad[64:65, at] = jnp.sum(grad, axis=0, keepdims=True)
 
     put(2).wait()
     put(3).wait()
-    gate_up_op.step(3)
-    down_op.step(3)
+    proj_op.step(5)
+    out_op.step(5)
+
+    def half(n, k):
+        rows, at = pl.ds(k * SEQ, SEQ), pl.ds(n * TILE, TILE)
+        return pltpu.make_async_copy(proj_all.at[rows, at], made_h.at[k], out_sem.at[k])
+
+    half(0, 0).start()
+    half(0, 1).start()
+    for n in range(D // TILE):
+        total = 0.0
+        for k in range(2):
+            half(n, k).wait()
+            total = total + tn(head_cols[pl.ds(k * SEQ, SEQ), :], made_h[k])
+            if n < D // TILE - 1:
+                half(n + 1, k).start()
+        rows, at = pl.ds(n // 2 * ROWS, ROWS), pl.ds(n % 2 * TILE, TILE)
+        out_grad[rows, at] = total.astype(bf16)
 
     def store(n):
         at = pl.ds(pl.multiple_of(n * TILE, TILE), TILE)
@@ -1316,7 +1357,6 @@
     up_store.wait()
     gate_up_op.step(4)
     down_op.step(4)
-    out_op.step(5)
     gate_up_op.step(5)
     down_op.step(5)
 
@@ -1332,13 +1372,10 @@
         ((HEADS_HERE, SEQ, 2 * NOPE), bf16),
         ((HEADS_HERE, SEQ, 2 * NOPE), bf16),
         ((HEADS_HERE, SEQ, VDIM), bf16),
-        ((SEQ, OW), bf16),
+        ((GROUP, ROWS), bf16),
         ((ROWS, D), f32),
         ((HEADS_HERE, SEQ, ROWS), f32),
-        ((2 * HALF, D), bf16),
-        ((FULL, D), bf16),
         ((RANK, KVW), bf16),
-        ((OW, D), bf16),
         ((SEQ, OW), bf16),
         ((HEADS_HERE, SEQ, 2 * NOPE), f32),
         ((HEADS_HERE, SEQ, VDIM), f32),
@@ -1356,14 +1393,17 @@
         name="attention_grad",
         out_shape=[
             jax.ShapeDtypeStruct((SEQ, D), bf16),
-            jax.ShapeDtypeStruct((GU_PART, D), bf16),
-            jax.ShapeDtypeStruct((DN_PART, D), bf16),
-            jax.ShapeDtypeStruct((D, GRAD_PACK), bf16),
+            jax.ShapeDtypeStruct((DP * GU_PART, ROWS), bf16),
+            jax.ShapeDtypeStruct((SP * DP * GU_PART, ROWS), bf16),
+            jax.ShapeDtypeStruct((FULL, D), bf16),
+            jax.ShapeDtypeStruct((D, PACK), bf16),
+            jax.ShapeDtypeStruct((GROUP, D), bf16),
+            jax.ShapeDtypeStruct((2 * ROWS, D // 2), bf16),
         ],
         in_specs=[any_spec] * 15 + [vmem] * 3,
-        out_specs=[any_spec, vmem, vmem, any_spec],
+        out_specs=[any_spec] * 6 + [vmem],
         scratch_shapes=[pltpu.VMEM(*shape) for shape in scratch]
-        + [pltpu.SemaphoreType.DMA((13,)), pltpu.SemaphoreType.DMA((3,))]
+        + [pltpu.SemaphoreType.DMA((10,)), pltpu.SemaphoreType.DMA((3,))]
         + [entry for op in attention_grad_ops() for entry in op.scratch()],
         compiler_params=pltpu.CompilerParams(
             collective_id=4, has_side_effects=True, vmem_limit_bytes=61 * 2**20
@@ -1485,7 +1525,7 @@
             jnp.zeros((1, D), f32),
         ]
     )
-    hidden_one_grad, gate_up_grad, down_grad, grads = attention_grad(
+    hidden_one_grad, _, gu_total, dn_total, grads, _, out_grad = attention_grad(
         proj_grad,
         tok_all,
         weights,
@@ -1506,33 +1546,26 @@
         norm_rows,
     )
 
-    _, hidden_one_grad, _, gu_total, dn_total, mixed, grads = exchange(
+    _, hidden_one_grad, mixed, grads, _, out_total = exchange(
         "sum_grads",
         6,
         [
-            Scatter("dp", ROWS, GRAD_PACK, bf16, spare=True),
+            Scatter("dp", ROWS, PACK, bf16, spare=True),
             Scatter("sp", ROWS, D),
-            Swap(
-                "dp",
-                (DP * GU_PART, ROWS),
-                lambda ref, j: ref.at[:, pl.ds(pl.multiple_of(j * ROWS, ROWS), ROWS)],
-                lambda ref, j: ref.at[pl.ds(pl.multiple_of(j * GU_PART, GU_PART), GU_PART)],
-            ),
-            Gather("sp", DP * GU_PART, ROWS),
-            Gather("sp", DN_PART, D, spare=True),
             Scatter("dp", ROWS, D, spare=True),
-            Gather("sp", ROWS, GRAD_PACK),
+            Gather("sp", ROWS, PACK),
+            Scatter("sp", 2 * ROWS // SP, D // 2, bf16),
+            Gather("sp", 2 * ROWS // SP, D // 2),
         ],
-        [grads, hidden_one_grad, gate_up_grad, down_grad, mixed_part],
-        plan=[(2, 0), (0, 0), (1, 0), (2, 5), (3, 0), (4, 0)]
-        + [(0, 1), (1, 1), (0, 2), (0, 3), (1, 2), (3, 1), (4, 1), (0, 4), (6, 0), (5, 0), (1, 3)]
-        + [(3, 2), (4, 2), (5, 1), (1, 4), (3, 3), (4, 3), (6, 1), (6, 2), (5, 2), (5, 3)]
-        + [(3, 4), (4, 4), (6, 3), (5, 4), (6, 4)]
-        + [(op, 5) for op in (0, 1, 3, 4, 5, 6)],
-        chained=[(3, 2), (6, 0)],
+        [grads, hidden_one_grad, mixed_part, out_grad],
+        plan=[(0, 0), (1, 0), (4, 0), (2, 0), (0, 1), (4, 1), (1, 1), (0, 2), (0, 3), (4, 2), (4, 3)]
+        + [(1, 2), (0, 4), (3, 0), (4, 4), (5, 0), (1, 3), (2, 1), (3, 1), (3, 2), (5, 1), (5, 2)]
+        + [(2, 2), (2, 3), (1, 4), (3, 3), (5, 3), (2, 4), (3, 4), (5, 4)]
+        + [(op, 5) for op in range(6)],
+        chained=[(3, 0), (5, 4)],
     )
     gu_total = gu_total.reshape(SP, DP, GU_PART, ROWS)
-    grads = grads.reshape(SP, ROWS, GRAD_PACK)
+    grads = grads.reshape(SP, ROWS, PACK)
     mixed = (resid_two + mixed).astype(bf16)
     resid_one = tokens.astype(f32)
     own_scale = inverse_rms(resid_one)
@@ -1555,8 +1588,8 @@
     query_total = side_by_side(query_total, QW)
     tail = jnp.sum(grads[:, :, QW:CORE_W].astype(f32), axis=0)
     down_total, tail = tail[:, : RANK + ROPE], tail[:, RANK + ROPE :]
-    out_total = side_by_side(grads[:, :, CORE_W:GRAD_UP_AT], OW)
-    up_total = grads[:, :, GRAD_UP_AT:].reshape(SP, 4, RANK // DP, ROWS).transpose(0, 2, 1, 3)
+    out_total = jnp.concatenate([out_total[:ROWS], out_total[ROWS:]], axis=1).astype(f32)
+    up_total = grads[:, :, UP_AT:].reshape(SP, 4, RANK // DP, ROWS).transpose(0, 2, 1, 3)
     up_total = side_by_side(up_total.reshape(SP, RANK // DP, KVW), KVW)
 
     gu_total = gu_total.transpose(0, 2, 1, 3).reshape(2, SETS, ROOM, DP, ROWS)[:, :, :SLICE]

time: 580 us -> 521 us (0.90)
  Pallas kernels: 492 us -> 440 us
  local copies, waits for them, and re-layouts: 55.1 us -> 44.9 us
    pallas_call x1, Pallas kernels: 130 us -> 90 us  [exchange(): pl.pallas_call(body, name=name, out_shape=[shape for shape, _ in outs], i...]
    pallas_call x1, Pallas kernels: 104 us -> 136 us  [experts(): pl.pallas_call(expert_kernel, name='experts', out_shape=[jax.ShapeDtypeSt...]
    pallas_call x1, Pallas kernels: 114 us -> 91.3 us  [attention_grad(): pl.pallas_call(attention_grad_kernel, name='attention_grad', out_shape=[j...]
    pallas_call x1, Pallas kernels: 144 us -> 122 us  [attention(): pl.pallas_call(attention_kernel, name='attention', out_shape=[jax.ShapeDt...]
    unnamed x31 -> x37, local copies, waits for them, and re-layouts: 22.2 us -> 19.7 us
where the time goes in v4:
time: 521 us; the launch traced here: 512 us
  Pallas kernels  440 us (84%)
  local copies, waits for them, and re-layouts  44.9 us (9%)
  other arithmetic  15.2 us (3%)
  matrix products  10.3 us (2%)
    pallas_call x1, Pallas kernels, experts(): pl.pallas_call(expert_kernel, name='experts', out_shape=[jax.ShapeDtypeSt...  136 us
    pallas_call x1, Pallas kernels, attention(): pl.pallas_call(attention_kernel, name='attention', out_shape=[jax.ShapeDt...  122 us
    pallas_call x1, Pallas kernels, attention_grad(): pl.pallas_call(attention_grad_kernel, name='attention_grad', out_shape=[j...  91.3 us
    pallas_call x1, Pallas kernels, exchange(): pl.pallas_call(body, name=name, out_shape=[shape for shape, _ in outs], i...  90 us
    unnamed x37, local copies, waits for them, and re-layouts  19.7 us

profile of v4, /device:TPU:1, one launch (start us, length us, event | category | flops | bytes accessed | tf_op | source)
XLA Modules:
  0.0 511.6 jit_solution(10258277605790396061)
XLA Ops:
  4.9 0.9 constant_dynamic-slice_fusion.1
  6.7 1.1 copy.121
  7.8 0.9 concatenate.12.pack
  8.7 122.0 %attention.1 = (f32[128,2048]{1,0:T(8,128)}, bf16[128,2048]{1,0:T(8,128)(2,1)}, bf16[2048,2048]{1,0:T(8,128)(2,1)}, bf16[144,2048]{1,0:T(8,128)(2,1)}, bf16[1152...) custom-call(bf16[128,2048]{1,0:T(8,128)(2,1)} %tokens.1, ...), custom_call_target="tpu_custom_call" | custom-call | flops 5368709120 | bytes 62914560 | tf_op jit(solution)/shard_map/attention/pallas_call | solution.py:1075
  130.7 1.4 multiply_reduce_fusion.2
  132.1 0.9 fusion.15
  133.0 1.3 convert.13
  135.5 1.9 slice.117.picks
  137.4 136.4 %experts.1 = (f32[128,2176]{1,0:T(8,128)}, bf16[2048,2048]{1,0:T(8,128)(2,1)}, bf16[144,2048]{1,0:T(8,128)(2,1)}, bf16[80,2048]{1,0:T(8,128)(2,1)}) custom-call(bf16[128,2048]{1,0:T(8,128)(2,1)} %get-tuple-element.48.hidden_own, bf16[1152,2048]{1,0:T(8,128)(2,1)} %get-tuple-element.49.weights, bf16[16,2048]{1,0:T(8,128)(2,1)} %slice.144.router_t, ...), custom_call_target="tpu_custom_call" | custom-call | flops 48318382080 | bytes 41943040 | tf_op jit(solution)/shard_map/experts/pallas_call | solution.py:736
  273.8 1.1 multiply_reduce_fusion.3
  274.9 1.0 multiply_convert_fusion
  275.9 2.6 multiply_reduce_fusion
  279.5 1.7 fusion.12
  281.2 7.2 %convolution_convert_fusion.head_tok = bf16[128,2048]{1,0:T(8,128)(2,1)} fusion(bf16[128,2048]{1,0:T(8,128)(2,1)S(1)} %get-tuple-element.162.proj_own, bf16[2048,2048]{1,0:T(8,128)(2,1)} %get-tuple-element.62), kind=kOutput, calls=%fused_computation.6 | convolution fusion | flops 1074003968 | bytes 9437184 | tf_op jit(solution)/shard_map/dot_general | solution.py:55
  288.5 91.3 %attention_grad.1 = (bf16[1024,2048]{1,0:T(8,128)(2,1)}, bf16[2304,128]{1,0:T(8,128)(2,1)}, bf16[18432,128]{1,0:T(8,128)(2,1)}, bf16[640,2048]{1,0:T(8,128)(2,1)...) custom-call(bf16[128,2048]{1,0:T(8,128)(2,1)} %copy-done.8, ...), custom_call_target="tpu_custom_call" | custom-call | flops 12884901888 | bytes 62914560 | tf_op jit(solution)/shard_map/attention_grad/pallas_call | solution.py:1391
  379.8 90.0 %sum_grads.1 = (bf16[128,1152]{1,0:T(8,128)(2,1)}, f32[128,2048]{1,0:T(8,128)}, f32[128,2048]{1,0:T(8,128)}, bf16[1024,1152]{1,0:T(8,128)(2,1)}, bf16[32,1024]{1,0:T(8,128)(2,1)}, /*index=5*/bf16[256,1024]{1,0:T(8,128)(2,1)}) custom-call(bf16[2048,1152]{1,0:T(8,128)(2,1)} %get-tuple-element.66.refs_0_, bf16[1024,2048]{1,0:T(8,128)(2,1)} %get-tuple-element.67.refs_1_, ...), custom_call_target="tpu_custom_call" | custom-call | tf_op jit(solution)/shard_map/sum_grads/pallas_call | solution.py:488
  469.9 2.7 fusion
  472.6 1.3 fusion.4
  478.4 1.1 copy.143
  479.8 1.3 copy.142
  481.2 1.1 maximum_convert_fusion
  482.8 1.3 convert_bitcast_fusion.1
  484.1 1.7 slice.161
  485.8 2.4 slice.164
  488.2 1.2 copy.132
  490.3 2.6 copy.133
  492.9 1.8 slice_bitcast_fusion.2
  494.7 1.9 slice_bitcast_fusion
  496.6 4.7 copy.140
  501.3 3.5 copy.138
  504.8 3.5 copy.137
  508.3 2.8 copy.139
  (70 shorter events, 13.5 us)
Async XLA Ops:
  0.6 1.6 copy-start
  130.6 3.7 copy-start.9
  137.4 138.5 %copy-start.2 = (f32[128,2048]{1,0:T(8,128)S(1)}, f32[128,2048]{1,0:T(8,128)}, u32[]{:S(2)}) copy-start(f32[128,2048]{1,0:T(8,128)} %get-tuple-element.46) | copy-start | bytes 3145732
  273.8 4.7 copy-start.10
  281.2 7.3 %copy-start.8 = (bf16[128,2048]{1,0:T(8,128)(2,1)}, bf16[128,2048]{1,0:T(8,128)(2,1)S(1)}, u32[]{:S(2)}) copy-start(bf16[128,2048]{1,0:T(8,128)(2,1)S(1)} %get-tuple-element.162.proj_own) | copy-start | bytes 1572868
  379.8 90.1 %copy-start.7 = (bf16[128,2048]{1,0:T(8,128)(2,1)S(1)}, bf16[128,2048]{1,0:T(8,128)(2,1)}, u32[]{:S(2)}) copy-start(bf16[128,2048]{1,0:T(8,128)(2,1)} %tokens.1) | copy-start | bytes 1572868
  469.8 2.8 copy-start.3
  472.6 1.9 copy-start.4
  474.4 3.2 copy-start.5
  479.5 1.6 copy-start.11
  479.8 2.4 copy-start.6
  482.8 5.4 %slice-start = ((s8[4718592]{0:T(1024)(128)(4,1)}), s8[4194304]{0:T(1024)(128)(4,1)S(1)}, s32[]{:S(2)}) async-start(s8[4718592]{0:T(1024)(128)(4,1)} %bitcast.52), calls=%async_computation | async-start | bytes 8388608
  484.1 4.1 slice-start.1
  504.8 6.4 %copy-start.1 = (bf16[32,4096]{1,0:T(8,128)(2,1)S(1)}, bf16[32,4096]{1,0:T(8,128)(2,1)}, u32[]{:S(2)}) copy-start(bf16[32,4096]{1,0:T(8,128)(2,1)} %param.26) | copy-start | bytes 786436

commit v5 on v4

--- a/solution.py
+++ b/solution.py
@@ -248,12 +248,13 @@
 
 
 class Scatter:
-    def __init__(self, axis, rows, width, kind=f32, spare=False):
+    def __init__(self, axis, rows, width, kind=f32, spare=False, load=False):
         self.axis, self.rows, self.width, self.kind, self.spare = axis, rows, width, kind, spare
+        self.load = load
         self.count = SP if axis == "sp" else DP
 
     def in_spec(self):
-        return pl.BlockSpec(memory_space=pltpu.VMEM)
+        return pl.BlockSpec(memory_space=pl.ANY if self.load else pltpu.VMEM)
 
     def out(self):
         return (
@@ -266,9 +267,10 @@
         first, second = (cut, self.width), (self.rows - cut, self.width)
         shapes = [block, block, block, first, second, block, block, block]
         shapes = shapes + [(8 if self.axis == "dp" else 5,) + block]
+        kept = [pltpu.VMEM((self.count * self.rows, self.width), bf16), pltpu.SemaphoreType.DMA]
         return [pltpu.SemaphoreType.DMA((17,)), pltpu.SemaphoreType.DMA((17,))] + [
             pltpu.VMEM(shape, bf16) for shape in shapes
-        ]
+        ] + kept * self.load
 
     partners = Gather.partners
     copy = Gather.copy
@@ -284,6 +286,10 @@
         self.send_sem, self.recv_sem = scratch[:2]
         self.got, self.made = scratch[2:10], scratch[10]
         self.seat = Seat(self.axis)
+        if self.load:
+            self.loading = pltpu.make_async_copy(src, scratch[11], scratch[12])
+            self.loading.start()
+            self.src = scratch[11]
 
     def given(self, *place):
         return block_of(self.src, self.seat.index(*place) * self.rows, self.rows)
@@ -350,6 +356,8 @@
 
     def step(self, number):
         if number == 0:
+            if self.load:
+                self.loading.wait()
             if self.axis == "dp":
                 self.go(*range(8, 16))
             self.ready((1, 2))
@@ -517,7 +525,7 @@
     router_t,
     down,
     cot_all,
-    picks,
+    attention_weights,
     sum_out,
     mixed_out,
     gate_up_sum,
@@ -537,6 +545,7 @@
     reached,
     spread,
     collect,
+    picks,
     running,
     load_sem,
     in_sem,
@@ -558,6 +567,7 @@
     loads = [
         pltpu.make_async_copy(down, down_w, load_sem.at[2]),
         pltpu.make_async_copy(weights, sums.at[pl.ds(0, 2 * HALF), pl.ds(0, D)], load_sem.at[0]),
+        pltpu.make_async_copy(attention_weights.at[:, pl.ds(MISC_AT, ROWS)], picks, load_sem.at[1]),
     ]
     for load in loads:
         load.start()
@@ -604,7 +614,7 @@
         fetch(i).wait()
         raw[chunk(i), :] = nt(stage[i % 2], down_w[...])
 
-    loads[1].wait()
+    wait_all(loads[1:])
     for k in range(2 * SETS):
         for part in range(SP):
             units = sums[part * RELAY + k * UNITS : part * RELAY + (k + 1) * UNITS, :D]
@@ -707,21 +717,22 @@
             turn_sem, inc=1, device_id=seat.device(partner), device_id_type=pl.DeviceIdType.MESH
         )
     scatter.step(2)
-    outputs(0, 4)
-    scatter.step(3)
+    outputs(0, 2)
     pl.semaphore_wait(turn_sem, len(NEAR))
     gate_up_op.step(0)
-    outputs(4, 8)
+    outputs(2, 6)
+    scatter.step(3)
+    outputs(6, 8)
     put(6).wait()
     put(7).wait()
     down_grads(0, 8)
     down_op.step(0)
     gate_up_op.step(1)
+    gate_up_op.step(2)
     scatter.step(4)
-    for step in (2, 3):
-        gate_up_op.step(step)
-        down_op.step(step - 1)
-    down_op.step(3)
+    gate_up_op.step(3)
+    for step in (1, 2, 3):
+        down_op.step(step)
     gate_up_op.step(4)
     down_op.step(4)
     gate_up_op.step(5)
@@ -742,7 +753,7 @@
             jax.ShapeDtypeStruct((GU_PART, D), bf16),
             jax.ShapeDtypeStruct((DN_PART, D), bf16),
         ],
-        in_specs=[any_spec, any_spec, vmem, any_spec, any_spec, vmem],
+        in_specs=[any_spec, any_spec, vmem, any_spec, any_spec, any_spec],
         out_specs=[vmem, any_spec, vmem, vmem],
         scratch_shapes=[
             pltpu.VMEM((GROUP, D), bf16),
@@ -760,6 +771,7 @@
             pltpu.VMEM((CHUNK, 2 * FULL), bf16),
             pltpu.VMEM((2 * ROWS, FULL), bf16),
             pltpu.VMEM((2 * FULL, ROWS), bf16),
+            pltpu.VMEM((GROUP, ROWS), bf16),
             pltpu.VMEM((4, GU_PART, D), bf16),
             pltpu.SemaphoreType.DMA((3,)),
             pltpu.SemaphoreType.DMA((4,)),
@@ -1127,7 +1139,7 @@
     key_all,
     value_all,
     head_all,
-    head_tok,
+    out_w_all,
     misc_all,
     total_all,
     gate_up_sum,
@@ -1150,6 +1162,9 @@
     query,
     key,
     value,
+    proj,
+    out_w,
+    head_own,
     head_cols,
     misc_t,
     totals,
@@ -1177,7 +1192,7 @@
         (gate_up_piece, gate_up_total),
         (down_sum, down_total),
         (head_all, head_cols),
-        (head_tok, head_grad),
+        (head_own, head_grad),
     )
     for op, (src, dst) in zip(ops, bound):
         count = len(op.scratch())
@@ -1187,6 +1202,8 @@
         pltpu.make_async_copy(src, dst, load_sem.at[k])
         for k, (src, dst) in enumerate(
             (
+                (proj_own, proj),
+                (out_w_all, out_w),
                 (tok_all, tok),
                 (query_all, query),
                 (key_all, key),
@@ -1203,12 +1220,14 @@
     for load in loads:
         load.start()
     meet(ops)
+    wait_all(loads[:2])
+    head_own[...] = nt(proj[...], out_w[...]).astype(bf16)
     head_op.step(0)
     piece_op.step(0)
     down_op.step(0)
     proj_op.step(0)
     out_op.step(0)
-    wait_all(loads)
+    wait_all(loads[2:])
 
     @pl.loop(0, SEQ // 32)
     def _(k):
@@ -1247,8 +1266,6 @@
             down_op.step(2)
             proj_op.step(1)
             proj_op.step(2)
-    gate_up_op.step(1)
-    gate_up_op.step(2)
     down_op.step(3)
     proj_op.step(3)
     kv_gain = misc_t[0:1, :RANK]
@@ -1291,8 +1308,8 @@
         qc_grad[at, QW : QW + RANK] = norm_back(inner, scale, kv_gain, latent_grad).astype(bf16)
     for d in range(DP):
         misc_grad[66:67, d * ROWS : d * ROWS + each] = kv_total[:, d * each : (d + 1) * each]
-    gate_up_op.step(3)
-    proj_op.step(4)
+    gate_up_op.step(1)
+    gate_up_op.step(2)
 
     def put(n):
         at = pl.ds(pl.multiple_of(n * TILE, TILE), TILE)
@@ -1314,6 +1331,31 @@
 
     put(2).wait()
     put(3).wait()
+    gate_up_op.step(3)
+    proj_op.step(4)
+    down_op.step(4)
+    def store(n):
+        at = pl.ds(pl.multiple_of(n * TILE, TILE), TILE)
+        return pltpu.make_async_copy(
+            made_w.at[n % 2], grads.at[at, pl.ds(0, CORE_W)], out_sem.at[n % 2]
+        )
+
+    @pl.loop(0, D // TILE)
+    def _(n):
+        at = pl.ds(pl.multiple_of(n * TILE, TILE), TILE)
+
+        @pl.when(n >= 2)
+        def _():
+            store(n - 2).wait()
+
+        made = tn(hidden[:, at], qc_grad[...])
+        made_w[n % 2, :, :MISC_AT] = made[:, :MISC_AT].astype(bf16)
+        made_w[n % 2, :, MISC_AT:] = (made[:, MISC_AT:] + misc_grad[:, at].T).astype(bf16)
+        store(n).start()
+
+    store(2).wait()
+    store(3).wait()
+    up_store.wait()
     proj_op.step(5)
     out_op.step(5)
 
@@ -1333,30 +1375,7 @@
         rows, at = pl.ds(n // 2 * ROWS, ROWS), pl.ds(n % 2 * TILE, TILE)
         out_grad[rows, at] = total.astype(bf16)
 
-    def store(n):
-        at = pl.ds(pl.multiple_of(n * TILE, TILE), TILE)
-        return pltpu.make_async_copy(
-            made_w.at[n % 2], grads.at[at, pl.ds(0, CORE_W)], out_sem.at[n % 2]
-        )
-
-    @pl.loop(0, D // TILE)
-    def _(n):
-        at = pl.ds(pl.multiple_of(n * TILE, TILE), TILE)
-
-        @pl.when(n >= 2)
-        def _():
-            store(n - 2).wait()
-
-        made = tn(hidden[:, at], qc_grad[...])
-        made_w[n % 2, :, :MISC_AT] = made[:, :MISC_AT].astype(bf16)
-        made_w[n % 2, :, MISC_AT:] = (made[:, MISC_AT:] + misc_grad[:, at].T).astype(bf16)
-        store(n).start()
-
-    store(2).wait()
-    store(3).wait()
-    up_store.wait()
     gate_up_op.step(4)
-    down_op.step(4)
     gate_up_op.step(5)
     down_op.step(5)
 
@@ -1372,6 +1391,9 @@
         ((HEADS_HERE, SEQ, 2 * NOPE), bf16),
         ((HEADS_HERE, SEQ, 2 * NOPE), bf16),
         ((HEADS_HERE, SEQ, VDIM), bf16),
+        ((ROWS, D), bf16),
+        ((D, D), bf16),
+        ((ROWS, D), bf16),
         ((GROUP, ROWS), bf16),
         ((ROWS, D), f32),
         ((HEADS_HERE, SEQ, ROWS), f32),
@@ -1403,7 +1425,7 @@
         in_specs=[any_spec] * 15 + [vmem] * 3,
         out_specs=[any_spec] * 6 + [vmem],
         scratch_shapes=[pltpu.VMEM(*shape) for shape in scratch]
-        + [pltpu.SemaphoreType.DMA((10,)), pltpu.SemaphoreType.DMA((3,))]
+        + [pltpu.SemaphoreType.DMA((12,)), pltpu.SemaphoreType.DMA((3,))]
         + [entry for op in attention_grad_ops() for entry in op.scratch()],
         compiler_params=pltpu.CompilerParams(
             collective_id=4, has_side_effects=True, vmem_limit_bytes=61 * 2**20
@@ -1412,6 +1434,70 @@
             flops=6 * SEQ * D * CORE_W, bytes_accessed=60 * 2**20, transcendentals=SEQ * SEQ
         ),
     )(*arrays)
+
+
+def unpack_kernel(
+    gate_up, down, gate_shared, up_shared, gate_routed, up_routed, down_shared, down_routed, block, rows, pick, sem
+):
+    def fetch(k):
+        part, skip = divmod(k * ROOM, GU_PART)
+        first = min(ROOM, GU_PART - skip)
+        pieces = [(part, skip, 0, first)] + ([(part + 1, 0, first, ROOM - first)] if first < ROOM else [])
+        return [
+            pltpu.make_async_copy(
+                gate_up.at[s, :, pl.ds(begin, size)], block.at[k % 2, :, pl.ds(at, size)], sem.at[k % 2, n]
+            )
+            for n, (s, begin, at, size) in enumerate(pieces)
+        ]
+
+    load = pltpu.make_async_copy(down, rows, sem.at[2, 0])
+    load.start()
+    for copy in fetch(0):
+        copy.start()
+    row = lax.broadcasted_iota(jnp.int32, pick.shape, 0)
+    column = lax.broadcasted_iota(jnp.int32, pick.shape, 1)
+    unit = row - row // ROOM * ROOM
+    pick[...] = ((row // ROOM * SLICE + unit == column) & (unit < SLICE)).astype(bf16)
+    for k in range(2 * SETS):
+        if k + 1 < 2 * SETS:
+            for copy in fetch(k + 1):
+                copy.start()
+        for copy in fetch(k):
+            copy.wait()
+        made = tn(block[k % 2].reshape(DP * ROOM, ROWS), pick[...])
+        e = k % SETS
+        shared, routed = (gate_shared, gate_routed) if k < SETS else (up_shared, up_routed)
+        if e < NS:
+            shared[:, e, :] = made
+        else:
+            routed[:, e - NS, :] = made
+    load.wait()
+    for e in range(SETS):
+        made = rows[e * ROOM : e * ROOM + SLICE, :].astype(f32)
+        if e < NS:
+            down_shared[:, e, :] = made
+        else:
+            down_routed[:, e - NS, :] = made
+
+
+def unpack(gate_up, down):
+    any_spec, vmem = pl.BlockSpec(memory_space=pl.ANY), pl.BlockSpec(memory_space=pltpu.VMEM)
+    width, height = SLICE, ROWS
+    return pl.pallas_call(
+        unpack_kernel,
+        name="unpack",
+        out_shape=[jax.ShapeDtypeStruct((height, n, FE), f32) for n in (NS, NS, EXPERTS, EXPERTS)]
+        + [jax.ShapeDtypeStruct((width, n, D), f32) for n in (NS, EXPERTS)],
+        in_specs=[any_spec] * 2,
+        out_specs=[vmem] * 6,
+        scratch_shapes=[
+            pltpu.VMEM((2, DP, ROOM, ROWS), bf16),
+            pltpu.VMEM((FULL, D), bf16),
+            pltpu.VMEM((DP * ROOM, FE), bf16),
+            pltpu.SemaphoreType.DMA((3, 2)),
+        ],
+        compiler_params=pltpu.CompilerParams(vmem_limit_bytes=56 * 2**20),
+    )(gate_up, down)
 
 
 def per_device(
@@ -1493,11 +1579,10 @@
     latent_gain = misc[GAIN_KV].reshape(DP, ROWS)[:, : RANK // DP].reshape(RANK)
     router_t = misc[ROUTER_LANE : ROUTER_LANE + 16].astype(bf16)
     router_w = router_t[:EXPERTS]
-    picks_all = weights[:, MISC_AT:CORE_W]
     scale_two = inverse_rms(resid_two)
 
     hidden_grad, mixed_part, gate_up_grad, down_grad = experts(
-        hidden_two, gate_up, router_t, down, cot_all, picks_all
+        hidden_two, gate_up, router_t, down, cot_all, weights
     )
     prob_grad = hidden_grad[:, D + PICK_LANE : D + PICK_LANE + EXPERTS]
     hidden_grad = hidden_grad[:, :D]
@@ -1515,7 +1600,6 @@
     resid_two_grad = upstream + norm_back(resid_two, scale_two, gain_two, hidden_grad)
     proj_grad = resid_two_grad.astype(bf16)
 
-    head_tok_grad = nt(proj_grad, out_w).astype(bf16)
     norm_rows = jnp.concatenate(
         [
             jnp.zeros((1, D), f32),
@@ -1536,7 +1620,7 @@
         keys,
         values,
         head_out,
-        head_tok_grad,
+        out_w,
         misc,
         log_totals,
         gate_up_grad,
@@ -1550,21 +1634,23 @@
         "sum_grads",
         6,
         [
-            Scatter("dp", ROWS, PACK, bf16, spare=True),
-            Scatter("sp", ROWS, D),
-            Scatter("dp", ROWS, D, spare=True),
+            Scatter("dp", ROWS, PACK, bf16, spare=True, load=True),
+            Scatter("sp", ROWS, D, load=True),
+            Scatter("dp", ROWS, D, spare=True, load=True),
             Gather("sp", ROWS, PACK),
             Scatter("sp", 2 * ROWS // SP, D // 2, bf16),
             Gather("sp", 2 * ROWS // SP, D // 2),
         ],
         [grads, hidden_one_grad, mixed_part, out_grad],
-        plan=[(0, 0), (1, 0), (4, 0), (2, 0), (0, 1), (4, 1), (1, 1), (0, 2), (0, 3), (4, 2), (4, 3)]
+        plan=[(0, 0), (1, 0), (4, 0), (0, 1), (4, 1), (1, 1), (0, 2), (0, 3), (2, 0), (4, 2), (4, 3)]
         + [(1, 2), (0, 4), (3, 0), (4, 4), (5, 0), (1, 3), (2, 1), (3, 1), (3, 2), (5, 1), (5, 2)]
         + [(2, 2), (2, 3), (1, 4), (3, 3), (5, 3), (2, 4), (3, 4), (5, 4)]
         + [(op, 5) for op in range(6)],
         chained=[(3, 0), (5, 4)],
     )
-    gu_total = gu_total.reshape(SP, DP, GU_PART, ROWS)
+    gate_shared, up_shared, gate_routed, up_routed, down_shared, down_routed = unpack(
+        gu_total.reshape(SP, DP, GU_PART, ROWS), dn_total
+    )
     grads = grads.reshape(SP, ROWS, PACK)
     mixed = (resid_two + mixed).astype(bf16)
     resid_one = tokens.astype(f32)
@@ -1592,9 +1678,6 @@
     up_total = grads[:, :, UP_AT:].reshape(SP, 4, RANK // DP, ROWS).transpose(0, 2, 1, 3)
     up_total = side_by_side(up_total.reshape(SP, RANK // DP, KVW), KVW)
 
-    gu_total = gu_total.transpose(0, 2, 1, 3).reshape(2, SETS, ROOM, DP, ROWS)[:, :, :SLICE]
-    gu_total = gu_total.transpose(0, 4, 1, 3, 2).reshape(2, ROWS, SETS, FE).astype(f32)
-    dn_total = dn_total[:HALF].reshape(SETS, ROOM, D)[:, :SLICE].transpose(1, 0, 2).astype(f32)
     return (
         mixed,
         tokens_grad,
@@ -1606,12 +1689,12 @@
         out_total,
         tail[:, 1],
         tail[:, 3:7],
-        gu_total[0, :, :NS],
-        gu_total[1, :, :NS],
-        dn_total[:, :NS],
-        gu_total[0, :, NS:],
-        gu_total[1, :, NS:],
-        dn_total[:, NS:],
+        gate_shared,
+        up_shared,
+        down_shared,
+        gate_routed,
+        up_routed,
+        down_routed,
     )
 
 

time: 521 us -> 489 us (0.939)
  local copies, waits for them, and re-layouts: 44.9 us -> 16.3 us
  matrix products: 10.3 us -> 3.08 us
    pallas_call x0 -> x1, Pallas kernels: none -> 17.5 us  [unpack(): pl.pallas_call(unpack_kernel, name='unpack', out_shape=[jax.ShapeDtypeStr...]
    unnamed x37 -> x27, local copies, waits for them, and re-layouts: 19.7 us -> 5.11 us
    pallas_call x1, Pallas kernels: 90 us -> 80.2 us  [exchange(): pl.pallas_call(body, name=name, out_shape=[shape for shape, _ in outs], i...]
    dot_general x4 -> x3, matrix products: 10.3 us -> 3.08 us  [mm(): lax.dot_general(left, right, ((dims[0], dims[1]), ((), ())), preferred_el...]
    slice x5 -> x0, local copies, waits for them, and re-layouts: 6.48 us -> none  [the longest x1 2.4 us: per_device(): dn_total[:, NS:]]
where the time goes in v5:
time: 489 us; the launch traced here: 480 us
  Pallas kernels  445 us (91%)
  local copies, waits for them, and re-layouts  16.3 us (3%)
  other arithmetic  13.8 us (3%)
    pallas_call x1, Pallas kernels, experts(): pl.pallas_call(expert_kernel, name='experts', out_shape=[jax.ShapeDtypeSt...  136 us
    pallas_call x1, Pallas kernels, attention(): pl.pallas_call(attention_kernel, name='attention', out_shape=[jax.ShapeDt...  122 us
    pallas_call x1, Pallas kernels, attention_grad(): pl.pallas_call(attention_grad_kernel, name='attention_grad', out_shape=[j...  89.2 us
    pallas_call x1, Pallas kernels, exchange(): pl.pallas_call(body, name=name, out_shape=[shape for shape, _ in outs], i...  80.2 us
    pallas_call x1, Pallas kernels, unpack(): pl.pallas_call(unpack_kernel, name='unpack', out_shape=[jax.ShapeDtypeStr...  17.5 us

profile of v5, /device:TPU:1, one launch (start us, length us, event | category | flops | bytes accessed | tf_op | source)
XLA Modules:
  0.0 479.6 jit_solution(13540272523365529965)
XLA Ops:
  0.7 0.7 fusion.11
  1.4 0.7 pad_bitcast_fusion
  2.4 0.8 copy.94
  3.2 0.8 copy.95
  4.0 0.8 copy.97
  4.9 0.9 constant_dynamic-slice_fusion.1
  5.8 0.9 constant_dynamic-slice_fusion.4
  6.7 1.1 copy.92
  7.8 0.9 concatenate.12.pack
  8.7 121.9 %attention.1 = (f32[128,2048]{1,0:T(8,128)}, bf16[128,2048]{1,0:T(8,128)(2,1)}, bf16[2048,2048]{1,0:T(8,128)(2,1)}, bf16[144,2048]{1,0:T(8,128)(2,1)}, bf16[1152...) custom-call(bf16[128,2048]{1,0:T(8,128)(2,1)} %tokens.1, ...), custom_call_target="tpu_custom_call" | custom-call | flops 5368709120 | bytes 62914560 | tf_op jit(solution)/shard_map/attention/pallas_call | solution.py:1087
  130.6 1.4 multiply_reduce_fusion.2
  132.1 0.9 fusion.15
  133.0 1.3 convert.10
  134.9 0.6 slice.104.router_t
  135.5 136.4 %experts.1 = (f32[128,2176]{1,0:T(8,128)}, bf16[2048,2048]{1,0:T(8,128)(2,1)}, bf16[144,2048]{1,0:T(8,128)(2,1)}, bf16[80,2048]{1,0:T(8,128)(2,1)}) custom-call(bf16[128,2048]{1,0:T(8,128)(2,1)} %get-tuple-element.54.hidden_own, bf16[1152,2048]{1,0:T(8,128)(2,1)} %get-tuple-element.55.weights, bf16[16,2048]{1,0:T(8,128)(2,1)} %slice.104.router_t, ...), custom_call_target="tpu_custom_call" | custom-call | flops 48318382080 | bytes 41943040 | tf_op jit(solution)/shard_map/experts/pallas_call | solution.py:747
  271.9 1.1 multiply_reduce_fusion.3
  273.0 1.0 multiply_convert_fusion
  274.1 2.6 multiply_reduce_fusion
  276.9 0.7 concatenate.13.norm_rows
  277.6 2.4 fusion.12
  280.1 89.2 %attention_grad.1 = (bf16[1024,2048]{1,0:T(8,128)(2,1)}, bf16[2304,128]{1,0:T(8,128)(2,1)}, bf16[18432,128]{1,0:T(8,128)(2,1)}, bf16[640,2048]{1,0:T(8,128)(2,1)...) custom-call(bf16[128,2048]{1,0:T(8,128)(2,1)} %get-tuple-element.158.proj_own, ...), custom_call_target="tpu_custom_call" | custom-call | flops 12884901888 | bytes 62914560 | tf_op jit(solution)/shard_map/attention_grad/pallas_call | solution.py:1413
  369.3 80.2 %sum_grads.1 = (bf16[128,1152]{1,0:T(8,128)(2,1)}, f32[128,2048]{1,0:T(8,128)}, f32[128,2048]{1,0:T(8,128)}, bf16[1024,1152]{1,0:T(8,128)(2,1)}, bf16[32,1024]{1,0:T(8,128)(2,1)}, /*index=5*/bf16[256,1024]{1,0:T(8,128)(2,1)}) custom-call(bf16[2048,1152]{1,0:T(8,128)(2,1)} %get-tuple-element.72.refs_0_, bf16[1024,2048]{1,0:T(8,128)(2,1)} %get-tuple-element.73.refs_1_, ...), custom_call_target="tpu_custom_call" | custom-call | tf_op jit(solution)/shard_map/sum_grads/pallas_call | solution.py:496
  449.5 2.7 fusion
  452.2 1.3 fusion.4
  454.3 0.7 slice_reduce_fusion.2
  455.0 0.7 slice_reduce_fusion
  455.7 0.7 copy.104
  456.4 0.9 copy.103
  458.0 1.1 copy.106
  459.4 1.3 copy.105
  460.8 1.1 maximum_convert_fusion
  461.9 17.5 %unpack.1 = (f32[128,2,1408]{2,1,0:T(2,128)}, f32[128,2,1408]{2,1,0:T(2,128)}, f32[128,4,1408]{2,1,0:T(4,128)}, f32[128,4,1408]{2,1,0:T(4,128)}, f32[88,2,2048]{2,1,0:T(2,128)}, /*index=5*/f32[88,4,2048]{2,1,0:T(4,128)}) custom-call(bf16[8,16,144,128]{3,2,1,0:T(8,128)(2,1)} %bitcast.29, bf16[640,2048]{1,0:T(8,128)(2,1)} %get-tuple-element.81.down), custom_call_target="tpu_custom_call" | custom-call | tf_op jit(solution)/shard_map/unpack/pallas_call | solution.py:1486
  (48 shorter events, 3.2 us)
Async XLA Ops:
  0.6 1.6 copy-start
  130.6 3.7 copy-start.7
  135.5 138.6 %copy-start.2 = (f32[128,2048]{1,0:T(8,128)S(1)}, f32[128,2048]{1,0:T(8,128)}, u32[]{:S(2)}) copy-start(f32[128,2048]{1,0:T(8,128)} %get-tuple-element.52) | copy-start | bytes 3145732
  271.9 4.8 copy-start.8
  273.0 4.6 copy-start.9
  369.3 80.2 %copy-start.6 = (bf16[128,2048]{1,0:T(8,128)(2,1)S(1)}, bf16[128,2048]{1,0:T(8,128)(2,1)}, u32[]{:S(2)}) copy-start(bf16[128,2048]{1,0:T(8,128)(2,1)} %tokens.1) | copy-start | bytes 1572868
  449.5 2.8 copy-start.3
  452.2 1.9 copy-start.4
  454.1 3.2 copy-start.5
  459.4 1.3 copy-start.10
  460.8 18.6 %copy-start.1 = (bf16[32,4096]{1,0:T(8,128)(2,1)S(1)}, bf16[32,4096]{1,0:T(8,128)(2,1)}, u32[]{:S(2)}) copy-start(bf16[32,4096]{1,0:T(8,128)(2,1)} %param.26) | copy-start | bytes 786436

commit v6 on v5

--- a/solution.py
+++ b/solution.py
@@ -1024,7 +1024,6 @@
         saves[k].start()
     gate_up_op.step(1)
     gate_up_op.step(2)
-    out_op.step(4)
     cot_op.step(1)
     cot_op.step(2)
     for h in range(HEADS_HERE):
@@ -1038,6 +1037,7 @@
             heads[at, h * VDIM : (h + 1) * VDIM] = nn(probs, value[h, :seen, :]).astype(bf16)
             totals[h, at, :] = jnp.broadcast_to(top + jnp.log(total), (256, ROWS))
         if h == 0:
+            out_op.step(4)
             gate_up_op.step(3)
     head_op.step(0)
     saves[11].start()

time: 489 us -> 504 us (1.031)
  Pallas kernels: 445 us -> 460 us
    pallas_call x1, Pallas kernels: 122 us -> 137 us  [attention(): pl.pallas_call(attention_kernel, name='attention', out_shape=[jax.ShapeDt...]
where the time goes in v6:
time: 504 us; the launch traced here: 495 us
  Pallas kernels  460 us (91%)
  local copies, waits for them, and re-layouts  16.3 us (3%)
  other arithmetic  13.8 us (3%)
    pallas_call x1, Pallas kernels, experts(): pl.pallas_call(expert_kernel, name='experts', out_shape=[jax.ShapeDtypeSt...  137 us
    pallas_call x1, Pallas kernels, attention(): pl.pallas_call(attention_kernel, name='attention', out_shape=[jax.ShapeDt...  137 us
    pallas_call x1, Pallas kernels, attention_grad(): pl.pallas_call(attention_grad_kernel, name='attention_grad', out_shape=[j...  88.4 us
    pallas_call x1, Pallas kernels, exchange(): pl.pallas_call(body, name=name, out_shape=[shape for shape, _ in outs], i...  80.5 us
    pallas_call x1, Pallas kernels, unpack(): pl.pallas_call(unpack_kernel, name='unpack', out_shape=[jax.ShapeDtypeStr...  17.5 us

profile of v6, /device:TPU:1, one launch (start us, length us, event | category | flops | bytes accessed | tf_op | source)
XLA Modules:
  0.0 494.5 jit_solution(8229998906175267203)
XLA Ops:
  0.7 0.7 fusion.11
  1.4 0.7 pad_bitcast_fusion
  2.4 0.8 copy.94
  3.2 0.8 copy.95
  4.0 0.8 copy.97
  4.9 0.9 constant_dynamic-slice_fusion.1
  5.8 0.9 constant_dynamic-slice_fusion.4
  6.7 1.1 copy.92
  7.8 0.9 concatenate.12.pack
  8.7 136.5 %attention.1 = (f32[128,2048]{1,0:T(8,128)}, bf16[128,2048]{1,0:T(8,128)(2,1)}, bf16[2048,2048]{1,0:T(8,128)(2,1)}, bf16[144,2048]{1,0:T(8,128)(2,1)}, bf16[1152...) custom-call(bf16[128,2048]{1,0:T(8,128)(2,1)} %tokens.1, ...), custom_call_target="tpu_custom_call" | custom-call | flops 5368709120 | bytes 62914560 | tf_op jit(solution)/shard_map/attention/pallas_call | solution.py:1087
  145.2 1.4 multiply_reduce_fusion.2
  146.7 0.9 fusion.15
  147.6 1.3 convert.10
  149.5 0.6 slice.104.router_t
  150.1 137.3 %experts.1 = (f32[128,2176]{1,0:T(8,128)}, bf16[2048,2048]{1,0:T(8,128)(2,1)}, bf16[144,2048]{1,0:T(8,128)(2,1)}, bf16[80,2048]{1,0:T(8,128)(2,1)}) custom-call(bf16[128,2048]{1,0:T(8,128)(2,1)} %get-tuple-element.54.hidden_own, bf16[1152,2048]{1,0:T(8,128)(2,1)} %get-tuple-element.55.weights, bf16[16,2048]{1,0:T(8,128)(2,1)} %slice.104.router_t, ...), custom_call_target="tpu_custom_call" | custom-call | flops 48318382080 | bytes 41943040 | tf_op jit(solution)/shard_map/experts/pallas_call | solution.py:747
  287.4 1.1 multiply_reduce_fusion.3
  288.5 1.0 multiply_convert_fusion
  289.6 2.6 multiply_reduce_fusion
  292.4 0.7 concatenate.13.norm_rows
  293.1 2.4 fusion.12
  295.5 88.4 %attention_grad.1 = (bf16[1024,2048]{1,0:T(8,128)(2,1)}, bf16[2304,128]{1,0:T(8,128)(2,1)}, bf16[18432,128]{1,0:T(8,128)(2,1)}, bf16[640,2048]{1,0:T(8,128)(2,1)...) custom-call(bf16[128,2048]{1,0:T(8,128)(2,1)} %get-tuple-element.158.proj_own, ...), custom_call_target="tpu_custom_call" | custom-call | flops 12884901888 | bytes 62914560 | tf_op jit(solution)/shard_map/attention_grad/pallas_call | solution.py:1413
  383.9 80.5 %sum_grads.1 = (bf16[128,1152]{1,0:T(8,128)(2,1)}, f32[128,2048]{1,0:T(8,128)}, f32[128,2048]{1,0:T(8,128)}, bf16[1024,1152]{1,0:T(8,128)(2,1)}, bf16[32,1024]{1,0:T(8,128)(2,1)}, /*index=5*/bf16[256,1024]{1,0:T(8,128)(2,1)}) custom-call(bf16[2048,1152]{1,0:T(8,128)(2,1)} %get-tuple-element.72.refs_0_, bf16[1024,2048]{1,0:T(8,128)(2,1)} %get-tuple-element.73.refs_1_, ...), custom_call_target="tpu_custom_call" | custom-call | tf_op jit(solution)/shard_map/sum_grads/pallas_call | solution.py:496
  464.4 2.7 fusion
  467.2 1.3 fusion.4
  469.2 0.7 slice_reduce_fusion.2
  469.9 0.7 slice_reduce_fusion
  470.7 0.7 copy.104
  471.3 0.9 copy.103
  472.9 1.1 copy.106
  474.4 1.3 copy.105
  475.7 1.1 maximum_convert_fusion
  476.8 17.5 %unpack.1 = (f32[128,2,1408]{2,1,0:T(2,128)}, f32[128,2,1408]{2,1,0:T(2,128)}, f32[128,4,1408]{2,1,0:T(4,128)}, f32[128,4,1408]{2,1,0:T(4,128)}, f32[88,2,2048]{2,1,0:T(2,128)}, /*index=5*/f32[88,4,2048]{2,1,0:T(4,128)}) custom-call(bf16[8,16,144,128]{3,2,1,0:T(8,128)(2,1)} %bitcast.29, bf16[640,2048]{1,0:T(8,128)(2,1)} %get-tuple-element.81.down), custom_call_target="tpu_custom_call" | custom-call | tf_op jit(solution)/shard_map/unpack/pallas_call | solution.py:1486
  (48 shorter events, 3.2 us)
Async XLA Ops:
  0.6 1.6 copy-start
  145.2 3.7 copy-start.7
  150.1 139.5 %copy-start.2 = (f32[128,2048]{1,0:T(8,128)S(1)}, f32[128,2048]{1,0:T(8,128)}, u32[]{:S(2)}) copy-start(f32[128,2048]{1,0:T(8,128)} %get-tuple-element.52) | copy-start | bytes 3145732
  287.4 4.8 copy-start.8
  288.5 4.6 copy-start.9
  383.9 80.5 %copy-start.6 = (bf16[128,2048]{1,0:T(8,128)(2,1)S(1)}, bf16[128,2048]{1,0:T(8,128)(2,1)}, u32[]{:S(2)}) copy-start(bf16[128,2048]{1,0:T(8,128)(2,1)} %tokens.1) | copy-start | bytes 1572868
  464.4 2.8 copy-start.3
  467.2 1.9 copy-start.4
  469.0 3.2 copy-start.5
  474.4 1.3 copy-start.10
  475.7 18.6 %copy-start.1 = (bf16[32,4096]{1,0:T(8,128)(2,1)S(1)}, bf16[32,4096]{1,0:T(8,128)(2,1)}, u32[]{:S(2)}) copy-start(bf16[32,4096]{1,0:T(8,128)(2,1)} %param.26) | copy-start | bytes 786436
